TPU v7x, 32 devices: a whole 2x2x4 slice. The times are simulated.
32 devices in a mesh: groups: 2 (over x), row: 4 (over y, core), col: 4 (over z).
Axes of the slice: x: 2, y: 2, z: 4, core: 2. Of those that a mesh axis runs over, the one named last changes fastest.
Arguments:
- zroot: float32 [4096, 2048], P(('groups', 'row')), parts along dimension 0, as said below
- panel_one: float32 [8, 2048, 1024], P(('groups', 'col'), 'row'), parts along dimension 0, may hold values from -0.125 to 0.125
- inv_one: float32 [8, 1024, 1024], P(('groups', 'col')), parts along dimension 0
- panel_two_j: float32 [16, 1024, 512], P(('groups', 'col'), 'row'), parts along dimension 0, may hold values from -0.109375 to 0.109375
- panel_two_r: float32 [16, 2048, 512], P(('groups', 'col'), 'row'), parts along dimension 0, may hold values from -0.109375 to 0.109375
- inv_two: float32 [16, 512, 512], P(('groups', 'col')), parts along dimension 0
- parents: int32 [16], P(('groups', 'col')), parts along dimension 0, may hold values from 0 to 3
- widths: int32 [16], P(('groups', 'col')), parts along dimension 0, may hold values from 256 to 512, as said below
- pattern_j: int32 [16, 16], P(('groups', 'col'), 'row'), parts along dimension 0, may hold values 0 or 1
- pattern_r: int32 [16, 32], P(('groups', 'col'), 'row'), parts along dimension 0, may hold values 0 or 1
Outputs:
- var_one: float32 [8, 1024], P(('groups', 'col'), 'row'), parts along dimension 0
- var_two: float32 [16, 512], P(('groups', 'col'), 'row'), parts along dimension 0
- z_two_j: float32 [16, 1024, 512], P(('groups', 'col'), 'row'), parts along dimension 0
- z_two_r: float32 [16, 2048, 512], P(('groups', 'col'), 'row'), parts along dimension 0
There are 2 independent parts, one for each index of `groups`. A program takes and returns all parts, laid end to end along the dimension named above; each array names one. Nothing has to cross between parts.
Inputs may be any that keep to these rules, and one draw needn't show every extreme that they name: zroot is symmetric: it equals its transpose up to rounding, as a selected inverse block of a symmetric matrix does. `widths`: the live width of each level-2 supernode; columns at or past it are padding. `parents`: index of the level-1 parent of each level-2 supernode. `pattern_j`: 1 where a tile of 64 rows of the panel is stored. `pattern_r`: 1 where a tile of 64 rows of the panel is stored.
All inputs are finite; a program needn't handle non-finite values. No bound on the sum of `pattern_j` or of `pattern_r` on one device may be relied on, other than what follows from the above.
Results may differ from a plain program's by a relative error of at most 0.0003.
Values sent between devices are 32-bit elements; how exact they have to be, the bound alone decides.
No kernel may reach another device: no remote copies, remote signals or barrier semaphores. Data moves between devices by JAX's collectives and lax.ppermute only.
A program may use at most 128 MiB of HBM per device.

v0:
```python
import jax
import jax.numpy as jnp
from jax import lax
from jax.experimental import pallas as pl
from jax.experimental.pallas import tpu as pltpu
from jax.sharding import PartitionSpec as P

TILE = 64
CHUNKS = 4


def product(left, right):
    return jnp.dot(left, right, precision=lax.Precision.HIGH, preferred_element_type=jnp.float32)


def product_t(left, right):
    return lax.dot_general(
        left,
        right,
        (((0,), (0,)), ((), ())),
        precision=lax.Precision.HIGH,
        preferred_element_type=jnp.float32,
    )


def batched(form, left, right):
    return jnp.einsum(
        form, left, right, precision=lax.Precision.HIGH, preferred_element_type=jnp.float32
    )


def masked_factors(panel_two_j, panel_two_r, inv_two, live, pattern_j, pattern_r):
    mask_j = jnp.repeat(pattern_j.astype(jnp.float32), TILE, axis=1)
    mask_r = jnp.repeat(pattern_r.astype(jnp.float32), TILE, axis=1)
    masked_j = panel_two_j * mask_j[:, :, None] * live[:, None, :]
    masked_r = panel_two_r * mask_r[:, :, None] * live[:, None, :]
    return batched("nak,nkm->nam", masked_j, inv_two), batched("nak,nkm->nam", masked_r, inv_two)


def live_columns(widths, width_two):
    return (jnp.arange(width_two)[None, :] < widths[:, None]).astype(jnp.float32)


def general_body(
    zroot,
    panel_one,
    inv_one,
    panel_two_j,
    panel_two_r,
    inv_two,
    parents,
    widths,
    pattern_j,
    pattern_r,
):
    rows = lax.axis_size("row")
    row = lax.axis_index("row")
    inverse = inv_one[0]
    width_one = inverse.shape[0]
    share_one = width_one // rows
    nodes, width_two = inv_two.shape[0], inv_two.shape[1]
    factor = product(panel_one[0], inverse)
    own_columns = lax.dynamic_slice_in_dim(inverse, row * share_one, share_one, 1)
    square = product_t(own_columns, inverse)
    factors = lax.all_gather(factor, "col", axis=0)
    squares_of = lax.all_gather(square, "col", axis=0)
    whole = lax.all_gather(factor, "row", axis=0, tiled=True)
    terms = jnp.sum(factor * product(zroot, whole), axis=0)
    var_one = jnp.sum(own_columns * own_columns, axis=0) + lax.psum_scatter(
        terms, "row", scatter_dimension=0, tiled=True
    )
    live = live_columns(widths, width_two)
    factor_j, factor_r = masked_factors(
        panel_two_j, panel_two_r, inv_two, live, pattern_j, pattern_r
    )
    whole_j = lax.all_gather(factor_j, "row", axis=1, tiled=True)
    parent = jnp.take(factors, parents, axis=0)
    parent_square = jnp.take(squares_of, parents, axis=0)
    head = batched("nab,nbm->nam", parent, whole_j) - factor_r
    whole_head = lax.all_gather(head, "row", axis=1, tiled=True)
    block_r = batched("ab,nbm->nam", zroot, whole_head)
    own_j = batched("nab,nbm->nam", parent_square, whole_j)
    block_j = -(
        own_j
        + lax.psum_scatter(
            batched("nab,nam->nbm", parent, block_r), "row", scatter_dimension=1, tiled=True
        )
    )
    terms_two = jnp.sum(head * block_r, axis=1) + jnp.sum(factor_j * own_j, axis=1)
    summed = lax.psum_scatter(terms_two, "row", scatter_dimension=1, tiled=True)
    share_two = summed.shape[1]
    squares = jnp.sum(inv_two * inv_two, axis=1)
    live_share = lax.dynamic_slice_in_dim(live, row * share_two, share_two, 1)
    square_share = lax.dynamic_slice_in_dim(squares, row * share_two, share_two, 1)
    return var_one[None, :], live_share * (square_share + summed), block_j, block_r


ACROSS = [(0, 2), (2, 0), (1, 3), (3, 1)]
SIBLING = [(0, 1), (1, 0), (2, 3), (3, 2)]
INNER = [(1, 2), (2, 1)]
INWARD = [(0, 1), (3, 2)]
OUTWARD = [(1, 0), (2, 3)]


VMEM_LIMIT = 48 * 1024 * 1024
ANYWHERE = pl.BlockSpec(memory_space=pl.ANY)
SCALARS = pl.BlockSpec(memory_space=pltpu.SMEM)
WHOLE = pl.BlockSpec(memory_space=pltpu.VMEM)


def cost():
    return pl.CostEstimate(flops=1, bytes_accessed=1, transcendentals=0)


def params(**more):
    return pltpu.CompilerParams(vmem_limit_bytes=VMEM_LIMIT, **more)


def split(x):
    high = x.astype(jnp.bfloat16)
    return high, (x - high.astype(jnp.float32)).astype(jnp.bfloat16)


def three(left, right, contract=((1,), (0,))):
    def dot(a, b):
        return lax.dot_general(a, b, (contract, ((), ())), preferred_element_type=jnp.float32)

    return dot(left[0], right[0]) + (dot(left[0], right[1]) + dot(left[1], right[0]))


def level_one(panel, inverse, sizes):
    root_rows, width = panel.shape
    tile = 256
    starts = [sum(sizes[:q]) for q in range(len(sizes))]

    def kernel(panel_ref, inverse_ref, *refs):
        outs, (high, low) = refs[: len(sizes)], refs[len(sizes) :]

        @pl.when(pl.program_id(0) == 0)
        def _():
            high[...], low[...] = split(panel_ref[...])

        result = three((high[...], low[...]), split(inverse_ref[...]))
        for q, size in enumerate(sizes):
            outs[q][...] = result[starts[q] : starts[q] + size]

    return pl.pallas_call(
        kernel,
        grid=(width // tile,),
        in_specs=[
            pl.BlockSpec((root_rows, width), lambda i: (0, 0)),
            pl.BlockSpec((width, tile), lambda i: (0, i)),
        ],
        out_specs=[pl.BlockSpec((size, tile), lambda i: (0, i)) for size in sizes],
        out_shape=[jax.ShapeDtypeStruct((size, width), jnp.float32) for size in sizes],
        scratch_shapes=[pltpu.VMEM((root_rows, width), jnp.bfloat16)] * 2,
        compiler_params=params(),
        cost_estimate=cost(),
    )(panel, inverse)


def route(flags, picks, releases, deps):
    count = len(picks)
    used = 2 * count + len(releases)

    def kernel(flags_ref, *refs):
        outs = refs[used + len(deps) :]
        for k, (which, _, _) in enumerate(picks):

            @pl.when(flags_ref[which] == 1)
            def _():
                outs[k][...] = refs[2 * k][...]

            @pl.when(flags_ref[which] != 1)
            def _():
                outs[k][...] = refs[2 * k + 1][...]

        for k in range(len(releases)):
            outs[count + k][...] = refs[2 * count + k][...]

    operands = [x for _, yes, no in picks for x in (yes, no)] + releases
    results = [yes for _, yes, _ in picks] + releases
    return pl.pallas_call(
        kernel,
        in_specs=[SCALARS] + [WHOLE] * used + [ANYWHERE] * len(deps),
        out_specs=[WHOLE] * len(results),
        out_shape=[jax.ShapeDtypeStruct(x.shape, x.dtype) for x in results],
        compiler_params=params(),
        cost_estimate=cost(),
    )(flags, *operands, *deps)


def square_parts(columns, inverse, part, deps):
    depth, share = columns.shape
    width = inverse.shape[1]
    tile = 256
    count = share // part

    def kernel(columns_ref, inverse_ref, *refs):
        outs, (high, low) = refs[len(deps) : len(deps) + count], refs[len(deps) + count :]

        @pl.when(pl.program_id(0) == 0)
        def _():
            high[...], low[...] = split(columns_ref[...])

        result = three((high[...], low[...]), split(inverse_ref[...]), ((0,), (0,)))
        for q in range(count):
            outs[q][...] = result[q * part : (q + 1) * part]

    return pl.pallas_call(
        kernel,
        grid=(width // tile,),
        in_specs=[
            pl.BlockSpec((depth, share), lambda i: (0, 0)),
            pl.BlockSpec((depth, tile), lambda i: (0, i)),
        ]
        + [ANYWHERE] * len(deps),
        out_specs=[pl.BlockSpec((part, tile), lambda i: (0, i))] * count,
        out_shape=[jax.ShapeDtypeStruct((part, width), jnp.float32)] * count,
        scratch_shapes=[pltpu.VMEM((depth, share), jnp.bfloat16)] * 2,
        compiler_params=params(),
        cost_estimate=cost(),
    )(columns, inverse, *deps)


def with_parent(choice, candidates, whole_j, minus, start, deps):
    nodes, depth, width = whole_j.shape
    listed = isinstance(candidates, list)
    part = candidates[0].shape[0]
    sources_in = candidates if listed else [candidates]
    count = len(sources_in)
    extra = [] if minus is None else [minus]

    def kernel(choice_ref, *refs):
        sources = refs[:count]
        whole_ref = refs[count]
        minus_ref = refs[count + 1] if extra else None
        out_ref, chosen_ref, sems = refs[-3:]
        for n in range(nodes):
            if not listed:
                source = sources[0].at[choice_ref[n]]
                pltpu.make_async_copy(source, chosen_ref.at[n], sems.at[n]).start()
                continue
            for k in range(count):

                @pl.when(choice_ref[n] == k)
                def _():
                    pltpu.make_async_copy(sources[k], chosen_ref.at[n], sems.at[n]).start()

        for n in range(nodes):
            source = sources[0] if listed else sources[0].at[0]
            pltpu.make_async_copy(source, chosen_ref.at[n], sems.at[n]).wait()
            result = three(split(chosen_ref[n]), split(whole_ref[n]))
            if extra:
                result = result - minus_ref[n]
            out_ref[:, n * width : (n + 1) * width] = result

    return pl.pallas_call(
        kernel,
        grid=(1,),
        in_specs=[SCALARS]
        + [ANYWHERE] * count
        + [pl.BlockSpec((nodes, depth, width), lambda i: (0, 0, 0))]
        + [pl.BlockSpec((nodes, part, width), lambda i: (0, start // part, 0))] * len(extra)
        + [ANYWHERE] * len(deps),
        out_specs=[
            pl.BlockSpec((part, nodes * width), lambda i: (0, 0)),
            pl.BlockSpec((nodes, part, depth), lambda i: (0, 0, 0)),
        ],
        out_shape=[
            jax.ShapeDtypeStruct((part, nodes * width), jnp.float32),
            jax.ShapeDtypeStruct((nodes, part, depth), jnp.float32),
        ],
        scratch_shapes=[pltpu.SemaphoreType.DMA((nodes,))],
        compiler_params=params(),
        cost_estimate=cost(),
    )(choice, *sources_in, whole_j, *extra, *deps)


def in_order(order, blocks, deps):
    nodes, share, width = blocks[0].shape
    count = len(blocks)

    def kernel(order_ref, *refs):
        out_ref = refs[-1]
        for k in range(count):
            start = pl.multiple_of(order_ref[k] * share, share)
            for n in range(nodes):
                out_ref[n, pl.ds(start, share), :] = refs[k][n]

    return pl.pallas_call(
        kernel,
        in_specs=[SCALARS] + [WHOLE] * count + [ANYWHERE] * len(deps),
        out_specs=WHOLE,
        out_shape=jax.ShapeDtypeStruct((nodes, count * share, width), jnp.float32),
        compiler_params=params(),
        cost_estimate=cost(),
    )(order, *blocks, *deps)


def halves_of(place, own, deps):
    width = own[0].shape[1]
    half = width // 2
    starts = [sum(x.shape[0] for x in own[:q]) for q in range(len(own))]
    rows = sum(x.shape[0] for x in own)

    def kernel(place_ref, *refs):
        outs = refs[len(own) + len(deps) :]
        for k in range(2):
            at = pl.ds(pl.multiple_of((1 - place_ref[k]) * half, half), half)
            for q, x in enumerate(own):
                outs[k][starts[q] : starts[q] + x.shape[0], :] = refs[q][:, at]

    return pl.pallas_call(
        kernel,
        in_specs=[SCALARS] + [WHOLE] * len(own) + [ANYWHERE] * len(deps),
        out_specs=[WHOLE] * 2,
        out_shape=[jax.ShapeDtypeStruct((rows, half), jnp.float32)] * 2,
        compiler_params=params(),
        cost_estimate=cost(),
    )(place, *own, *deps)


def pair_terms(heads, block_r, deps):
    nodes, _, width = block_r.shape
    starts = [sum(x.shape[0] for x in heads[:q]) for q in range(len(heads))]

    def kernel(*refs):
        block_ref, out_ref = refs[len(heads)], refs[-1]
        for n in range(nodes):
            total = jnp.zeros((1, width), jnp.float32)
            for q, head in enumerate(heads):
                total = total + jnp.sum(
                    refs[q][:, n * width : (n + 1) * width]
                    * block_ref[n, starts[q] : starts[q] + head.shape[0], :],
                    axis=0,
                    keepdims=True,
                )
            out_ref[n : n + 1, :] = total

    return pl.pallas_call(
        kernel,
        in_specs=[WHOLE] * (len(heads) + 1) + [ANYWHERE] * len(deps),
        out_specs=WHOLE,
        out_shape=jax.ShapeDtypeStruct((nodes, width), jnp.float32),
        compiler_params=params(),
        cost_estimate=cost(),
    )(*heads, block_r, *deps)


def root_terms(place, zroot, own, sibling, across_same, across_other, deps):
    root_rows = zroot.shape[0]
    width = own[0].shape[1]
    half = width // 2
    count = len(own)
    starts = [sum(x.shape[0] for x in own[:q]) for q in range(count)]

    def kernel(place_ref, root_ref, *refs):
        sibling_ref, same_ref, other_ref = refs[count : count + 3]
        out_ref, factor = refs[-2:]
        chip, core = place_ref[0], place_ref[1]
        for q, x in enumerate(own):
            factor[starts[q] : starts[q] + x.shape[0], :] = refs[q][...]

        def root(which):
            start = pl.multiple_of(which * root_rows, root_rows)
            return split(root_ref[:, pl.ds(start, root_rows)])

        def halved(which):
            return factor[:, pl.ds(pl.multiple_of(which * half, half), half)]

        def put(which, value):
            at = pl.ds(pl.multiple_of(which * half, half), half)
            out_ref[:, at] = out_ref[:, at] + 2 * jnp.sum(value, axis=0, keepdims=True)

        out_ref[...] = jnp.sum(
            factor[...] * three(root(2 * chip + core), split(factor[...])), axis=0, keepdims=True
        )
        put(core, halved(core) * three(root(2 * chip + 1 - core), split(sibling_ref[...])))
        put(
            chip,
            halved(chip)
            * (
                three(root(2 * (1 - chip) + core), split(same_ref[...]))
                + three(root(2 * (1 - chip) + 1 - core), split(other_ref[...]))
            ),
        )

    return pl.pallas_call(
        kernel,
        in_specs=[SCALARS] + [WHOLE] * (1 + count + 3) + [ANYWHERE] * len(deps),
        out_specs=WHOLE,
        out_shape=jax.ShapeDtypeStruct((1, width), jnp.float32),
        scratch_shapes=[pltpu.VMEM((root_rows, width), jnp.float32)],
        compiler_params=params(),
        cost_estimate=cost(),
    )(place, zroot, *own, sibling, across_same, across_other, *deps)


def root_step(order, zroot, start, parts, before, nodes, deps):
    root_rows = zroot.shape[0]
    size, columns = parts[0].shape
    width = columns // nodes
    count = len(parts)
    tile = 256
    tiles = width // tile
    extra = [] if before is None else [before]

    def kernel(order_ref, *refs):
        out_ref, high, low, head_high, head_low = refs[-5:]
        heads = refs[count : 2 * count]

        @pl.when(pl.program_id(0) == 0)
        def _():
            for k in range(count):
                at = slice(k * size, (k + 1) * size)
                high[:, at], low[:, at] = split(refs[k][...])

        for k in range(count):
            at = slice(k * size, (k + 1) * size)
            head_high[at, :], head_low[at, :] = split(heads[k][...])
        result = three((high[...], low[...]), (head_high[...], head_low[...]))
        out_ref[...] = result + refs[2 * count][...] if extra else result

    def root_block(k):
        return pl.BlockSpec(
            (root_rows, size), lambda i, order: (0, order[k] * (root_rows // size) + start // size)
        )

    block = pl.BlockSpec((None, root_rows, tile), lambda i, order: (i // tiles, 0, i % tiles))
    return pl.pallas_call(
        kernel,
        grid_spec=pltpu.PrefetchScalarGridSpec(
            num_scalar_prefetch=1,
            grid=(nodes * tiles,),
            in_specs=[root_block(k) for k in range(count)]
            + [pl.BlockSpec((size, tile), lambda i, order: (0, i))] * count
            + [block] * len(extra)
            + [ANYWHERE] * len(deps),
            out_specs=block,
            scratch_shapes=[pltpu.VMEM((root_rows, count * size), jnp.bfloat16)] * 2
            + [pltpu.VMEM((count * size, tile), jnp.bfloat16)] * 2,
        ),
        out_shape=jax.ShapeDtypeStruct((nodes, root_rows, width), jnp.float32),
        compiler_params=params(),
        cost_estimate=cost(),
    )(order, *[zroot] * count, *parts, *extra, *deps)


def transposed(which, taken, node, block_r, deps):
    depth = taken[0].shape[2]
    _, rows, width = block_r.shape
    share = depth // 4
    count = len(taken)
    starts = [sum(x.shape[1] for x in taken[:q]) for q in range(count)]

    def kernel(which_ref, *refs):
        block_ref = refs[count]
        out_ref, left = refs[-2:]
        for q, x in enumerate(taken):
            for chip in range(2):
                start = pl.multiple_of((2 * chip + which_ref[0]) * share, share)
                left[
                    starts[q] : starts[q] + x.shape[1], chip * share : (chip + 1) * share
                ] = refs[q][:, pl.ds(start, share)]
        out_ref[...] = three(split(left[...]), split(block_ref[...]), ((0,), (0,)))

    return pl.pallas_call(
        kernel,
        grid=(1,),
        in_specs=[SCALARS]
        + [pl.BlockSpec((None,) + x.shape[1:], lambda i: (node, 0, 0)) for x in taken]
        + [pl.BlockSpec((None, rows, width), lambda i: (node, 0, 0))]
        + [ANYWHERE] * len(deps),
        out_specs=pl.BlockSpec((2 * share, width), lambda i: (0, 0)),
        out_shape=jax.ShapeDtypeStruct((2 * share, width), jnp.float32),
        scratch_shapes=[pltpu.VMEM((rows, 2 * share), jnp.float32)],
        compiler_params=params(),
        cost_estimate=cost(),
    )(which, *taken, block_r, *deps)


def line_body(
    zroot,
    panel_one,
    inv_one,
    panel_two_j,
    panel_two_r,
    inv_two,
    parents,
    widths,
    pattern_j,
    pattern_r,
):
    rows, cols = 4, 4
    row = lax.axis_index("row")
    col = lax.axis_index("col")
    chip, core = row // 2, row % 2
    root_rows = zroot.shape[0]
    inverse = inv_one[0]
    width_one = inverse.shape[0]
    share_one = width_one // rows
    nodes, width_two = inv_two.shape[0], inv_two.shape[1]

    mirror = col >= cols // 2
    at_end = jnp.where(mirror, cols - 1 - col, col) == 0

    def seen(index):
        return jnp.where(mirror, cols - 1 - index, index)

    outer_parents = lax.ppermute(parents, "col", INWARD)
    outer_needs = seen(outer_parents)
    flags = jnp.stack([jnp.any(outer_needs == 1), jnp.any(outer_needs == 3)]).astype(jnp.int32)
    needs = seen(parents)
    end_choice = jnp.where(
        (needs == 3) | ((needs == 2) & jnp.any(needs == 1)), 5, jnp.where(needs == 0, 0, 4)
    )
    inside_choice = jnp.where(
        needs == 0, 1, jnp.where(needs == 1, 0, jnp.where(needs == 2, 2, 3))
    )
    choice = jnp.where(at_end, end_choice, inside_choice).astype(jnp.int32)
    here = jnp.stack([chip, core]).astype(jnp.int32)

    order = jnp.stack([row, row ^ 1, row ^ 2, row ^ 3]).astype(jnp.int32)
    chain = []

    def exchange(x):
        across = lax.ppermute(x, "row", ACROSS)
        beside = lax.ppermute(x, "row", SIBLING)
        return [x, beside, across, lax.ppermute(across, "row", SIBLING)]

    sizes = [root_rows // CHUNKS] * CHUNKS
    starts = [sum(sizes[:q]) for q in range(CHUNKS)]
    own = list(level_one(panel_one[0], inverse, sizes))
    gathered = [lax.all_gather(x, "col", axis=0) for x in own]
    own_columns = lax.dynamic_slice_in_dim(inverse, row * share_one, share_one, 1)
    (square,) = square_parts(own_columns, inverse, share_one, [own[0], outer_parents])
    chain.append([square])

    live = live_columns(widths, width_two)
    factor_j, factor_r = masked_factors(
        panel_two_j, panel_two_r, inv_two, live, pattern_j, pattern_r
    )
    shares_j = exchange(factor_j)
    whole_j = in_order(order, shares_j, chain[-1])
    chain.append([whole_j])
    to_chip, to_core = halves_of(here, own, chain[-1])
    chain.append([to_chip])
    across_same = lax.ppermute(to_chip, "row", ACROSS)
    across_other = lax.ppermute(across_same, "row", SIBLING)
    sibling = lax.ppermute(to_core, "row", SIBLING)

    heads, taken, wholes = [], [], []
    parents_here = parents.astype(jnp.int32)

    def parent_step(q, also=()):
        deps = list(chain[-1]) + list(also)
        out, chosen = with_parent(parents_here, gathered[q], whole_j, factor_r, starts[q], deps)
        heads.append(out)
        taken.append(chosen)
        wholes.append(exchange(out))
        chain.append([out])

    def gather_step(q, before):
        out = root_step(order, zroot, starts[q], wholes[q], before, nodes, chain[-1])
        chain.append([out])
        return out

    def route_step(*picks, also=()):
        moved = list(route(flags, list(picks), [], list(chain[-1]) + list(also)))
        chain.append([moved[0]])
        return [lax.ppermute(x, "col", OUTWARD) for x in moved]

    parent_step(0)
    terms_one = root_terms(here, zroot, own, sibling, across_same, across_other, chain[-1])
    chain.append([terms_one])
    parent_step(1, wholes[0])
    block_r = gather_step(0, None)
    parent_step(2, wholes[1])
    (released,) = route(flags, [], [square], chain[-1])
    inner = lax.ppermute(released, "col", INNER)
    outer = lax.ppermute(released, "col", INWARD)
    block_r = gather_step(1, block_r)
    parent_step(3, wholes[2])
    far = lax.ppermute(outer, "col", INNER)
    (first,) = route_step((0, square, inner), also=[outer])
    block_r = gather_step(2, block_r)
    block_r = gather_step(3, block_r)
    received, kept, sums = [], [], []
    for n in range(nodes):
        which = (1 - core)[None].astype(jnp.int32)
        sent = transposed(which, taken, n, block_r, chain[-1])
        received.append(lax.ppermute(sent, "row", SIBLING))
        chain.append([sent])
    (second,) = route_step((1, far, inner))
    for n in range(nodes):
        which = core[None].astype(jnp.int32)
        keep = transposed(which, taken, n, block_r, chain[-1])
        kept.append(keep)
        chain.append([keep])
    for n in range(nodes):
        both = (kept[n] + received[n]).reshape(2, share_one, width_two)
        mine = lax.dynamic_index_in_dim(both, chip, 0, keepdims=False)
        theirs = lax.dynamic_index_in_dim(both, 1 - chip, 0, keepdims=False)
        sums.append(mine + lax.ppermute(theirs, "row", ACROSS))
    pairs = pair_terms(heads, block_r, chain[-1])
    chain.append([pairs])
    own_rows, _ = with_parent(
        choice, [square, outer, inner, far, first, second], whole_j, None, 0, chain[-1]
    )
    blocks_j, terms_two = [], []
    for n in range(nodes):
        own_j = own_rows[:, n * width_two : (n + 1) * width_two]
        blocks_j.append(-(own_j + sums[n]))
        terms_two.append(pairs[n] + jnp.sum(factor_j[n] * own_j, axis=0))
    block_j = jnp.stack(blocks_j)

    share_two = width_two // rows
    packed = jnp.concatenate(
        [terms_one.reshape(rows, share_one)] + [t.reshape(rows, share_two) for t in terms_two],
        axis=1,
    ).reshape(2, 2, -1)
    packed = lax.dynamic_index_in_dim(packed, core, 1, keepdims=False) + lax.ppermute(
        lax.dynamic_index_in_dim(packed, 1 - core, 1, keepdims=False), "row", SIBLING
    )
    packed = lax.dynamic_index_in_dim(packed, chip, 0, keepdims=False) + lax.ppermute(
        lax.dynamic_index_in_dim(packed, 1 - chip, 0, keepdims=False), "row", ACROSS
    )
    var_one = packed[:share_one] + jnp.sum(own_columns * own_columns, axis=0)
    squares = jnp.sum(inv_two * inv_two, axis=1)
    live_share = lax.dynamic_slice_in_dim(live, row * share_two, share_two, 1)
    square_share = lax.dynamic_slice_in_dim(squares, row * share_two, share_two, 1)
    var_two = live_share * (square_share + packed[share_one:].reshape(nodes, share_two))
    return var_one[None, :], var_two, block_j, block_r


def solution(mesh):
    line = mesh.shape["row"] == 4 and mesh.shape["col"] == 4

    def body(*args):
        two_nodes = args[5].shape[0] == 2
        return (line_body if line and two_nodes else general_body)(*args)

    return jax.shard_map(
        body,
        mesh=mesh,
        in_specs=(
            P(("groups", "row"), None),
            P(("groups", "col"), "row", None),
            P(("groups", "col"), None, None),
            P(("groups", "col"), "row", None),
            P(("groups", "col"), "row", None),
            P(("groups", "col"), None, None),
            P(("groups", "col")),
            P(("groups", "col")),
            P(("groups", "col"), "row"),
            P(("groups", "col"), "row"),
        ),
        out_specs=(
            P(("groups", "col"), "row"),
            P(("groups", "col"), "row"),
            P(("groups", "col"), "row", None),
            P(("groups", "col"), "row", None),
        ),
        check_vma=False,
    )
```

profile of v0, /device:TPU:0, one launch (start us, length us, event | category | flops | bytes accessed | tf_op | source)
XLA Modules:
  0.0 332.4 jit_solution(841963076097569765)
XLA Ops:
  8.8 6.8 %shard_map.129 = (f32[128,1024]{1,0:T(8,128)}, f32[128,1024]{1,0:T(8,128)}, f32[128,1024]{1,0:T(8,128)}, f32[128,1024]{1,0:T(8,128)}) custom-call(f32[512,1024]{1,0:T(8,128)S(1)} %bitcast.72, f32[1024,1024]{1,0:T(8,128)} %bitcast.77), custom_call_target="tpu_custom_call" | custom-call | flops 1 | bytes 1 | tf_op jit(solution)/shard_map/pallas_call | solution.py:147
  22.3 23.0 %collective-permute-done.1.refs_2_ = f32[2,256,512]{2,1,0:T(8,128)S(1)} collective-permute-done((f32[2,256,512]{2,1,0:T(8,128)S(1)}, f32[2,256,512]{2,1,0:T(8,128)S(1)}, u32[]{:S(2)}, u32[]{:S(2)}) %collective-permute-start.1) | collective-permute-done | bytes 1048608 | tf_op jit(solution)/shard_map/ppermute | solution.py:528
  45.3 3.9 %collective-permute-start.3 = (s32[2]{0:T(128)S(1)}, s32[2]{0:T(128)S(1)}, u32[]{:S(2)}, u32[]{:S(2)}) collective-permute-start(s32[2]{0:T(128)S(1)} %copy-done.30), channel_id=1, source_target_pairs={{0,1},{3,2},{4,5},{7,6},{8,9},{11,10},{12,13},{15,14},{16,17},{19,... | collective-permute-start | bytes 32 | tf_op jit(solution)/shard_map/ppermute | solution.py:511
  50.7 4.6 %shard_map.130.refs_4_.refs_0_ = f32[256,1024]{1,0:T(8,128)S(1)} custom-call(f32[1024,256]{1,0:T(8,128)S(1)} %get-tuple-element.39.columns_ref, f32[1024,1024]{1,0:T(8,128)} %bitcast.78, f32[128,1024]{1,0:T(8,128)} %get-tuple-element.19.refs_0_, s32[2]{0:T(128)S(1)} %collective-permute-done.3.refs_1_), custom_call_target="tpu_custom_call" | custom-call | flops 1 | bytes 1 | tf_op jit(solution)/shard_map/pallas_call | solution.py:210
  55.4 3.8 %shard_map.131.refs_4_.refs_1_.refs_6_ = f32[2,1024,512]{2,1,0:T(8,128)} custom-call(s32[4]{0:T(128)S(1)} %pad_add_fusion.1.order_ref, f32[2,256,512]{2,1,0:T(8,128)S(1)} %fusion.5.refs_0_, f32[2,256,512]{2,1,0:T(8,128)} %collective-permute-done.refs_1_, f32[2,256,512]{2,1,0:T(8,128)S(1)} %collective-permute-done.1.refs_2_, ...), custom_call_target="tpu_custom_call" | custom-call | flops 1 | bytes 1 | tf_op jit(solution)/shard_map/pallas_call | solution.py:291
  63.5 5.4 %fusion.refs_2_ = f32[2,512,512]{2,1,0:T(8,128)} fusion(f32[2,512,512]{2,1,0:T(8,128)} %param.15, f32[2,512,512]{2,1,0:T(8,128)} %param.14, f32[2,512]{1,0:T(2,128)S(1)} %compare_convert_fusion, f32[2,512]{1,0:T(2,128)S(1)} %mul.64), kind=kOutput, calls=%fused_computation.1 | convolution fusion | flops 1611661312 | bytes 6299648 | tf_op jit(solution)/shard_map/nak,nkm->nam/dot_general | solution.py:27
  69.0 18.3 %collective-permute-done.5.refs_5_ = f32[512,512]{1,0:T(8,128)} collective-permute-done((f32[512,512]{1,0:T(8,128)S(1)}, f32[512,512]{1,0:T(8,128)}, u32[]{:S(2)}, u32[]{:S(2)}) %collective-permute-start.5) | collective-permute-done | bytes 1048608 | tf_op jit(solution)/shard_map/ppermute | solution.py:549
  90.1 3.8 %shard_map.133 = (f32[128,1024]{1,0:T(8,128)S(1)}, f32[2,128,1024]{2,1,0:T(8,128)S(1)}) custom-call(s32[2]{0:T(128)S(1)} %copy-done.30, f32[4,128,1024]{2,1,0:T(8,128)S(1)} %bitcast.75, f32[2,1024,512]{2,1,0:T(8,128)} %shard_map.131.refs_4_.refs_1_.refs_6_, f32[2,512,512]{2,1,0:T(8,128)} %fusion.refs_2_, f32[512,512]{1,0:T(8,128)S(1)} %copy-done.29), custom_call_target="tpu_custom_call" | custom-call | flops 1 | bytes 1 | tf_op jit(solution)/shard_map/pallas_call | solution.py:258
  95.8 12.5 %collective-permute-done.8.refs_6_ = f32[128,1024]{1,0:T(8,128)S(1)} collective-permute-done((f32[128,1024]{1,0:T(8,128)S(1)}, f32[128,1024]{1,0:T(8,128)S(1)}, u32[]{:S(2)}, u32[]{:S(2)}) %collective-permute-start.8) | collective-permute-done | bytes 524320 | tf_op jit(solution)/shard_map/ppermute | solution.py:528
  108.3 8.1 %shard_map.134.refs_3_ = f32[1,1024]{1,0:T(1,128)S(1)} custom-call(s32[2]{0:T(128)S(1)} %pad_add_fusion.place_ref, f32[512,2048]{1,0:T(8,128)} %refs_3_.7, f32[128,1024]{1,0:T(8,128)} %get-tuple-element.19.refs_0_, f32[128,1024]{1,0:T(8,128)} %get-tuple-element.20.refs_1_, f32[128,1024]{1,0:T(8,128)} %get-tuple-element.21.refs_2_, ...), custom_call_target="tpu_custom_call" | custom-call | flops 1 | bytes 1 | tf_op jit(solution)/shard_map/pallas_call | solution.py:389
  120.4 4.6 %shard_map.135 = (f32[128,1024]{1,0:T(8,128)}, f32[2,128,1024]{2,1,0:T(8,128)S(1)}) custom-call(s32[2]{0:T(128)S(1)} %copy-done.30, f32[4,128,1024]{2,1,0:T(8,128)S(1)} %bitcast.74, f32[2,1024,512]{2,1,0:T(8,128)} %shard_map.131.refs_4_.refs_1_.refs_6_, f32[2,512,512]{2,1,0:T(8,128)} %fusion.refs_2_, f32[1,1024]{1,0:T(1,128)S(1)} %shard_map.134.refs_3_, ...), custom_call_target="tpu_custom_call" | custom-call | flops 1 | bytes 1 | tf_op jit(solution)/shard_map/pallas_call | solution.py:258
  126.7 12.9 %collective-permute-done.11.refs_6_ = f32[128,1024]{1,0:T(8,128)} collective-permute-done((f32[128,1024]{1,0:T(8,128)}, f32[128,1024]{1,0:T(8,128)}, u32[]{:S(2)}, u32[]{:S(2)}) %collective-permute-start.11) | collective-permute-done | bytes 524320 | tf_op jit(solution)/shard_map/ppermute | solution.py:528
  139.7 5.2 %shard_map.136.refs_3_.refs_8_ = f32[2,512,512]{2,1,0:T(8,128)S(1)} custom-call(s32[4]{0:T(128)S(1)} %pad_add_fusion.1.order_ref, f32[512,2048]{1,0:T(8,128)} %refs_3_.7, f32[512,2048]{1,0:T(8,128)} %refs_3_.7, f32[512,2048]{1,0:T(8,128)} %refs_3_.7, f32[512,2048]{1,0:T(8,128)} %refs_3_.7, f32[128,1024]{1,0:T(8,128)S(1)} %copy-done.18, ...), custom_call_target="tpu_custom_call" | custom-call | flops 1 | bytes 1 | tf_op jit(solution)/shard_map/pallas_call | solution.py:431
  146.2 10.7 %all-gather.13.cloned.1.call-done = f32[512,1024]{1,0:T(8,128)} async-done(((f32[128,1024]{1,0:T(8,128)}), f32[512,1024]{1,0:T(8,128)}) %all-gather.13.cloned.1.call-update) | async-done | bytes 2097168 | tf_op jit(solution)/shard_map/all_gather | solution.py:535
  158.5 4.6 %shard_map.137 = (f32[128,1024]{1,0:T(8,128)}, f32[2,128,1024]{2,1,0:T(8,128)S(1)}) custom-call(s32[2]{0:T(128)S(1)} %copy-done.30, f32[4,128,1024]{2,1,0:T(8,128)S(1)} %bitcast.73, f32[2,1024,512]{2,1,0:T(8,128)} %shard_map.131.refs_4_.refs_1_.refs_6_, f32[2,512,512]{2,1,0:T(8,128)} %fusion.refs_2_, f32[2,512,512]{2,1,0:T(8,128)} %copy-done.1, ...), custom_call_target="tpu_custom_call" | custom-call | flops 1 | bytes 1 | tf_op jit(solution)/shard_map/pallas_call | solution.py:258
  165.6 12.5 %collective-permute-done.14.refs_6_ = f32[128,1024]{1,0:T(8,128)} collective-permute-done((f32[128,1024]{1,0:T(8,128)}, f32[128,1024]{1,0:T(8,128)}, u32[]{:S(2)}, u32[]{:S(2)}) %collective-permute-start.14) | collective-permute-done | bytes 524320 | tf_op jit(solution)/shard_map/ppermute | solution.py:528
  186.2 5.9 %shard_map.138.refs_3_.refs_8_ = f32[2,512,512]{2,1,0:T(8,128)S(1)} custom-call(s32[4]{0:T(128)S(1)} %pad_add_fusion.1.order_ref, f32[512,2048]{1,0:T(8,128)} %refs_3_.7, f32[512,2048]{1,0:T(8,128)} %refs_3_.7, f32[512,2048]{1,0:T(8,128)} %refs_3_.7, f32[512,2048]{1,0:T(8,128)} %refs_3_.7, f32[128,1024]{1,0:T(8,128)} %get-tuple-element.26.refs_8_.refs_4_.refs_1_, ...), custom_call_target="tpu_custom_call" | custom-call | flops 1 | bytes 1 | tf_op jit(solution)/shard_map/pallas_call | solution.py:431
  193.4 21.1 %all-gather.15.cloned.1.call-done = f32[512,1024]{1,0:T(8,128)} async-done(((f32[128,1024]{1,0:T(8,128)}), f32[512,1024]{1,0:T(8,128)}) %all-gather.15.cloned.1.call-update) | async-done | bytes 2097168 | tf_op jit(solution)/shard_map/all_gather | solution.py:535
  216.1 4.6 %shard_map.139 = (f32[128,1024]{1,0:T(8,128)}, f32[2,128,1024]{2,1,0:T(8,128)S(1)}) custom-call(s32[2]{0:T(128)S(1)} %copy-done.30, f32[4,128,1024]{2,1,0:T(8,128)S(1)} %bitcast.76, f32[2,1024,512]{2,1,0:T(8,128)} %shard_map.131.refs_4_.refs_1_.refs_6_, f32[2,512,512]{2,1,0:T(8,128)} %fusion.refs_2_, f32[2,512,512]{2,1,0:T(8,128)} %copy-done.2, ...), custom_call_target="tpu_custom_call" | custom-call | flops 1 | bytes 1 | tf_op jit(solution)/shard_map/pallas_call | solution.py:258
  223.3 12.4 %collective-permute-done.17.refs_6_ = f32[128,1024]{1,0:T(8,128)} collective-permute-done((f32[128,1024]{1,0:T(8,128)}, f32[128,1024]{1,0:T(8,128)}, u32[]{:S(2)}, u32[]{:S(2)}) %collective-permute-start.17) | collective-permute-done | bytes 524320 | tf_op jit(solution)/shard_map/ppermute | solution.py:528
  239.7 5.9 %shard_map.142.refs_8_.refs_9_ = f32[2,512,512]{2,1,0:T(8,128)S(1)} custom-call(s32[4]{0:T(128)S(1)} %pad_add_fusion.1.order_ref, f32[512,2048]{1,0:T(8,128)} %refs_3_.7, f32[512,2048]{1,0:T(8,128)} %refs_3_.7, f32[512,2048]{1,0:T(8,128)} %refs_3_.7, f32[512,2048]{1,0:T(8,128)} %refs_3_.7, f32[128,1024]{1,0:T(8,128)} %get-tuple-element.27.refs_9_.refs_4_.refs_1_.refs_2_, ...), custom_call_target="tpu_custom_call" | custom-call | flops 1 | bytes 1 | tf_op jit(solution)/shard_map/pallas_call | solution.py:431
  245.6 6.3 %shard_map.143.refs_4_.refs_5_ = f32[2,512,512]{2,1,0:T(8,128)} custom-call(s32[4]{0:T(128)S(1)} %pad_add_fusion.1.order_ref, f32[512,2048]{1,0:T(8,128)} %refs_3_.7, f32[512,2048]{1,0:T(8,128)} %refs_3_.7, f32[512,2048]{1,0:T(8,128)} %refs_3_.7, f32[512,2048]{1,0:T(8,128)} %refs_3_.7, f32[128,1024]{1,0:T(8,128)} %get-tuple-element.28.refs_2_.refs_4_.refs_3_, ...), custom_call_target="tpu_custom_call" | custom-call | flops 1 | bytes 1 | tf_op jit(solution)/shard_map/pallas_call | solution.py:431
  290.0 22.1 %collective-permute-done.23.refs_5_ = f32[256,1024]{1,0:T(8,128)} collective-permute-done((f32[256,1024]{1,0:T(8,128)}, f32[256,1024]{1,0:T(8,128)}, u32[]{:S(2)}, u32[]{:S(2)}) %collective-permute-start.23) | collective-permute-done | bytes 1048608 | tf_op jit(solution)/shard_map/ppermute | solution.py:572
  312.1 5.8 %shard_map.150 = (f32[256,1024]{1,0:T(8,128)S(1)}, f32[2,256,1024]{2,1,0:T(8,128)}) custom-call(s32[2]{0:T(128)S(1)} %broadcast_select_fusion.choice_ref, f32[256,1024]{1,0:T(8,128)S(1)} %shard_map.130.refs_4_.refs_0_, f32[256,1024]{1,0:T(8,128)} %collective-permute-done.20.refs_3_.refs_1_, f32[256,1024]{1,0:T(8,128)} %collective-permute-done.19.refs_1_.refs_2_, ...), custom_call_target="tpu_custom_call" | custom-call | flops 1 | bytes 1 | tf_op jit(solution)/shard_map/pallas_call | solution.py:258
  (187 shorter events, 93.2 us)
Async XLA Ops:
  7.2 80.1 %all-gather.9.cloned.1.call-start = ((), (), s32[]{:S(2)}) async-start(), calls=%async_computation | async-start | bytes 2621440 | tf_op jit(solution)/shard_map/all_gather | solution.py:535
  15.6 100.8 %all-gather.11.cloned.1.call-start = ((), (), s32[]{:S(2)}) async-start(), calls=%async_computation.1 | async-start | bytes 2621440 | tf_op jit(solution)/shard_map/all_gather | solution.py:535
  16.4 140.6 %all-gather.13.cloned.1.call-start = ((), (), s32[]{:S(2)}) async-start(), calls=%async_computation.2 | async-start | bytes 2621440 | tf_op jit(solution)/shard_map/all_gather | solution.py:535
  19.1 26.2 %collective-permute-start.1 = (f32[2,256,512]{2,1,0:T(8,128)S(1)}, f32[2,256,512]{2,1,0:T(8,128)S(1)}, u32[]{:S(2)}, u32[]{:S(2)}) collective-permute-start(f32[2,256,512]{2,1,0:T(8,128)S(1)} %fusion.5.refs_0_), channel_id=1, source_target_pairs={{0,8},{8,0},{4,12},{12,4},{1,9},{9,1},{5,13},{13,5},{2,10},{10,2},... | collective-permute-start | bytes 3145736 | tf_op jit(solution)/shard_map/ppermute | solution.py:528
  22.1 192.4 %all-gather.15.cloned.1.call-start = ((), (), s32[]{:S(2)}) async-start(), calls=%async_computation.3 | async-start | bytes 2621440 | tf_op jit(solution)/shard_map/all_gather | solution.py:535
  22.2 33.2 %collective-permute-start = (f32[2,256,512]{2,1,0:T(8,128)S(1)}, f32[2,256,512]{2,1,0:T(8,128)}, u32[]{:S(2)}, u32[]{:S(2)}) collective-permute-start(f32[2,256,512]{2,1,0:T(8,128)S(1)} %fusion.5.refs_0_), channel_id=1, source_target_pairs={{0,4},{4,0},{8,12},{12,8},{1,5},{5,1},{9,13},{13,9},{2,6},{6,2},{1... | collective-permute-start | bytes 3145736 | tf_op jit(solution)/shard_map/ppermute | solution.py:529
  61.8 25.4 %collective-permute-start.5 = (f32[512,512]{1,0:T(8,128)S(1)}, f32[512,512]{1,0:T(8,128)}, u32[]{:S(2)}, u32[]{:S(2)}) collective-permute-start(f32[512,512]{1,0:T(8,128)S(1)} %get-tuple-element.24.refs_3_), channel_id=1, source_target_pairs={{0,8},{8,0},{4,12},{12,4},{1,9},{9,1},{5,13},{13,5},{2,10},{10,2},... | collective-permute-start | bytes 3145736 | tf_op jit(solution)/shard_map/ppermute | solution.py:549
  69.0 39.3 %collective-permute-start.4 = (f32[512,512]{1,0:T(8,128)}, f32[512,512]{1,0:T(8,128)}, u32[]{:S(2)}, u32[]{:S(2)}) collective-permute-start(f32[512,512]{1,0:T(8,128)} %get-tuple-element.23), channel_id=1, source_target_pairs={{0,4},{4,0},{8,12},{12,8},{1,5},{5,1},{9,13},{13,9},{2,6},{6,2},{1... | collective-permute-start | bytes 3145736 | tf_op jit(solution)/shard_map/ppermute | solution.py:551
  87.2 21.1 %collective-permute-start.6 = (f32[512,512]{1,0:T(8,128)}, f32[512,512]{1,0:T(8,128)}, u32[]{:S(2)}, u32[]{:S(2)}) collective-permute-start(f32[512,512]{1,0:T(8,128)} %collective-permute-done.5.refs_5_), channel_id=1, source_target_pairs={{0,4},{4,0},{8,12},{12,8},{1,5},{5,1},{9,13},{13,9},{2,6},{6,2},{1... | collective-permute-start | bytes 3145736 | tf_op jit(solution)/shard_map/ppermute | solution.py:550
  95.4 21.0 %collective-permute-start.7 = (f32[128,1024]{1,0:T(8,128)S(1)}, f32[128,1024]{1,0:T(8,128)}, u32[]{:S(2)}, u32[]{:S(2)}) collective-permute-start(f32[128,1024]{1,0:T(8,128)S(1)} %get-tuple-element.25.refs_7_.refs_4_.refs_0_), channel_id=1, source_target_pairs={{0,4},{4,0},{8,12},{12,8},{1,5},{5,1},{9,13},{13,9},{2,6},{6,2},{1... | collective-permute-start | bytes 1572872 | tf_op jit(solution)/shard_map/ppermute | solution.py:529
  126.6 30.4 %collective-permute-start.10 = (f32[128,1024]{1,0:T(8,128)}, f32[128,1024]{1,0:T(8,128)}, u32[]{:S(2)}, u32[]{:S(2)}) collective-permute-start(f32[128,1024]{1,0:T(8,128)} %get-tuple-element.26.refs_8_.refs_4_.refs_1_), channel_id=1, source_target_pairs={{0,4},{4,0},{8,12},{12,8},{1,5},{5,1},{9,13},{13,9},{2,6},{6,2},{1... | collective-permute-start | bytes 1572872 | tf_op jit(solution)/shard_map/ppermute | solution.py:529
  139.6 17.3 %collective-permute-start.12 = (f32[128,1024]{1,0:T(8,128)}, f32[128,1024]{1,0:T(8,128)}, u32[]{:S(2)}, u32[]{:S(2)}) collective-permute-start(f32[128,1024]{1,0:T(8,128)} %collective-permute-done.11.refs_6_), channel_id=1, source_target_pairs={{0,4},{4,0},{8,12},{12,8},{1,5},{5,1},{9,13},{13,9},{2,6},{6,2},{1... | collective-permute-start | bytes 1572872 | tf_op jit(solution)/shard_map/ppermute | solution.py:530
  165.6 48.9 %collective-permute-start.13 = (f32[128,1024]{1,0:T(8,128)}, f32[128,1024]{1,0:T(8,128)}, u32[]{:S(2)}, u32[]{:S(2)}) collective-permute-start(f32[128,1024]{1,0:T(8,128)} %get-tuple-element.27.refs_9_.refs_4_.refs_1_.refs_2_), channel_id=1, source_target_pairs={{0,4},{4,0},{8,12},{12,8},{1,5},{5,1},{9,13},{13,9},{2,6},{6,2},{1... | collective-permute-start | bytes 1572872 | tf_op jit(solution)/shard_map/ppermute | solution.py:529
  178.1 36.4 %collective-permute-start.15 = (f32[128,1024]{1,0:T(8,128)}, f32[128,1024]{1,0:T(8,128)}, u32[]{:S(2)}, u32[]{:S(2)}) collective-permute-start(f32[128,1024]{1,0:T(8,128)} %collective-permute-done.14.refs_6_), channel_id=1, source_target_pairs={{0,4},{4,0},{8,12},{12,8},{1,5},{5,1},{9,13},{13,9},{2,6},{6,2},{1... | collective-permute-start | bytes 1572872 | tf_op jit(solution)/shard_map/ppermute | solution.py:530
  181.7 54.0 %collective-permute-start.20 = (f32[256,1024]{1,0:T(8,128)}, f32[256,1024]{1,0:T(8,128)}, u32[]{:S(2)}, u32[]{:S(2)}) collective-permute-start(f32[256,1024]{1,0:T(8,128)} %shard_map.140), channel_id=1, source_target_pairs={{0,1},{3,2},{4,5},{7,6},{8,9},{11,10},{12,13},{15,14},{16,17},{19,... | collective-permute-start | bytes 3145736 | tf_op jit(solution)/shard_map/ppermute | solution.py:582
  184.5 52.9 %collective-permute-start.19 = (f32[256,1024]{1,0:T(8,128)}, f32[256,1024]{1,0:T(8,128)}, u32[]{:S(2)}, u32[]{:S(2)}) collective-permute-start(f32[256,1024]{1,0:T(8,128)} %shard_map.140), channel_id=1, source_target_pairs={{1,2},{2,1},{5,6},{6,5},{9,10},{10,9},{13,14},{14,13},{17,18},{18,... | collective-permute-start | bytes 3145736 | tf_op jit(solution)/shard_map/ppermute | solution.py:581
  223.3 22.3 %collective-permute-start.16 = (f32[128,1024]{1,0:T(8,128)}, f32[128,1024]{1,0:T(8,128)}, u32[]{:S(2)}, u32[]{:S(2)}) collective-permute-start(f32[128,1024]{1,0:T(8,128)} %get-tuple-element.28.refs_2_.refs_4_.refs_3_), channel_id=1, source_target_pairs={{0,4},{4,0},{8,12},{12,8},{1,5},{5,1},{9,13},{13,9},{2,6},{6,2},{1... | collective-permute-start | bytes 1572872 | tf_op jit(solution)/shard_map/ppermute | solution.py:529
  235.7 24.5 %collective-permute-start.21 = (f32[256,1024]{1,0:T(8,128)}, f32[256,1024]{1,0:T(8,128)}, u32[]{:S(2)}, u32[]{:S(2)}) collective-permute-start(f32[256,1024]{1,0:T(8,128)} %collective-permute-done.20.refs_3_.refs_1_), channel_id=1, source_target_pairs={{1,2},{2,1},{5,6},{6,5},{9,10},{10,9},{13,14},{14,13},{17,18},{18,... | collective-permute-start | bytes 3145736 | tf_op jit(solution)/shard_map/ppermute | solution.py:585
  255.1 19.5 %collective-permute-start.26 = (f32[512,512]{1,0:T(8,128)}, f32[512,512]{1,0:T(8,128)}, u32[]{:S(2)}, u32[]{:S(2)}) collective-permute-start(f32[512,512]{1,0:T(8,128)} %shard_map.144.refs_5_), channel_id=1, source_target_pairs={{0,4},{4,0},{8,12},{12,8},{1,5},{5,1},{9,13},{13,9},{2,6},{6,2},{1... | collective-permute-start | bytes 3145736 | tf_op jit(solution)/shard_map/ppermute | solution.py:593
  258.9 19.6 %collective-permute-start.28 = (f32[512,512]{1,0:T(8,128)}, f32[512,512]{1,0:T(8,128)}, u32[]{:S(2)}, u32[]{:S(2)}) collective-permute-start(f32[512,512]{1,0:T(8,128)} %shard_map.145.refs_2_), channel_id=1, source_target_pairs={{0,4},{4,0},{8,12},{12,8},{1,5},{5,1},{9,13},{13,9},{2,6},{6,2},{1... | collective-permute-start | bytes 3145736 | tf_op jit(solution)/shard_map/ppermute | solution.py:593
  258.9 31.1 %collective-permute-start.22 = (f32[256,1024]{1,0:T(8,128)}, f32[256,1024]{1,0:T(8,128)}, u32[]{:S(2)}, u32[]{:S(2)}) collective-permute-start(f32[256,1024]{1,0:T(8,128)} %shard_map.141.refs_9_), channel_id=1, source_target_pairs={{1,0},{2,3},{5,4},{6,7},{9,8},{10,11},{13,12},{14,15},{17,16},{18,... | collective-permute-start | bytes 3145736 | tf_op jit(solution)/shard_map/ppermute | solution.py:572
  262.9 49.3 %collective-permute-start.23 = (f32[256,1024]{1,0:T(8,128)}, f32[256,1024]{1,0:T(8,128)}, u32[]{:S(2)}, u32[]{:S(2)}) collective-permute-start(f32[256,1024]{1,0:T(8,128)} %shard_map.146.refs_5_), channel_id=1, source_target_pairs={{1,0},{2,3},{5,4},{6,7},{9,8},{10,11},{13,12},{14,15},{17,16},{18,... | collective-permute-start | bytes 3145736 | tf_op jit(solution)/shard_map/ppermute | solution.py:572
  277.4 40.5 %collective-permute-start.27 = (f32[256,512]{1,0:T(8,128)}, f32[256,512]{1,0:T(8,128)}, u32[]{:S(2)}, u32[]{:S(2)}) collective-permute-start(f32[256,512]{1,0:T(8,128)} %dynamic-slice_bitcast_fusion.2), channel_id=1, source_target_pairs={{0,8},{8,0},{4,12},{12,4},{1,9},{9,1},{5,13},{13,5},{2,10},{10,2},... | collective-permute-start | bytes 1572872 | tf_op jit(solution)/shard_map/ppermute | solution.py:605
  280.9 37.0 %collective-permute-start.29 = (f32[256,512]{1,0:T(8,128)}, f32[256,512]{1,0:T(8,128)}, u32[]{:S(2)}, u32[]{:S(2)}) collective-permute-start(f32[256,512]{1,0:T(8,128)} %dynamic-slice_bitcast_fusion.1), channel_id=1, source_target_pairs={{0,8},{8,0},{4,12},{12,4},{1,9},{9,1},{5,13},{13,5},{2,10},{10,2},... | collective-permute-start | bytes 1572872 | tf_op jit(solution)/shard_map/ppermute | solution.py:605
  (50 other events, 391.7 us)
Sparse Core Ops, SparseCore 0:
  15.8 48.6 all-gather.8
  66.0 44.6 all-gather.10
  112.3 44.6 all-gather.12
  158.4 56.0 all-gather.14
where the time goes:
time: 334 us; the launch traced here: 332 us
  waiting for transfers between devices  150 us (45%)
  Pallas kernels  91.8 us (27%)
  starting transfers between devices  28.2 us (8%)
  local copies, waits for them, and re-layouts  27 us (8%)
  between operations  14.4 us (4%)
  other arithmetic  13 us (4%)
  matrix products  7.8 us (2%)
    ppermute x5, waiting for transfers between devices, exchange(): across = lax.ppermute(x, 'row', ACROSS)  73.3 us
    all_gather x4, waiting for transfers between devices, line_body(): gathered = [lax.all_gather(x, 'col', axis=0) for x in own]  31.8 us
    unnamed x81, local copies, waits for them, and re-layouts  24.3 us
    ppermute x2, waiting for transfers between devices, route_step(): return [lax.ppermute(x, 'col', OUTWARD) for x in moved]  23.9 us
    pallas_call x5, Pallas kernels, with_parent(): pl.pallas_call(kernel, grid=(1,), in_specs=[SCALARS] + [ANYWHERE] * count...  23.3 us
    pallas_call x4, Pallas kernels, root_step(): pl.pallas_call(kernel, grid_spec=pltpu.PrefetchScalarGridSpec(num_scalar_...  23.2 us
    ppermute x1, waiting for transfers between devices, line_body(): across_same = lax.ppermute(to_chip, 'row', ACROSS)  18.3 us
    pallas_call x4, Pallas kernels, transposed(): pl.pallas_call(kernel, grid=(1,), in_specs=[SCALARS] + [pl.BlockSpec((Non...  11.2 us
  transfers between devices with their start and end apart: 34, of which 12 were waited for; matrix products, arithmetic and copies ran while one was open for 6% of the time, Pallas kernels for 26%

commit v1 on v0

--- a/solution.py
+++ b/solution.py
@@ -97,9 +97,6 @@
 
 ACROSS = [(0, 2), (2, 0), (1, 3), (3, 1)]
 SIBLING = [(0, 1), (1, 0), (2, 3), (3, 2)]
-INNER = [(1, 2), (2, 1)]
-INWARD = [(0, 1), (3, 2)]
-OUTWARD = [(1, 0), (2, 3)]
 
 
 VMEM_LIMIT = 48 * 1024 * 1024
@@ -159,53 +156,37 @@
     )(panel, inverse)
 
 
-def route(flags, picks, releases, deps):
-    count = len(picks)
-    used = 2 * count + len(releases)
-
-    def kernel(flags_ref, *refs):
-        outs = refs[used + len(deps) :]
-        for k, (which, _, _) in enumerate(picks):
-
-            @pl.when(flags_ref[which] == 1)
-            def _():
-                outs[k][...] = refs[2 * k][...]
-
-            @pl.when(flags_ref[which] != 1)
-            def _():
-                outs[k][...] = refs[2 * k + 1][...]
-
-        for k in range(len(releases)):
-            outs[count + k][...] = refs[2 * count + k][...]
-
-    operands = [x for _, yes, no in picks for x in (yes, no)] + releases
-    results = [yes for _, yes, _ in picks] + releases
-    return pl.pallas_call(
-        kernel,
-        in_specs=[SCALARS] + [WHOLE] * used + [ANYWHERE] * len(deps),
-        out_specs=[WHOLE] * len(results),
-        out_shape=[jax.ShapeDtypeStruct(x.shape, x.dtype) for x in results],
-        compiler_params=params(),
-        cost_estimate=cost(),
-    )(flags, *operands, *deps)
-
-
-def square_parts(columns, inverse, part, deps):
+def after(deps, *arrays):
+    count = len(arrays)
+
+    def kernel(*refs):
+        outs = refs[count + len(deps) :]
+        for k in range(count):
+            outs[k][...] = refs[k][...]
+
+    return pl.pallas_call(
+        kernel,
+        in_specs=[WHOLE] * count + [ANYWHERE] * len(deps),
+        out_specs=[WHOLE] * count,
+        out_shape=[jax.ShapeDtypeStruct(x.shape, x.dtype) for x in arrays],
+        compiler_params=params(),
+        cost_estimate=cost(),
+    )(*arrays, *deps)
+
+
+def square_rows(columns, inverse, deps):
     depth, share = columns.shape
     width = inverse.shape[1]
     tile = 256
-    count = share // part
 
     def kernel(columns_ref, inverse_ref, *refs):
-        outs, (high, low) = refs[len(deps) : len(deps) + count], refs[len(deps) + count :]
+        out_ref, high, low = refs[-3:]
 
         @pl.when(pl.program_id(0) == 0)
         def _():
             high[...], low[...] = split(columns_ref[...])
 
-        result = three((high[...], low[...]), split(inverse_ref[...]), ((0,), (0,)))
-        for q in range(count):
-            outs[q][...] = result[q * part : (q + 1) * part]
+        out_ref[...] = three((high[...], low[...]), split(inverse_ref[...]), ((0,), (0,)))
 
     return pl.pallas_call(
         kernel,
@@ -215,53 +196,41 @@
             pl.BlockSpec((depth, tile), lambda i: (0, i)),
         ]
         + [ANYWHERE] * len(deps),
-        out_specs=[pl.BlockSpec((part, tile), lambda i: (0, i))] * count,
-        out_shape=[jax.ShapeDtypeStruct((part, width), jnp.float32)] * count,
+        out_specs=pl.BlockSpec((share, tile), lambda i: (0, i)),
+        out_shape=jax.ShapeDtypeStruct((share, width), jnp.float32),
         scratch_shapes=[pltpu.VMEM((depth, share), jnp.bfloat16)] * 2,
         compiler_params=params(),
         cost_estimate=cost(),
     )(columns, inverse, *deps)
 
 
-def with_parent(choice, candidates, whole_j, minus, start, deps):
+def with_parent(parents, gathered, whole_j, minus, start, deps):
     nodes, depth, width = whole_j.shape
-    listed = isinstance(candidates, list)
-    part = candidates[0].shape[0]
-    sources_in = candidates if listed else [candidates]
-    count = len(sources_in)
+    part = gathered.shape[1]
     extra = [] if minus is None else [minus]
 
-    def kernel(choice_ref, *refs):
-        sources = refs[:count]
-        whole_ref = refs[count]
-        minus_ref = refs[count + 1] if extra else None
+    def kernel(parents_ref, gathered_ref, whole_ref, *refs):
         out_ref, chosen_ref, sems = refs[-3:]
+
+        def copy(n):
+            return pltpu.make_async_copy(
+                gathered_ref.at[parents_ref[n]], chosen_ref.at[n], sems.at[n]
+            )
+
         for n in range(nodes):
-            if not listed:
-                source = sources[0].at[choice_ref[n]]
-                pltpu.make_async_copy(source, chosen_ref.at[n], sems.at[n]).start()
-                continue
-            for k in range(count):
-
-                @pl.when(choice_ref[n] == k)
-                def _():
-                    pltpu.make_async_copy(sources[k], chosen_ref.at[n], sems.at[n]).start()
-
+            copy(n).start()
         for n in range(nodes):
-            source = sources[0] if listed else sources[0].at[0]
-            pltpu.make_async_copy(source, chosen_ref.at[n], sems.at[n]).wait()
+            copy(n).wait()
             result = three(split(chosen_ref[n]), split(whole_ref[n]))
             if extra:
-                result = result - minus_ref[n]
+                result = result - refs[0][n, start : start + part, :]
             out_ref[:, n * width : (n + 1) * width] = result
 
     return pl.pallas_call(
         kernel,
         grid=(1,),
-        in_specs=[SCALARS]
-        + [ANYWHERE] * count
-        + [pl.BlockSpec((nodes, depth, width), lambda i: (0, 0, 0))]
-        + [pl.BlockSpec((nodes, part, width), lambda i: (0, start // part, 0))] * len(extra)
+        in_specs=[SCALARS, ANYWHERE]
+        + [pl.BlockSpec(x.shape, lambda i: (0, 0, 0)) for x in [whole_j] + extra]
         + [ANYWHERE] * len(deps),
         out_specs=[
             pl.BlockSpec((part, nodes * width), lambda i: (0, 0)),
@@ -274,7 +243,7 @@
         scratch_shapes=[pltpu.SemaphoreType.DMA((nodes,))],
         compiler_params=params(),
         cost_estimate=cost(),
-    )(choice, *sources_in, whole_j, *extra, *deps)
+    )(parents, gathered, whole_j, *extra, *deps)
 
 
 def in_order(order, blocks, deps):
@@ -406,45 +375,44 @@
     tiles = width // tile
     extra = [] if before is None else [before]
 
-    def kernel(order_ref, *refs):
-        out_ref, high, low, head_high, head_low = refs[-5:]
-        heads = refs[count : 2 * count]
+    def kernel(order_ref, root_ref, *refs):
+        out_ref, root, high, low, head_high, head_low, sems = refs[-7:]
 
         @pl.when(pl.program_id(0) == 0)
         def _():
+            copies = []
+            for k in range(count):
+                at = pl.ds(pl.multiple_of(order_ref[k] * root_rows + start, 128), size)
+                copies.append(pltpu.make_async_copy(root_ref.at[:, at], root.at[k], sems.at[k]))
+                copies[k].start()
             for k in range(count):
                 at = slice(k * size, (k + 1) * size)
-                high[:, at], low[:, at] = split(refs[k][...])
+                copies[k].wait()
+                high[:, at], low[:, at] = split(root[k])
 
         for k in range(count):
             at = slice(k * size, (k + 1) * size)
-            head_high[at, :], head_low[at, :] = split(heads[k][...])
+            head_high[at, :], head_low[at, :] = split(refs[k][...])
         result = three((high[...], low[...]), (head_high[...], head_low[...]))
-        out_ref[...] = result + refs[2 * count][...] if extra else result
-
-    def root_block(k):
-        return pl.BlockSpec(
-            (root_rows, size), lambda i, order: (0, order[k] * (root_rows // size) + start // size)
-        )
-
-    block = pl.BlockSpec((None, root_rows, tile), lambda i, order: (i // tiles, 0, i % tiles))
-    return pl.pallas_call(
-        kernel,
-        grid_spec=pltpu.PrefetchScalarGridSpec(
-            num_scalar_prefetch=1,
-            grid=(nodes * tiles,),
-            in_specs=[root_block(k) for k in range(count)]
-            + [pl.BlockSpec((size, tile), lambda i, order: (0, i))] * count
-            + [block] * len(extra)
-            + [ANYWHERE] * len(deps),
-            out_specs=block,
-            scratch_shapes=[pltpu.VMEM((root_rows, count * size), jnp.bfloat16)] * 2
-            + [pltpu.VMEM((count * size, tile), jnp.bfloat16)] * 2,
-        ),
+        out_ref[...] = result + refs[count][...] if extra else result
+
+    block = pl.BlockSpec((None, root_rows, tile), lambda i: (i // tiles, 0, i % tiles))
+    return pl.pallas_call(
+        kernel,
+        grid=(nodes * tiles,),
+        in_specs=[SCALARS, ANYWHERE]
+        + [pl.BlockSpec((size, tile), lambda i: (0, i))] * count
+        + [block] * len(extra)
+        + [ANYWHERE] * len(deps),
+        out_specs=block,
         out_shape=jax.ShapeDtypeStruct((nodes, root_rows, width), jnp.float32),
-        compiler_params=params(),
-        cost_estimate=cost(),
-    )(order, *[zroot] * count, *parts, *extra, *deps)
+        scratch_shapes=[pltpu.VMEM((count, root_rows, size), jnp.float32)]
+        + [pltpu.VMEM((root_rows, count * size), jnp.bfloat16)] * 2
+        + [pltpu.VMEM((count * size, tile), jnp.bfloat16)] * 2
+        + [pltpu.SemaphoreType.DMA((count,))],
+        compiler_params=params(),
+        cost_estimate=cost(),
+    )(order, zroot, *parts, *extra, *deps)
 
 
 def transposed(which, taken, node, block_r, deps):
@@ -478,6 +446,28 @@
         compiler_params=params(),
         cost_estimate=cost(),
     )(which, *taken, block_r, *deps)
+
+
+def halved_sums(chip, kept, received, deps):
+    nodes = len(kept)
+    rows, width = kept[0].shape
+    share = rows // 2
+
+    def kernel(chip_ref, *refs):
+        theirs_ref, mine_ref = refs[-2:]
+        for out_ref, which in ((theirs_ref, 1 - chip_ref[0]), (mine_ref, chip_ref[0])):
+            at = pl.ds(pl.multiple_of(which * share, share), share)
+            for n in range(nodes):
+                out_ref[n] = refs[n][at, :] + refs[nodes + n][at, :]
+
+    return pl.pallas_call(
+        kernel,
+        in_specs=[SCALARS] + [WHOLE] * (2 * nodes) + [ANYWHERE] * len(deps),
+        out_specs=[WHOLE] * 2,
+        out_shape=[jax.ShapeDtypeStruct((nodes, share, width), jnp.float32)] * 2,
+        compiler_params=params(),
+        cost_estimate=cost(),
+    )(chip, *kept, *received, *deps)
 
 
 def line_body(
@@ -502,23 +492,6 @@
     share_one = width_one // rows
     nodes, width_two = inv_two.shape[0], inv_two.shape[1]
 
-    mirror = col >= cols // 2
-    at_end = jnp.where(mirror, cols - 1 - col, col) == 0
-
-    def seen(index):
-        return jnp.where(mirror, cols - 1 - index, index)
-
-    outer_parents = lax.ppermute(parents, "col", INWARD)
-    outer_needs = seen(outer_parents)
-    flags = jnp.stack([jnp.any(outer_needs == 1), jnp.any(outer_needs == 3)]).astype(jnp.int32)
-    needs = seen(parents)
-    end_choice = jnp.where(
-        (needs == 3) | ((needs == 2) & jnp.any(needs == 1)), 5, jnp.where(needs == 0, 0, 4)
-    )
-    inside_choice = jnp.where(
-        needs == 0, 1, jnp.where(needs == 1, 0, jnp.where(needs == 2, 2, 3))
-    )
-    choice = jnp.where(at_end, end_choice, inside_choice).astype(jnp.int32)
     here = jnp.stack([chip, core]).astype(jnp.int32)
 
     order = jnp.stack([row, row ^ 1, row ^ 2, row ^ 3]).astype(jnp.int32)
@@ -529,12 +502,12 @@
         beside = lax.ppermute(x, "row", SIBLING)
         return [x, beside, across, lax.ppermute(across, "row", SIBLING)]
 
-    sizes = [root_rows // CHUNKS] * CHUNKS
-    starts = [sum(sizes[:q]) for q in range(CHUNKS)]
+    sizes = [root_rows - root_rows // 4, root_rows // 4]
+    starts = [0, sizes[0]]
     own = list(level_one(panel_one[0], inverse, sizes))
     gathered = [lax.all_gather(x, "col", axis=0) for x in own]
     own_columns = lax.dynamic_slice_in_dim(inverse, row * share_one, share_one, 1)
-    (square,) = square_parts(own_columns, inverse, share_one, [own[0], outer_parents])
+    square = square_rows(own_columns, inverse, [own[0]])
     chain.append([square])
 
     live = live_columns(widths, width_two)
@@ -550,64 +523,52 @@
     across_other = lax.ppermute(across_same, "row", SIBLING)
     sibling = lax.ppermute(to_core, "row", SIBLING)
 
-    heads, taken, wholes = [], [], []
+    heads, taken = [], []
     parents_here = parents.astype(jnp.int32)
 
-    def parent_step(q, also=()):
-        deps = list(chain[-1]) + list(also)
-        out, chosen = with_parent(parents_here, gathered[q], whole_j, factor_r, starts[q], deps)
+    def parent_step(q):
+        out, chosen = with_parent(
+            parents_here, gathered[q], whole_j, factor_r, starts[q], chain[-1]
+        )
         heads.append(out)
         taken.append(chosen)
-        wholes.append(exchange(out))
-        chain.append([out])
-
-    def gather_step(q, before):
-        out = root_step(order, zroot, starts[q], wholes[q], before, nodes, chain[-1])
         chain.append([out])
         return out
 
-    def route_step(*picks, also=()):
-        moved = list(route(flags, list(picks), [], list(chain[-1]) + list(also)))
-        chain.append([moved[0]])
-        return [lax.ppermute(x, "col", OUTWARD) for x in moved]
-
-    parent_step(0)
+    def gather_step(q, parts, before):
+        out = root_step(order, zroot, starts[q], parts, before, nodes, chain[-1])
+        chain.append([out])
+        return out
+
     terms_one = root_terms(here, zroot, own, sibling, across_same, across_other, chain[-1])
     chain.append([terms_one])
-    parent_step(1, wholes[0])
-    block_r = gather_step(0, None)
-    parent_step(2, wholes[1])
-    (released,) = route(flags, [], [square], chain[-1])
-    inner = lax.ppermute(released, "col", INNER)
-    outer = lax.ppermute(released, "col", INWARD)
-    block_r = gather_step(1, block_r)
-    parent_step(3, wholes[2])
-    far = lax.ppermute(outer, "col", INNER)
-    (first,) = route_step((0, square, inner), also=[outer])
-    block_r = gather_step(2, block_r)
-    block_r = gather_step(3, block_r)
-    received, kept, sums = [], [], []
+    early = exchange(parent_step(0))
+    (square,) = after(chain[-1], square)
+    squares_of = lax.all_gather(square, "col", axis=0)
+    late = parent_step(1)
+    late_across = lax.ppermute(late, "row", ACROSS)
+    late_beside = lax.ppermute(late, "row", SIBLING)
+    block_r = gather_step(0, early, None)
+    (late_across,) = after(chain[-1], late_across)
+    late_other = lax.ppermute(late_across, "row", SIBLING)
+    block_r = gather_step(1, [late, late_beside, late_across, late_other], block_r)
+    received, kept = [], []
     for n in range(nodes):
         which = (1 - core)[None].astype(jnp.int32)
         sent = transposed(which, taken, n, block_r, chain[-1])
         received.append(lax.ppermute(sent, "row", SIBLING))
         chain.append([sent])
-    (second,) = route_step((1, far, inner))
     for n in range(nodes):
         which = core[None].astype(jnp.int32)
         keep = transposed(which, taken, n, block_r, chain[-1])
         kept.append(keep)
         chain.append([keep])
-    for n in range(nodes):
-        both = (kept[n] + received[n]).reshape(2, share_one, width_two)
-        mine = lax.dynamic_index_in_dim(both, chip, 0, keepdims=False)
-        theirs = lax.dynamic_index_in_dim(both, 1 - chip, 0, keepdims=False)
-        sums.append(mine + lax.ppermute(theirs, "row", ACROSS))
+    theirs, mine = halved_sums(here, kept, received, chain[-1])
+    chain.append([mine])
+    sums = mine + lax.ppermute(theirs, "row", ACROSS)
     pairs = pair_terms(heads, block_r, chain[-1])
     chain.append([pairs])
-    own_rows, _ = with_parent(
-        choice, [square, outer, inner, far, first, second], whole_j, None, 0, chain[-1]
-    )
+    own_rows, _ = with_parent(parents_here, squares_of, whole_j, None, 0, chain[-1])
     blocks_j, terms_two = [], []
     for n in range(nodes):
         own_j = own_rows[:, n * width_two : (n + 1) * width_two]

time: 334 us -> 281 us (0.84)
  Pallas kernels: 91.8 us -> 75.4 us
  starting transfers between devices: 28.2 us -> 12.2 us
  local copies, waits for them, and re-layouts: 27 us -> 13.4 us
  other arithmetic: 13 us -> 6.52 us
    pallas_call x13 -> x9, Pallas kernels: 57.7 us -> 42.5 us  [the longest x3 17.8 us: with_parent(): pl.pallas_call(kernel, grid=(1,), in_specs=[SCALARS, ANYWHERE] + [pl.Bloc...]
    ppermute x5 -> x2, waiting for transfers between devices: 73.3 us -> 58.2 us  [exchange(): across = lax.ppermute(x, 'row', ACROSS)]
    unnamed x81 -> x39, local copies, waits for them, and re-layouts: 24.3 us -> 12.5 us
    ppermute x8 -> x4, starting transfers between devices: 14.6 us -> 3.23 us  [the longest x1 1.54 us: line_body(): late_across = lax.ppermute(late, 'row', ACROSS)]
    all_gather x0 -> x1, waiting for transfers between devices: none -> 5.89 us  [line_body(): squares_of = lax.all_gather(square, 'col', axis=0)]
    ppermute x1, waiting for transfers between devices: 18.3 us -> 23.7 us  [line_body(): across_same = lax.ppermute(to_chip, 'row', ACROSS)]
    ppermute x5 -> x2, starting transfers between devices: 9.24 us -> 4.56 us  [exchange(): across = lax.ppermute(x, 'row', ACROSS)]
    all_gather x4 -> x2, waiting for transfers between devices: 31.8 us -> 36.4 us  [line_body(): gathered = [lax.all_gather(x, 'col', axis=0) for x in own]]
  transfers between devices with their start and end apart: 34 -> 20, of which waited for: 12 -> 9; matrix products, arithmetic and copies ran while one was open for 6% -> 5% of each run, Pallas kernels for 26% -> 22%
where the time goes in v1:
time: 281 us; the launch traced here: 280 us
  waiting for transfers between devices  150 us (53%)
  Pallas kernels  75.4 us (27%)
  between operations  14.1 us (5%)
  local copies, waits for them, and re-layouts  13.4 us (5%)
  starting transfers between devices  12.2 us (4%)
  matrix products  7.82 us (3%)
  other arithmetic  6.52 us (2%)
    ppermute x2, waiting for transfers between devices, exchange(): across = lax.ppermute(x, 'row', ACROSS)  58.2 us
    all_gather x2, waiting for transfers between devices, line_body(): gathered = [lax.all_gather(x, 'col', axis=0) for x in own]  36.4 us
    ppermute x1, waiting for transfers between devices, line_body(): across_same = lax.ppermute(to_chip, 'row', ACROSS)  23.7 us
    ppermute x1, waiting for transfers between devices, line_body(): sums = mine + lax.ppermute(theirs, 'row', ACROSS)  20.2 us
    pallas_call x3, Pallas kernels, with_parent(): pl.pallas_call(kernel, grid=(1,), in_specs=[SCALARS, ANYWHERE] + [pl.Bloc...  17.8 us
    pallas_call x2, Pallas kernels, root_step(): pl.pallas_call(kernel, grid=(nodes * tiles,), in_specs=[SCALARS, ANYWHERE...  16.6 us
    unnamed x39, local copies, waits for them, and re-layouts  12.5 us
    pallas_call x4, Pallas kernels, transposed(): pl.pallas_call(kernel, grid=(1,), in_specs=[SCALARS] + [pl.BlockSpec((Non...  9.77 us
  transfers between devices with their start and end apart: 20, of which 9 were waited for; matrix products, arithmetic and copies ran while one was open for 5% of the time, Pallas kernels for 22%

profile of v1, /device:TPU:0, one launch (start us, length us, event | category | flops | bytes accessed | tf_op | source)
XLA Modules:
  0.0 279.9 jit_solution(16405720198627747862)
XLA Ops:
  8.8 6.9 %shard_map.129 = (f32[384,1024]{1,0:T(8,128)}, f32[128,1024]{1,0:T(8,128)}) custom-call(f32[512,1024]{1,0:T(8,128)S(1)} %bitcast.63, f32[1024,1024]{1,0:T(8,128)} %bitcast.65), custom_call_target="tpu_custom_call" | custom-call | flops 1 | bytes 1 | tf_op jit(solution)/shard_map/pallas_call | solution.py:144
  18.4 3.0 %collective-permute-start.1 = (f32[2,256,512]{2,1,0:T(8,128)S(1)}, f32[2,256,512]{2,1,0:T(8,128)}, u32[]{:S(2)}, u32[]{:S(2)}) collective-permute-start(f32[2,256,512]{2,1,0:T(8,128)S(1)} %fusion.5.refs_0_), channel_id=1, source_target_pairs={{0,8},{8,0},{4,12},{12,4},{1,9},{9,1},{5,13},{13,5},{2,10},{10,2},... | collective-permute-start | bytes 3145736 | tf_op jit(solution)/shard_map/ppermute | solution.py:501
  21.5 23.3 %collective-permute-done.1.refs_2_ = f32[2,256,512]{2,1,0:T(8,128)} collective-permute-done((f32[2,256,512]{2,1,0:T(8,128)S(1)}, f32[2,256,512]{2,1,0:T(8,128)}, u32[]{:S(2)}, u32[]{:S(2)}) %collective-permute-start.1) | collective-permute-done | bytes 1048608 | tf_op jit(solution)/shard_map/ppermute | solution.py:501
  46.2 4.8 %shard_map.130.refs_4_.refs_0_ = f32[256,1024]{1,0:T(8,128)S(1)} custom-call(f32[1024,256]{1,0:T(8,128)S(1)} %get-tuple-element.29.columns_ref, f32[1024,1024]{1,0:T(8,128)} %bitcast.66, f32[384,1024]{1,0:T(8,128)} %get-tuple-element.15.refs_0_), custom_call_target="tpu_custom_call" | custom-call | flops 1 | bytes 1 | tf_op jit(solution)/shard_map/pallas_call | solution.py:191
  51.2 4.2 %shard_map.131.refs_2_.whole_ref = f32[2,1024,512]{2,1,0:T(8,128)} custom-call(s32[4]{0:T(128)S(1)} %pad_add_fusion.1.order_ref, f32[2,256,512]{2,1,0:T(8,128)S(1)} %fusion.5.refs_0_, f32[2,256,512]{2,1,0:T(8,128)} %collective-permute-done.refs_1_, f32[2,256,512]{2,1,0:T(8,128)} %collective-permute-done.1.refs_2_, ...), custom_call_target="tpu_custom_call" | custom-call | flops 1 | bytes 1 | tf_op jit(solution)/shard_map/pallas_call | solution.py:260
  55.4 2.6 shard_map.132
  60.0 23.7 %collective-permute-done.4.refs_3_ = f32[512,512]{1,0:T(8,128)} collective-permute-done((f32[512,512]{1,0:T(8,128)S(1)}, f32[512,512]{1,0:T(8,128)}, u32[]{:S(2)}, u32[]{:S(2)}) %collective-permute-start.4) | collective-permute-done | bytes 1048608 | tf_op jit(solution)/shard_map/ppermute | solution.py:522
  83.9 5.5 %fusion.refs_0_ = f32[2,512,512]{2,1,0:T(8,128)} fusion(f32[2,512,512]{2,1,0:T(8,128)} %param.15, f32[2,512,512]{2,1,0:T(8,128)} %param.14, f32[2,512]{1,0:T(2,128)S(1)} %compare_convert_fusion, f32[2,512]{1,0:T(2,128)S(1)} %mul.64), kind=kOutput, calls=%fused_computation.1 | convolution fusion | flops 1611661312 | bytes 6299648 | tf_op jit(solution)/shard_map/nak,nkm->nam/dot_general | solution.py:27
  89.4 8.1 %shard_map.133.refs_1_ = f32[1,1024]{1,0:T(1,128)S(1)} custom-call(s32[2]{0:T(128)S(1)} %pad_add_fusion.place_ref.chip_ref, f32[512,2048]{1,0:T(8,128)} %root_ref.5, f32[384,1024]{1,0:T(8,128)} %get-tuple-element.15.refs_0_, f32[128,1024]{1,0:T(8,128)} %get-tuple-element.16.refs_1_, f32[512,512]{1,0:T(8,128)} %collective-permute-done.3.refs_2_, ...), custom_call_target="tpu_custom_call" | custom-call | flops 1 | bytes 1 | tf_op jit(solution)/shard_map/pallas_call | solution.py:358
  97.5 36.4 %all-gather.7.cloned.1.call-done = f32[1536,1024]{1,0:T(8,128)} async-done(((f32[384,1024]{1,0:T(8,128)}), f32[1536,1024]{1,0:T(8,128)}) %all-gather.7.cloned.1.call-update) | async-done | bytes 6291472 | tf_op jit(solution)/shard_map/all_gather | solution.py:508
  135.5 6.8 %shard_map.134 = (f32[384,1024]{1,0:T(8,128)S(1)}, f32[2,384,1024]{2,1,0:T(8,128)}) custom-call(s32[2]{0:T(128)S(1)} %copy-done.12, f32[4,384,1024]{2,1,0:T(8,128)} %bitcast.67, f32[2,1024,512]{2,1,0:T(8,128)} %shard_map.131.refs_2_.whole_ref, f32[2,512,512]{2,1,0:T(8,128)S(1)} %copy-done.6, f32[1,1024]{1,0:T(1,128)S(1)} %shard_map.133.refs_1_), custom_call_target="tpu_custom_call" | custom-call | flops 1 | bytes 1 | tf_op jit(solution)/shard_map/pallas_call | solution.py:229
  145.0 35.0 %collective-permute-done.9.refs_2_ = f32[384,1024]{1,0:T(8,128)} collective-permute-done((f32[384,1024]{1,0:T(8,128)S(1)}, f32[384,1024]{1,0:T(8,128)}, u32[]{:S(2)}, u32[]{:S(2)}) %collective-permute-start.9) | collective-permute-done | bytes 1572896 | tf_op jit(solution)/shard_map/ppermute | solution.py:501
  181.6 5.1 %shard_map.135 = (f32[128,1024]{1,0:T(8,128)}, f32[2,128,1024]{2,1,0:T(8,128)S(1)}) custom-call(s32[2]{0:T(128)S(1)} %copy-done.12, f32[4,128,1024]{2,1,0:T(8,128)S(1)} %bitcast.64, f32[2,1024,512]{2,1,0:T(8,128)} %shard_map.131.refs_2_.whole_ref, f32[2,512,512]{2,1,0:T(8,128)} %fusion.refs_0_, f32[384,1024]{1,0:T(8,128)S(1)} %get-tuple-element.19.refs_1_.refs_0_), custom_call_target="tpu_custom_call" | custom-call | flops 1 | bytes 1 | tf_op jit(solution)/shard_map/pallas_call | solution.py:229
  188.5 10.1 %shard_map.136.refs_1_.refs_4_.refs_5_ = f32[2,512,512]{2,1,0:T(8,128)} custom-call(s32[4]{0:T(128)S(1)} %pad_add_fusion.1.order_ref, f32[512,2048]{1,0:T(8,128)} %root_ref.5, f32[384,1024]{1,0:T(8,128)S(1)} %get-tuple-element.19.refs_1_.refs_0_, f32[384,1024]{1,0:T(8,128)} %collective-permute-done.8.refs_1_, f32[384,1024]{1,0:T(8,128)} %collective-permute-done.9.refs_2_, ...), custom_call_target="tpu_custom_call" | custom-call | flops 1 | bytes 1 | tf_op jit(solution)/shard_map/pallas_call | solution.py:400
  198.7 2.7 collective-permute-done.7.refs_0_
  206.1 6.4 %shard_map.138.refs_2_.refs_3_ = f32[2,512,512]{2,1,0:T(8,128)} custom-call(s32[4]{0:T(128)S(1)} %pad_add_fusion.1.order_ref, f32[512,2048]{1,0:T(8,128)} %root_ref.5, f32[128,1024]{1,0:T(8,128)} %get-tuple-element.20.refs_4_.refs_0_.refs_1_, f32[128,1024]{1,0:T(8,128)} %collective-permute-done.6.refs_1_, f32[128,1024]{1,0:T(8,128)} %shard_map.137.refs_2_, ...), custom_call_target="tpu_custom_call" | custom-call | flops 1 | bytes 1 | tf_op jit(solution)/shard_map/pallas_call | solution.py:400
  214.1 2.4 shard_map.139.refs_3_
  216.7 2.5 shard_map.140.refs_3_
  219.6 2.4 shard_map.141.refs_3_.refs_0_
  222.1 2.4 shard_map.142.refs_1_.refs_4_
  225.5 2.4 shard_map.143
  233.3 20.2 %collective-permute-done.16 = f32[2,256,512]{2,1,0:T(8,128)} collective-permute-done((f32[2,256,512]{2,1,0:T(8,128)}, f32[2,256,512]{2,1,0:T(8,128)}, u32[]{:S(2)}, u32[]{:S(2)}) %collective-permute-start.16) | collective-permute-done | bytes 1048608 | tf_op jit(solution)/shard_map/ppermute | solution.py:568
  254.9 5.9 %all-gather.11.cloned.1.call-done = f32[1024,1024]{1,0:T(8,128)} async-done(((f32[256,1024]{1,0:T(8,128)}), f32[1024,1024]{1,0:T(8,128)}) %all-gather.11.cloned.1.call-update) | async-done | bytes 4194320 | tf_op jit(solution)/shard_map/all_gather | solution.py:547
  260.8 5.9 %shard_map.146 = (f32[256,1024]{1,0:T(8,128)S(1)}, f32[2,256,1024]{2,1,0:T(8,128)}) custom-call(s32[2]{0:T(128)S(1)} %copy-done.12, f32[4,256,1024]{2,1,0:T(8,128)} %bitcast.68, f32[2,1024,512]{2,1,0:T(8,128)} %shard_map.131.refs_2_.whole_ref, f32[2,512]{1,0:T(2,128)S(1)} %shard_map.144.refs_0_), custom_call_target="tpu_custom_call" | custom-call | flops 1 | bytes 1 | tf_op jit(solution)/shard_map/pallas_call | solution.py:229
  (105 shorter events, 36.9 us)
Async XLA Ops:
  7.2 126.8 %all-gather.7.cloned.1.call-start = ((), (), s32[]{:S(2)}) async-start(), calls=%async_computation | async-start | bytes 7864320 | tf_op jit(solution)/shard_map/all_gather | solution.py:508
  15.7 164.3 %all-gather.9.cloned.1.call-start = ((), (), s32[]{:S(2)}) async-start(), calls=%async_computation.1 | async-start | bytes 2621440 | tf_op jit(solution)/shard_map/all_gather | solution.py:508
  18.4 32.7 %copy-start.7 = (f32[2,256,512]{2,1,0:T(8,128)}, f32[2,256,512]{2,1,0:T(8,128)S(1)}, u32[]{:S(2)}) copy-start(f32[2,256,512]{2,1,0:T(8,128)S(1)} %fusion.5.refs_0_) | copy-start | bytes 3145732
  18.4 26.3 %collective-permute-start.1 = (f32[2,256,512]{2,1,0:T(8,128)S(1)}, f32[2,256,512]{2,1,0:T(8,128)}, u32[]{:S(2)}, u32[]{:S(2)}) collective-permute-start(f32[2,256,512]{2,1,0:T(8,128)S(1)} %fusion.5.refs_0_), channel_id=1, source_target_pairs={{0,8},{8,0},{4,12},{12,4},{1,9},{9,1},{5,13},{13,5},{2,10},{10,2},... | collective-permute-start | bytes 3145736 | tf_op jit(solution)/shard_map/ppermute | solution.py:501
  21.5 29.7 %collective-permute-start = (f32[2,256,512]{2,1,0:T(8,128)S(1)}, f32[2,256,512]{2,1,0:T(8,128)}, u32[]{:S(2)}, u32[]{:S(2)}) collective-permute-start(f32[2,256,512]{2,1,0:T(8,128)S(1)} %fusion.5.refs_0_), channel_id=1, source_target_pairs={{0,4},{4,0},{8,12},{12,8},{1,5},{5,1},{9,13},{13,9},{2,6},{6,2},{1... | collective-permute-start | bytes 3145736 | tf_op jit(solution)/shard_map/ppermute | solution.py:502
  44.7 6.4 %collective-permute-start.2 = (f32[2,256,512]{2,1,0:T(8,128)}, f32[2,256,512]{2,1,0:T(8,128)}, u32[]{:S(2)}, u32[]{:S(2)}) collective-permute-start(f32[2,256,512]{2,1,0:T(8,128)} %collective-permute-done.1.refs_2_), channel_id=1, source_target_pairs={{0,4},{4,0},{8,12},{12,8},{1,5},{5,1},{9,13},{13,9},{2,6},{6,2},{1... | collective-permute-start | bytes 3145736 | tf_op jit(solution)/shard_map/ppermute | solution.py:503
  44.7 216.1 %all-gather.11.cloned.1.call-start = ((), (), s32[]{:S(2)}) async-start(), calls=%async_computation.2 | async-start | bytes 5242880 | tf_op jit(solution)/shard_map/all_gather | solution.py:547
  55.4 28.3 %copy-start.17 = (s32[2,8]{1,0:T(2,128)S(1)}, s32[2,8]{1,0:T(2,128)}, u32[]{:S(2)}) copy-start(s32[2,8]{1,0:T(2,128)} %param.19) | copy-start | bytes 196
  58.1 25.7 %collective-permute-start.4 = (f32[512,512]{1,0:T(8,128)S(1)}, f32[512,512]{1,0:T(8,128)}, u32[]{:S(2)}, u32[]{:S(2)}) collective-permute-start(f32[512,512]{1,0:T(8,128)S(1)} %get-tuple-element.18.refs_5_), channel_id=1, source_target_pairs={{0,8},{8,0},{4,12},{12,4},{1,9},{9,1},{5,13},{13,5},{2,10},{10,2},... | collective-permute-start | bytes 3145736 | tf_op jit(solution)/shard_map/ppermute | solution.py:522
  59.8 29.6 %collective-permute-start.3 = (f32[512,512]{1,0:T(8,128)}, f32[512,512]{1,0:T(8,128)}, u32[]{:S(2)}, u32[]{:S(2)}) collective-permute-start(f32[512,512]{1,0:T(8,128)} %get-tuple-element.17), channel_id=1, source_target_pairs={{0,4},{4,0},{8,12},{12,8},{1,5},{5,1},{9,13},{13,9},{2,6},{6,2},{1... | collective-permute-start | bytes 3145736 | tf_op jit(solution)/shard_map/ppermute | solution.py:524
  83.7 5.6 %collective-permute-start.5 = (f32[512,512]{1,0:T(8,128)}, f32[512,512]{1,0:T(8,128)}, u32[]{:S(2)}, u32[]{:S(2)}) collective-permute-start(f32[512,512]{1,0:T(8,128)} %collective-permute-done.4.refs_3_), channel_id=1, source_target_pairs={{0,4},{4,0},{8,12},{12,8},{1,5},{5,1},{9,13},{13,9},{2,6},{6,2},{1... | collective-permute-start | bytes 3145736 | tf_op jit(solution)/shard_map/ppermute | solution.py:523
  89.4 44.6 %copy-start.12 = (s32[2]{0:T(128)S(1)}, s32[2]{0:T(128)}, u32[]{:S(2)}) copy-start(s32[2]{0:T(128)} %parents_ref.5) | copy-start | bytes 28
  142.3 46.2 %copy-start.4 = (f32[384,1024]{1,0:T(8,128)}, f32[384,1024]{1,0:T(8,128)S(1)}, u32[]{:S(2)}) copy-start(f32[384,1024]{1,0:T(8,128)S(1)} %get-tuple-element.19.refs_1_.refs_0_) | copy-start | bytes 4718596
  143.5 36.5 %collective-permute-start.9 = (f32[384,1024]{1,0:T(8,128)S(1)}, f32[384,1024]{1,0:T(8,128)}, u32[]{:S(2)}, u32[]{:S(2)}) collective-permute-start(f32[384,1024]{1,0:T(8,128)S(1)} %get-tuple-element.19.refs_1_.refs_0_), channel_id=1, source_target_pairs={{0,8},{8,0},{4,12},{12,4},{1,9},{9,1},{5,13},{13,5},{2,10},{10,2},... | collective-permute-start | bytes 4718600 | tf_op jit(solution)/shard_map/ppermute | solution.py:501
  145.0 43.5 %collective-permute-start.8 = (f32[384,1024]{1,0:T(8,128)S(1)}, f32[384,1024]{1,0:T(8,128)}, u32[]{:S(2)}, u32[]{:S(2)}) collective-permute-start(f32[384,1024]{1,0:T(8,128)S(1)} %get-tuple-element.19.refs_1_.refs_0_), channel_id=1, source_target_pairs={{0,4},{4,0},{8,12},{12,8},{1,5},{5,1},{9,13},{13,9},{2,6},{6,2},{1... | collective-permute-start | bytes 4718600 | tf_op jit(solution)/shard_map/ppermute | solution.py:502
  180.0 8.5 %collective-permute-start.10 = (f32[384,1024]{1,0:T(8,128)}, f32[384,1024]{1,0:T(8,128)}, u32[]{:S(2)}, u32[]{:S(2)}) collective-permute-start(f32[384,1024]{1,0:T(8,128)} %collective-permute-done.9.refs_2_), channel_id=1, source_target_pairs={{0,4},{4,0},{8,12},{12,8},{1,5},{5,1},{9,13},{13,9},{2,6},{6,2},{1... | collective-permute-start | bytes 4718600 | tf_op jit(solution)/shard_map/ppermute | solution.py:503
  186.7 14.6 %collective-permute-start.7 = (f32[128,1024]{1,0:T(8,128)}, f32[128,1024]{1,0:T(8,128)S(1)}, u32[]{:S(2)}, u32[]{:S(2)}) collective-permute-start(f32[128,1024]{1,0:T(8,128)} %get-tuple-element.20.refs_4_.refs_0_.refs_1_), channel_id=1, source_target_pairs={{0,8},{8,0},{4,12},{12,4},{1,9},{9,1},{5,13},{13,5},{2,10},{10,2},... | collective-permute-start | bytes 1572872 | tf_op jit(solution)/shard_map/ppermute | solution.py:549
  188.3 15.5 %collective-permute-start.6 = (f32[128,1024]{1,0:T(8,128)}, f32[128,1024]{1,0:T(8,128)}, u32[]{:S(2)}, u32[]{:S(2)}) collective-permute-start(f32[128,1024]{1,0:T(8,128)} %get-tuple-element.20.refs_4_.refs_0_.refs_1_), channel_id=1, source_target_pairs={{0,4},{4,0},{8,12},{12,8},{1,5},{5,1},{9,13},{13,9},{2,6},{6,2},{1... | collective-permute-start | bytes 1572872 | tf_op jit(solution)/shard_map/ppermute | solution.py:550
  203.8 2.3 collective-permute-start.11
  216.6 8.0 %collective-permute-start.12 = (f32[512,512]{1,0:T(8,128)S(1)}, f32[512,512]{1,0:T(8,128)S(1)}, u32[]{:S(2)}, u32[]{:S(2)}) collective-permute-start(f32[512,512]{1,0:T(8,128)S(1)} %shard_map.139.refs_3_), channel_id=1, source_target_pairs={{0,4},{4,0},{8,12},{12,8},{1,5},{5,1},{9,13},{13,9},{2,6},{6,2},{1... | collective-permute-start | bytes 3145736 | tf_op jit(solution)/shard_map/ppermute | solution.py:559
  219.2 5.4 %collective-permute-start.13 = (f32[512,512]{1,0:T(8,128)S(1)}, f32[512,512]{1,0:T(8,128)S(1)}, u32[]{:S(2)}, u32[]{:S(2)}) collective-permute-start(f32[512,512]{1,0:T(8,128)S(1)} %shard_map.140.refs_3_), channel_id=1, source_target_pairs={{0,4},{4,0},{8,12},{12,8},{1,5},{5,1},{9,13},{13,9},{2,6},{6,2},{1... | collective-permute-start | bytes 3145736 | tf_op jit(solution)/shard_map/ppermute | solution.py:559
  228.0 25.5 %collective-permute-start.16 = (f32[2,256,512]{2,1,0:T(8,128)}, f32[2,256,512]{2,1,0:T(8,128)}, u32[]{:S(2)}, u32[]{:S(2)}) collective-permute-start(f32[2,256,512]{2,1,0:T(8,128)} %get-tuple-element.25), channel_id=1, source_target_pairs={{0,8},{8,0},{4,12},{12,4},{1,9},{9,1},{5,13},{13,5},{2,10},{10,2},... | collective-permute-start | bytes 3145736 | tf_op jit(solution)/shard_map/ppermute | solution.py:568
  267.2 1.3 collective-permute-start.14
  268.6 3.7 %collective-permute-start.15 = (f32[512]{0:T(512)S(1)}, f32[512]{0:T(512)S(1)}, u32[]{:S(2)}, u32[]{:S(2)}) collective-permute-start(f32[512]{0:T(512)S(1)} %bitcast.75), channel_id=1, source_target_pairs={{0,8},{8,0},{4,12},{12,4},{1,9},{9,1},{5,13},{13,5},{2,10},{10,2},... | collective-permute-start | bytes 6152 | tf_op jit(solution)/shard_map/ppermute | solution.py:587
  (15 other events, 49.6 us)
Sparse Core Ops, SparseCore 0:
  15.9 118.0 all-gather.6
  135.5 44.1 all-gather.8
  181.3 79.4 all-gather.10

commit v2 on v1

--- a/solution.py
+++ b/solution.py
@@ -99,6 +99,7 @@
 SIBLING = [(0, 1), (1, 0), (2, 3), (3, 2)]
 
 
+CHUNKS = 4
 VMEM_LIMIT = 48 * 1024 * 1024
 ANYWHERE = pl.BlockSpec(memory_space=pl.ANY)
 SCALARS = pl.BlockSpec(memory_space=pltpu.SMEM)
@@ -204,32 +205,34 @@
     )(columns, inverse, *deps)
 
 
-def with_parent(parents, gathered, whole_j, minus, start, deps):
+def with_parent(choice, rotated, whole_j, minus, start, deps):
     nodes, depth, width = whole_j.shape
-    part = gathered.shape[1]
+    part = rotated[0].shape[0]
+    count = len(rotated)
     extra = [] if minus is None else [minus]
 
-    def kernel(parents_ref, gathered_ref, whole_ref, *refs):
+    def kernel(choice_ref, *refs):
+        whole_ref = refs[count]
         out_ref, chosen_ref, sems = refs[-3:]
-
-        def copy(n):
-            return pltpu.make_async_copy(
-                gathered_ref.at[parents_ref[n]], chosen_ref.at[n], sems.at[n]
-            )
-
         for n in range(nodes):
-            copy(n).start()
+            for k in range(count):
+
+                @pl.when(choice_ref[n] == k)
+                def _():
+                    pltpu.make_async_copy(refs[k], chosen_ref.at[n], sems.at[n]).start()
+
         for n in range(nodes):
-            copy(n).wait()
+            pltpu.make_async_copy(refs[0], chosen_ref.at[n], sems.at[n]).wait()
             result = three(split(chosen_ref[n]), split(whole_ref[n]))
             if extra:
-                result = result - refs[0][n, start : start + part, :]
+                result = result - refs[count + 1][n, start : start + part, :]
             out_ref[:, n * width : (n + 1) * width] = result
 
     return pl.pallas_call(
         kernel,
         grid=(1,),
-        in_specs=[SCALARS, ANYWHERE]
+        in_specs=[SCALARS]
+        + [ANYWHERE] * count
         + [pl.BlockSpec(x.shape, lambda i: (0, 0, 0)) for x in [whole_j] + extra]
         + [ANYWHERE] * len(deps),
         out_specs=[
@@ -243,7 +246,7 @@
         scratch_shapes=[pltpu.SemaphoreType.DMA((nodes,))],
         compiler_params=params(),
         cost_estimate=cost(),
-    )(parents, gathered, whole_j, *extra, *deps)
+    )(choice, *rotated, whole_j, *extra, *deps)
 
 
 def in_order(order, blocks, deps):
@@ -502,56 +505,76 @@
         beside = lax.ppermute(x, "row", SIBLING)
         return [x, beside, across, lax.ppermute(across, "row", SIBLING)]
 
-    sizes = [root_rows - root_rows // 4, root_rows // 4]
-    starts = [0, sizes[0]]
-    own = list(level_one(panel_one[0], inverse, sizes))
-    gathered = [lax.all_gather(x, "col", axis=0) for x in own]
-    own_columns = lax.dynamic_slice_in_dim(inverse, row * share_one, share_one, 1)
-    square = square_rows(own_columns, inverse, [own[0]])
-    chain.append([square])
+    def turn(x):
+        return lax.ppermute(x, "col", [(i, (i + 1) % cols) for i in range(cols)])
+
+    size = root_rows // CHUNKS
+    starts = [q * size for q in range(CHUNKS)]
+    own = list(level_one(panel_one[0], inverse, [size] * CHUNKS))
+    rounds = [own]
+    rounds.append([turn(x) for x in own])
 
     live = live_columns(widths, width_two)
     factor_j, factor_r = masked_factors(
         panel_two_j, panel_two_r, inv_two, live, pattern_j, pattern_r
     )
-    shares_j = exchange(factor_j)
-    whole_j = in_order(order, shares_j, chain[-1])
-    chain.append([whole_j])
-    to_chip, to_core = halves_of(here, own, chain[-1])
-    chain.append([to_chip])
+    (factor_j,) = after([own[0]], factor_j)
+    across_j = lax.ppermute(factor_j, "row", ACROSS)
+    beside_j = lax.ppermute(factor_j, "row", SIBLING)
+    own_columns = lax.dynamic_slice_in_dim(inverse, row * share_one, share_one, 1)
+    square = square_rows(own_columns, inverse, [factor_j])
+    half = CHUNKS // 2
+    (across_j,) = after(rounds[1][:half] + [square, factor_r], across_j)
+    other_j = lax.ppermute(across_j, "row", SIBLING)
+    to_chip, to_core = halves_of(here, own, [across_j])
     across_same = lax.ppermute(to_chip, "row", ACROSS)
+    sibling = lax.ppermute(to_core, "row", SIBLING)
+    whole_j = in_order(
+        order, [factor_j, beside_j, across_j, other_j], rounds[1][half:] + [to_chip]
+    )
+    rounds.append([turn(x) for x in rounds[1]])
+    (across_same,) = after(rounds[2] + [whole_j, sibling], across_same)
+    chain.append([across_same])
+    rounds.append([turn(x) for x in rounds[2]])
     across_other = lax.ppermute(across_same, "row", SIBLING)
-    sibling = lax.ppermute(to_core, "row", SIBLING)
-
-    heads, taken = [], []
-    parents_here = parents.astype(jnp.int32)
+
+    heads, taken, wholes = [], [], []
+    choice = ((col - parents) % cols).astype(jnp.int32)
 
     def parent_step(q):
         out, chosen = with_parent(
-            parents_here, gathered[q], whole_j, factor_r, starts[q], chain[-1]
+            choice, [r[q] for r in rounds], whole_j, factor_r, starts[q], chain[-1]
         )
         heads.append(out)
         taken.append(chosen)
+        wholes.append(exchange(out) if q < CHUNKS - 1 else None)
         chain.append([out])
         return out
 
-    def gather_step(q, parts, before):
-        out = root_step(order, zroot, starts[q], parts, before, nodes, chain[-1])
+    def gather_step(q, before):
+        out = root_step(order, zroot, starts[q], wholes[q], before, nodes, chain[-1])
         chain.append([out])
         return out
 
-    terms_one = root_terms(here, zroot, own, sibling, across_same, across_other, chain[-1])
-    chain.append([terms_one])
-    early = exchange(parent_step(0))
+    parent_step(0)
+    parent_step(1)
     (square,) = after(chain[-1], square)
-    squares_of = lax.all_gather(square, "col", axis=0)
-    late = parent_step(1)
+    chain.append([square])
+    square_rounds = [square, turn(square)]
+    parent_step(2)
+    block_r = gather_step(0, None)
+    late = parent_step(3)
     late_across = lax.ppermute(late, "row", ACROSS)
     late_beside = lax.ppermute(late, "row", SIBLING)
-    block_r = gather_step(0, early, None)
+    block_r = gather_step(1, block_r)
+    chain.append(chain[-1] + square_rounds[1:])
+    block_r = gather_step(2, block_r)
+    square_rounds.append(turn(square_rounds[-1]))
     (late_across,) = after(chain[-1], late_across)
+    chain.append([late_across])
     late_other = lax.ppermute(late_across, "row", SIBLING)
-    block_r = gather_step(1, [late, late_beside, late_across, late_other], block_r)
+    wholes[-1] = [late, late_beside, late_across, late_other]
+    block_r = gather_step(3, block_r)
     received, kept = [], []
     for n in range(nodes):
         which = (1 - core)[None].astype(jnp.int32)
@@ -563,12 +586,15 @@
         keep = transposed(which, taken, n, block_r, chain[-1])
         kept.append(keep)
         chain.append([keep])
-    theirs, mine = halved_sums(here, kept, received, chain[-1])
+    theirs, mine = halved_sums(here, kept, received, chain[-1] + square_rounds[2:])
+    square_rounds.append(turn(square_rounds[-1]))
     chain.append([mine])
     sums = mine + lax.ppermute(theirs, "row", ACROSS)
+    terms_one = root_terms(here, zroot, own, sibling, across_same, across_other, chain[-1])
+    chain.append([terms_one])
     pairs = pair_terms(heads, block_r, chain[-1])
     chain.append([pairs])
-    own_rows, _ = with_parent(parents_here, squares_of, whole_j, None, 0, chain[-1])
+    own_rows, _ = with_parent(choice, square_rounds, whole_j, None, 0, chain[-1])
     blocks_j, terms_two = [], []
     for n in range(nodes):
         own_j = own_rows[:, n * width_two : (n + 1) * width_two]

time: 281 us -> 257 us (0.915)
  waiting for transfers between devices: 150 us -> 113 us
  Pallas kernels: 75.4 us -> 89 us
  between operations: 14.1 us -> 1.33 us
  local copies, waits for them, and re-layouts: 13.4 us -> 22.5 us
    ppermute x0 -> x18, waiting for transfers between devices: none -> 102 us  [the longest x15 102 us: turn(): return lax.ppermute(x, 'col', [(i, (i + 1) % cols) for i in range(cols)])]
    ppermute x2 -> x3, waiting for transfers between devices: 58.2 us -> 4.07 us  [exchange(): across = lax.ppermute(x, 'row', ACROSS)]
    all_gather x3 -> x0, waiting for transfers between devices: 42.3 us -> none  [the longest x2 36.4 us: line_body(): gathered = [lax.all_gather(x, 'col', axis=0) for x in own]]
    ppermute x1, waiting for transfers between devices: 23.7 us -> 0.01 us  [line_body(): across_same = lax.ppermute(to_chip, 'row', ACROSS)]
    ppermute x1, waiting for transfers between devices: 20.2 us -> 3.31 us  [line_body(): sums = mine + lax.ppermute(theirs, 'row', ACROSS)]
    ppermute x0 -> x18, starting transfers between devices: none -> 9.68 us  [the longest x15 6.57 us: turn(): return lax.ppermute(x, 'col', [(i, (i + 1) % cols) for i in range(cols)])]
    unnamed x39 -> x101, local copies, waits for them, and re-layouts: 12.5 us -> 21.6 us
    pallas_call x3 -> x5, Pallas kernels: 17.8 us -> 24.7 us  [with_parent(): pl.pallas_call(kernel, grid=(1,), in_specs=[SCALARS] + [ANYWHERE] * count...]
  transfers between devices with their start and end apart: 20 -> 38, of which waited for: 9 -> 17; matrix products, arithmetic and copies ran while one was open for 5% -> 4% of each run, Pallas kernels for 22% -> 32%
where the time goes in v2:
time: 257 us; the launch traced here: 255 us
  waiting for transfers between devices  113 us (44%)
  Pallas kernels  89 us (35%)
  local copies, waits for them, and re-layouts  22.5 us (9%)
  starting transfers between devices  14.2 us (6%)
  other arithmetic  8.05 us (3%)
  matrix products  6.55 us (3%)
    ppermute x15, waiting for transfers between devices, turn(): return lax.ppermute(x, 'col', [(i, (i + 1) % cols) for i in range(cols)])  102 us
    pallas_call x5, Pallas kernels, with_parent(): pl.pallas_call(kernel, grid=(1,), in_specs=[SCALARS] + [ANYWHERE] * count...  24.7 us
    pallas_call x4, Pallas kernels, root_step(): pl.pallas_call(kernel, grid=(nodes * tiles,), in_specs=[SCALARS, ANYWHERE...  22.3 us
    unnamed x101, local copies, waits for them, and re-layouts  21.6 us
    pallas_call x4, Pallas kernels, transposed(): pl.pallas_call(kernel, grid=(1,), in_specs=[SCALARS] + [pl.BlockSpec((Non...  9.16 us
    pallas_call x1, Pallas kernels, root_terms(): pl.pallas_call(kernel, in_specs=[SCALARS] + [WHOLE] * (1 + count + 3) + [...  7.5 us
    pallas_call x1, Pallas kernels, level_one(): pl.pallas_call(kernel, grid=(width // tile,), in_specs=[pl.BlockSpec((roo...  6.83 us
    ppermute x15, starting transfers between devices, turn(): return lax.ppermute(x, 'col', [(i, (i + 1) % cols) for i in range(cols)])  6.57 us
  transfers between devices with their start and end apart: 38, of which 17 were waited for; matrix products, arithmetic and copies ran while one was open for 4% of the time, Pallas kernels for 32%

profile of v2, /device:TPU:0, one launch (start us, length us, event | category | flops | bytes accessed | tf_op | source)
XLA Modules:
  0.0 254.9 jit_solution(1776540892785599881)
XLA Ops:
  3.8 6.8 %shard_map.129 = (f32[128,1024]{1,0:T(8,128)S(1)}, f32[128,1024]{1,0:T(8,128)S(1)}, f32[128,1024]{1,0:T(8,128)}, f32[128,1024]{1,0:T(8,128)}) custom-call(f32[512,1024]{1,0:T(8,128)S(1)} %bitcast.60, f32[1024,1024]{1,0:T(8,128)} %bitcast.61), custom_call_target="tpu_custom_call" | custom-call | flops 1 | bytes 1 | tf_op jit(solution)/shard_map/pallas_call | solution.py:145
  19.8 5.4 %fusion.refs_4_.refs_5_ = f32[2,512,512]{2,1,0:T(8,128)} fusion(f32[2,512,512]{2,1,0:T(8,128)} %param.15, f32[2,512,512]{2,1,0:T(8,128)} %param.14, f32[2,512]{1,0:T(2,128)S(1)} %compare_convert_fusion, f32[2,512]{1,0:T(2,128)S(1)} %mul.64), kind=kOutput, calls=%fused_computation.1 | convolution fusion | flops 1611661312 | bytes 6299648 | tf_op jit(solution)/shard_map/nak,nkm->nam/dot_general | solution.py:27
  25.2 6.4 %collective-permute-done.1.refs_1_ = f32[128,1024]{1,0:T(8,128)} collective-permute-done((f32[128,1024]{1,0:T(8,128)S(1)}, f32[128,1024]{1,0:T(8,128)}, u32[]{:S(2)}, u32[]{:S(2)}) %collective-permute-start.1) | collective-permute-done | bytes 524320 | tf_op jit(solution)/shard_map/ppermute | solution.py:509
  31.7 11.1 %collective-permute-done.2.refs_2_.refs_1_ = f32[128,1024]{1,0:T(8,128)S(1)} collective-permute-done((f32[128,1024]{1,0:T(8,128)S(1)}, f32[128,1024]{1,0:T(8,128)S(1)}, u32[]{:S(2)}, u32[]{:S(2)}) %collective-permute-start.2) | collective-permute-done | bytes 524320 | tf_op jit(solution)/shard_map/ppermute | solution.py:509
  44.4 4.6 %shard_map.131.refs_3_.refs_0_ = f32[256,1024]{1,0:T(8,128)S(1)} custom-call(f32[1024,256]{1,0:T(8,128)S(1)} %get-tuple-element.41.columns_ref, f32[1024,1024]{1,0:T(8,128)} %bitcast.62, f32[2,256,512]{2,1,0:T(8,128)S(1)} %shard_map.130.refs_0_), custom_call_target="tpu_custom_call" | custom-call | flops 1 | bytes 1 | tf_op jit(solution)/shard_map/pallas_call | solution.py:192
  51.5 13.8 %collective-permute-done.9.refs_5_.refs_1_ = f32[128,1024]{1,0:T(8,128)} collective-permute-done((f32[128,1024]{1,0:T(8,128)}, f32[128,1024]{1,0:T(8,128)}, u32[]{:S(2)}, u32[]{:S(2)}) %collective-permute-start.9) | collective-permute-done | bytes 524320 | tf_op jit(solution)/shard_map/ppermute | solution.py:509
  70.6 6.0 %collective-permute-done.5.refs_1_.refs_2_ = f32[128,1024]{1,0:T(8,128)} collective-permute-done((f32[128,1024]{1,0:T(8,128)}, f32[128,1024]{1,0:T(8,128)}, u32[]{:S(2)}, u32[]{:S(2)}) %collective-permute-start.5) | collective-permute-done | bytes 524320 | tf_op jit(solution)/shard_map/ppermute | solution.py:509
  76.6 11.1 %collective-permute-done.10.refs_4_.refs_2_ = f32[128,1024]{1,0:T(8,128)S(1)} collective-permute-done((f32[128,1024]{1,0:T(8,128)}, f32[128,1024]{1,0:T(8,128)S(1)}, u32[]{:S(2)}, u32[]{:S(2)}) %collective-permute-start.10) | collective-permute-done | bytes 524320 | tf_op jit(solution)/shard_map/ppermute | solution.py:509
  88.5 10.5 %collective-permute-done.6.refs_2_ = f32[128,1024]{1,0:T(8,128)} collective-permute-done((f32[128,1024]{1,0:T(8,128)S(1)}, f32[128,1024]{1,0:T(8,128)}, u32[]{:S(2)}, u32[]{:S(2)}) %collective-permute-start.6) | collective-permute-done | bytes 524320 | tf_op jit(solution)/shard_map/ppermute | solution.py:509
  104.5 5.8 %collective-permute-done.8.refs_3_.refs_2_ = f32[128,1024]{1,0:T(8,128)} collective-permute-done((f32[128,1024]{1,0:T(8,128)}, f32[128,1024]{1,0:T(8,128)}, u32[]{:S(2)}, u32[]{:S(2)}) %collective-permute-start.8) | collective-permute-done | bytes 524320 | tf_op jit(solution)/shard_map/ppermute | solution.py:509
  111.6 9.9 %collective-permute-done.14.refs_3_ = f32[128,1024]{1,0:T(8,128)} collective-permute-done((f32[128,1024]{1,0:T(8,128)}, f32[128,1024]{1,0:T(8,128)}, u32[]{:S(2)}, u32[]{:S(2)}) %collective-permute-start.14) | collective-permute-done | bytes 524320 | tf_op jit(solution)/shard_map/ppermute | solution.py:509
  121.5 4.7 %shard_map.136 = (f32[128,1024]{1,0:T(8,128)S(1)}, f32[2,128,1024]{2,1,0:T(8,128)S(1)}) custom-call(s32[2]{0:T(128)S(1)} %and_select_fusion.choice_ref, f32[128,1024]{1,0:T(8,128)S(1)} %copy-done.21, f32[128,1024]{1,0:T(8,128)} %collective-permute-done.1.refs_1_, f32[128,1024]{1,0:T(8,128)} %collective-permute-done.5.refs_1_.refs_2_, ...), custom_call_target="tpu_custom_call" | custom-call | flops 1 | bytes 1 | tf_op jit(solution)/shard_map/pallas_call | solution.py:231
  126.6 6.2 %collective-permute-done.15.refs_3_ = f32[128,1024]{1,0:T(8,128)} collective-permute-done((f32[128,1024]{1,0:T(8,128)}, f32[128,1024]{1,0:T(8,128)}, u32[]{:S(2)}, u32[]{:S(2)}) %collective-permute-start.15) | collective-permute-done | bytes 524320 | tf_op jit(solution)/shard_map/ppermute | solution.py:509
  132.8 4.4 %shard_map.137 = (f32[128,1024]{1,0:T(8,128)S(1)}, f32[2,128,1024]{2,1,0:T(8,128)S(1)}) custom-call(s32[2]{0:T(128)S(1)} %and_select_fusion.choice_ref, f32[128,1024]{1,0:T(8,128)S(1)} %copy-done.25, f32[128,1024]{1,0:T(8,128)S(1)} %copy-done.41, f32[128,1024]{1,0:T(8,128)} %collective-permute-done.6.refs_2_, f32[128,1024]{1,0:T(8,128)} %collective-permute-done.15.refs_3_, ...), custom_call_target="tpu_custom_call" | custom-call | flops 1 | bytes 1 | tf_op jit(solution)/shard_map/pallas_call | solution.py:231
  138.6 5.3 %collective-permute-done.16.refs_3_ = f32[128,1024]{1,0:T(8,128)S(1)} collective-permute-done((f32[128,1024]{1,0:T(8,128)}, f32[128,1024]{1,0:T(8,128)S(1)}, u32[]{:S(2)}, u32[]{:S(2)}) %collective-permute-start.16) | collective-permute-done | bytes 524320 | tf_op jit(solution)/shard_map/ppermute | solution.py:509
  143.9 5.3 %shard_map.139 = (f32[128,1024]{1,0:T(8,128)S(1)}, f32[2,128,1024]{2,1,0:T(8,128)S(1)}) custom-call(s32[2]{0:T(128)S(1)} %and_select_fusion.choice_ref, f32[128,1024]{1,0:T(8,128)} %get-tuple-element.23.refs_2_.refs_0_, f32[128,1024]{1,0:T(8,128)} %collective-permute-done.7.refs_4_.refs_1_, f32[128,1024]{1,0:T(8,128)} %collective-permute-done.8.refs_3_.refs_2_, ...), custom_call_target="tpu_custom_call" | custom-call | flops 1 | bytes 1 | tf_op jit(solution)/shard_map/pallas_call | solution.py:231
  151.3 4.6 %shard_map.140.refs_6_.refs_4_ = f32[2,512,512]{2,1,0:T(8,128)S(1)} custom-call(s32[4]{0:T(128)S(1)} %pad_add_fusion.1.order_ref, f32[512,2048]{1,0:T(8,128)} %root_ref.9, f32[128,1024]{1,0:T(8,128)S(1)} %get-tuple-element.28.refs_6_.refs_0_, f32[128,1024]{1,0:T(8,128)S(1)} %collective-permute-done.18.refs_1_, ...), custom_call_target="tpu_custom_call" | custom-call | flops 1 | bytes 1 | tf_op jit(solution)/shard_map/pallas_call | solution.py:403
  161.4 5.5 %shard_map.141 = (f32[128,1024]{1,0:T(8,128)}, f32[2,128,1024]{2,1,0:T(8,128)S(1)}) custom-call(s32[2]{0:T(128)S(1)} %and_select_fusion.choice_ref, f32[128,1024]{1,0:T(8,128)} %get-tuple-element.24.refs_3_.refs_0_, f32[128,1024]{1,0:T(8,128)} %collective-permute-done.9.refs_5_.refs_1_, f32[128,1024]{1,0:T(8,128)S(1)} %copy-done.43, ...), custom_call_target="tpu_custom_call" | custom-call | flops 1 | bytes 1 | tf_op jit(solution)/shard_map/pallas_call | solution.py:231
  167.5 5.6 %shard_map.142.refs_4_.refs_5_ = f32[2,512,512]{2,1,0:T(8,128)S(1)} custom-call(s32[4]{0:T(128)S(1)} %pad_add_fusion.1.order_ref, f32[512,2048]{1,0:T(8,128)} %root_ref.9, f32[128,1024]{1,0:T(8,128)S(1)} %get-tuple-element.30.refs_1_.refs_0_, f32[128,1024]{1,0:T(8,128)S(1)} %collective-permute-done.26.refs_1_, ...), custom_call_target="tpu_custom_call" | custom-call | flops 1 | bytes 1 | tf_op jit(solution)/shard_map/pallas_call | solution.py:403
  176.3 5.6 %shard_map.143.refs_1_.refs_4_ = f32[2,512,512]{2,1,0:T(8,128)S(1)} custom-call(s32[4]{0:T(128)S(1)} %pad_add_fusion.1.order_ref, f32[512,2048]{1,0:T(8,128)} %root_ref.9, f32[128,1024]{1,0:T(8,128)S(1)} %get-tuple-element.32.refs_4_.refs_0_.refs_2_, f32[128,1024]{1,0:T(8,128)S(1)} %collective-permute-done.23.refs_1_, ...), custom_call_target="tpu_custom_call" | custom-call | flops 1 | bytes 1 | tf_op jit(solution)/shard_map/pallas_call | solution.py:403
  185.1 6.4 %shard_map.145.refs_4_.refs_5_ = f32[2,512,512]{2,1,0:T(8,128)} custom-call(s32[4]{0:T(128)S(1)} %pad_add_fusion.1.order_ref, f32[512,2048]{1,0:T(8,128)} %root_ref.9, f32[128,1024]{1,0:T(8,128)} %get-tuple-element.34.refs_5_.refs_0_.refs_3_, f32[128,1024]{1,0:T(8,128)} %collective-permute-done.21.refs_1_, f32[128,1024]{1,0:T(8,128)} %shard_map.144.refs_2_.refs_5_, ...), custom_call_target="tpu_custom_call" | custom-call | flops 1 | bytes 1 | tf_op jit(solution)/shard_map/pallas_call | solution.py:403
  197.8 12.7 %collective-permute-done.33.refs_5_.refs_2_ = f32[256,1024]{1,0:T(8,128)} collective-permute-done((f32[256,1024]{1,0:T(8,128)}, f32[256,1024]{1,0:T(8,128)}, u32[]{:S(2)}, u32[]{:S(2)}) %collective-permute-start.33) | collective-permute-done | bytes 1048608 | tf_op jit(solution)/shard_map/ppermute | solution.py:509
  224.3 7.5 %shard_map.151.refs_5_ = f32[1,1024]{1,0:T(1,128)S(1)} custom-call(s32[2]{0:T(128)S(1)} %pad_add_fusion.place_ref.chip_ref, f32[512,2048]{1,0:T(8,128)} %root_ref.9, f32[128,1024]{1,0:T(8,128)S(1)} %copy-done.22, f32[128,1024]{1,0:T(8,128)S(1)} %copy-done.26, f32[128,1024]{1,0:T(8,128)} %get-tuple-element.23.refs_2_.refs_0_, ...), custom_call_target="tpu_custom_call" | custom-call | flops 1 | bytes 1 | tf_op jit(solution)/shard_map/pallas_call | solution.py:361
  237.4 4.9 %shard_map.153 = (f32[256,1024]{1,0:T(8,128)S(1)}, f32[2,256,1024]{2,1,0:T(8,128)}) custom-call(s32[2]{0:T(128)S(1)} %and_select_fusion.choice_ref, f32[256,1024]{1,0:T(8,128)S(1)} %copy-done.18, f32[256,1024]{1,0:T(8,128)} %collective-permute-done.29.refs_6_.refs_1_, f32[256,1024]{1,0:T(8,128)} %collective-permute-done.33.refs_5_.refs_2_, ...), custom_call_target="tpu_custom_call" | custom-call | flops 1 | bytes 1 | tf_op jit(solution)/shard_map/pallas_call | solution.py:231
  (208 shorter events, 83.2 us)
Async XLA Ops:
  11.9 37.1 %collective-permute-start = (f32[2,256,512]{2,1,0:T(8,128)S(1)}, f32[2,256,512]{2,1,0:T(8,128)}, u32[]{:S(2)}, u32[]{:S(2)}) collective-permute-start(f32[2,256,512]{2,1,0:T(8,128)S(1)} %shard_map.130.refs_0_), channel_id=1, source_target_pairs={{0,8},{8,0},{4,12},{12,4},{1,9},{9,1},{5,13},{13,5},{2,10},{10,2},... | collective-permute-start | bytes 3145736 | tf_op jit(solution)/shard_map/ppermute | solution.py:522
  16.5 26.3 %collective-permute-start.2 = (f32[128,1024]{1,0:T(8,128)S(1)}, f32[128,1024]{1,0:T(8,128)S(1)}, u32[]{:S(2)}, u32[]{:S(2)}) collective-permute-start(f32[128,1024]{1,0:T(8,128)S(1)} %get-tuple-element.22.refs_1_.refs_0_), channel_id=1, source_target_pairs={{0,1},{1,2},{2,3},{3,0},{4,5},{5,6},{6,7},{7,4},{8,9},{9,10},{10,1... | collective-permute-start | bytes 1572872 | tf_op jit(solution)/shard_map/ppermute | solution.py:509
  18.1 52.1 %collective-permute-start.11 = (f32[2,256,512]{2,1,0:T(8,128)S(1)}, f32[2,256,512]{2,1,0:T(8,128)}, u32[]{:S(2)}, u32[]{:S(2)}) collective-permute-start(f32[2,256,512]{2,1,0:T(8,128)S(1)} %shard_map.130.refs_0_), channel_id=1, source_target_pairs={{0,4},{4,0},{8,12},{12,8},{1,5},{5,1},{9,13},{13,9},{2,6},{6,2},{1... | collective-permute-start | bytes 3145736 | tf_op jit(solution)/shard_map/ppermute | solution.py:523
  18.1 52.1 %collective-permute-start.7 = (f32[128,1024]{1,0:T(8,128)}, f32[128,1024]{1,0:T(8,128)}, u32[]{:S(2)}, u32[]{:S(2)}) collective-permute-start(f32[128,1024]{1,0:T(8,128)} %get-tuple-element.23.refs_2_.refs_0_), channel_id=1, source_target_pairs={{0,1},{1,2},{2,3},{3,0},{4,5},{5,6},{6,7},{7,4},{8,9},{9,10},{10,1... | collective-permute-start | bytes 1572872 | tf_op jit(solution)/shard_map/ppermute | solution.py:509
  31.7 33.7 %collective-permute-start.9 = (f32[128,1024]{1,0:T(8,128)}, f32[128,1024]{1,0:T(8,128)}, u32[]{:S(2)}, u32[]{:S(2)}) collective-permute-start(f32[128,1024]{1,0:T(8,128)} %get-tuple-element.24.refs_3_.refs_0_), channel_id=1, source_target_pairs={{0,1},{1,2},{2,3},{3,0},{4,5},{5,6},{6,7},{7,4},{8,9},{9,10},{10,1... | collective-permute-start | bytes 1572872 | tf_op jit(solution)/shard_map/ppermute | solution.py:509
  42.8 33.8 %collective-permute-start.5 = (f32[128,1024]{1,0:T(8,128)}, f32[128,1024]{1,0:T(8,128)}, u32[]{:S(2)}, u32[]{:S(2)}) collective-permute-start(f32[128,1024]{1,0:T(8,128)} %collective-permute-done.1.refs_1_), channel_id=1, source_target_pairs={{0,1},{1,2},{2,3},{3,0},{4,5},{5,6},{6,7},{7,4},{8,9},{9,10},{10,1... | collective-permute-start | bytes 1572872 | tf_op jit(solution)/shard_map/ppermute | solution.py:509
  51.3 47.7 %collective-permute-start.12 = (f32[2,256,512]{2,1,0:T(8,128)S(1)}, f32[2,256,512]{2,1,0:T(8,128)}, u32[]{:S(2)}, u32[]{:S(2)}) collective-permute-start(f32[2,256,512]{2,1,0:T(8,128)S(1)} %shard_map.132.refs_4_.refs_2_), channel_id=1, source_target_pairs={{0,4},{4,0},{8,12},{12,8},{1,5},{5,1},{9,13},{13,9},{2,6},{6,2},{1... | collective-permute-start | bytes 3145736 | tf_op jit(solution)/shard_map/ppermute | solution.py:528
  65.4 22.4 %collective-permute-start.10 = (f32[128,1024]{1,0:T(8,128)}, f32[128,1024]{1,0:T(8,128)S(1)}, u32[]{:S(2)}, u32[]{:S(2)}) collective-permute-start(f32[128,1024]{1,0:T(8,128)} %collective-permute-done.9.refs_5_.refs_1_), channel_id=1, source_target_pairs={{0,1},{1,2},{2,3},{3,0},{4,5},{5,6},{6,7},{7,4},{8,9},{9,10},{10,1... | collective-permute-start | bytes 1572872 | tf_op jit(solution)/shard_map/ppermute | solution.py:509
  70.2 40.1 %collective-permute-start.3 = (f32[512,512]{1,0:T(8,128)}, f32[512,512]{1,0:T(8,128)}, u32[]{:S(2)}, u32[]{:S(2)}) collective-permute-start(f32[512,512]{1,0:T(8,128)} %get-tuple-element.25), channel_id=1, source_target_pairs={{0,4},{4,0},{8,12},{12,8},{1,5},{5,1},{9,13},{13,9},{2,6},{6,2},{1... | collective-permute-start | bytes 3145736 | tf_op jit(solution)/shard_map/ppermute | solution.py:531
  70.2 40.1 %collective-permute-start.4 = (f32[512,512]{1,0:T(8,128)}, f32[512,512]{1,0:T(8,128)}, u32[]{:S(2)}, u32[]{:S(2)}) collective-permute-start(f32[512,512]{1,0:T(8,128)} %get-tuple-element.26.refs_6_), channel_id=1, source_target_pairs={{0,8},{8,0},{4,12},{12,4},{1,9},{9,1},{5,13},{13,5},{2,10},{10,2},... | collective-permute-start | bytes 3145736 | tf_op jit(solution)/shard_map/ppermute | solution.py:530
  76.6 22.5 %collective-permute-start.6 = (f32[128,1024]{1,0:T(8,128)S(1)}, f32[128,1024]{1,0:T(8,128)}, u32[]{:S(2)}, u32[]{:S(2)}) collective-permute-start(f32[128,1024]{1,0:T(8,128)S(1)} %copy-done.40), channel_id=1, source_target_pairs={{0,1},{1,2},{2,3},{3,0},{4,5},{5,6},{6,7},{7,4},{8,9},{9,10},{10,1... | collective-permute-start | bytes 1572872 | tf_op jit(solution)/shard_map/ppermute | solution.py:509
  88.5 21.8 %collective-permute-start.8 = (f32[128,1024]{1,0:T(8,128)}, f32[128,1024]{1,0:T(8,128)}, u32[]{:S(2)}, u32[]{:S(2)}) collective-permute-start(f32[128,1024]{1,0:T(8,128)} %collective-permute-done.7.refs_4_.refs_1_), channel_id=1, source_target_pairs={{0,1},{1,2},{2,3},{3,0},{4,5},{5,6},{6,7},{7,4},{8,9},{9,10},{10,1... | collective-permute-start | bytes 1572872 | tf_op jit(solution)/shard_map/ppermute | solution.py:509
  99.1 22.5 %collective-permute-start.14 = (f32[128,1024]{1,0:T(8,128)}, f32[128,1024]{1,0:T(8,128)}, u32[]{:S(2)}, u32[]{:S(2)}) collective-permute-start(f32[128,1024]{1,0:T(8,128)} %collective-permute-done.5.refs_1_.refs_2_), channel_id=1, source_target_pairs={{0,1},{1,2},{2,3},{3,0},{4,5},{5,6},{6,7},{7,4},{8,9},{9,10},{10,1... | collective-permute-start | bytes 1572872 | tf_op jit(solution)/shard_map/ppermute | solution.py:509
  99.1 33.7 %collective-permute-start.15 = (f32[128,1024]{1,0:T(8,128)}, f32[128,1024]{1,0:T(8,128)}, u32[]{:S(2)}, u32[]{:S(2)}) collective-permute-start(f32[128,1024]{1,0:T(8,128)} %collective-permute-done.6.refs_2_), channel_id=1, source_target_pairs={{0,1},{1,2},{2,3},{3,0},{4,5},{5,6},{6,7},{7,4},{8,9},{9,10},{10,1... | collective-permute-start | bytes 1572872 | tf_op jit(solution)/shard_map/ppermute | solution.py:509
  126.5 17.4 %collective-permute-start.16 = (f32[128,1024]{1,0:T(8,128)}, f32[128,1024]{1,0:T(8,128)S(1)}, u32[]{:S(2)}, u32[]{:S(2)}) collective-permute-start(f32[128,1024]{1,0:T(8,128)} %collective-permute-done.8.refs_3_.refs_2_), channel_id=1, source_target_pairs={{0,1},{1,2},{2,3},{3,0},{4,5},{5,6},{6,7},{7,4},{8,9},{9,10},{10,1... | collective-permute-start | bytes 1572872 | tf_op jit(solution)/shard_map/ppermute | solution.py:509
  126.5 24.1 %collective-permute-start.18 = (f32[128,1024]{1,0:T(8,128)S(1)}, f32[128,1024]{1,0:T(8,128)S(1)}, u32[]{:S(2)}, u32[]{:S(2)}) collective-permute-start(f32[128,1024]{1,0:T(8,128)S(1)} %get-tuple-element.28.refs_6_.refs_0_), channel_id=1, source_target_pairs={{0,4},{4,0},{8,12},{12,8},{1,5},{5,1},{9,13},{13,9},{2,6},{6,2},{1... | collective-permute-start | bytes 1572872 | tf_op jit(solution)/shard_map/ppermute | solution.py:505
  138.4 18.8 %collective-permute-start.17 = (f32[128,1024]{1,0:T(8,128)S(1)}, f32[128,1024]{1,0:T(8,128)S(1)}, u32[]{:S(2)}, u32[]{:S(2)}) collective-permute-start(f32[128,1024]{1,0:T(8,128)S(1)} %copy-done.43), channel_id=1, source_target_pairs={{0,1},{1,2},{2,3},{3,0},{4,5},{5,6},{6,7},{7,4},{8,9},{9,10},{10,1... | collective-permute-start | bytes 1572872 | tf_op jit(solution)/shard_map/ppermute | solution.py:509
  150.6 25.7 %collective-permute-start.29 = (f32[256,1024]{1,0:T(8,128)S(1)}, f32[256,1024]{1,0:T(8,128)}, u32[]{:S(2)}, u32[]{:S(2)}) collective-permute-start(f32[256,1024]{1,0:T(8,128)S(1)} %shard_map.138.refs_6_.refs_0_), channel_id=1, source_target_pairs={{0,1},{1,2},{2,3},{3,0},{4,5},{5,6},{6,7},{7,4},{8,9},{9,10},{10,1... | collective-permute-start | bytes 3145736 | tf_op jit(solution)/shard_map/ppermute | solution.py:509
  182.8 27.7 %collective-permute-start.33 = (f32[256,1024]{1,0:T(8,128)}, f32[256,1024]{1,0:T(8,128)}, u32[]{:S(2)}, u32[]{:S(2)}) collective-permute-start(f32[256,1024]{1,0:T(8,128)} %collective-permute-done.29.refs_6_.refs_1_), channel_id=1, source_target_pairs={{0,1},{1,2},{2,3},{3,0},{4,5},{5,6},{6,7},{7,4},{8,9},{9,10},{10,1... | collective-permute-start | bytes 3145736 | tf_op jit(solution)/shard_map/ppermute | solution.py:509
  197.1 18.9 %collective-permute-start.32 = (f32[512,512]{1,0:T(8,128)S(1)}, f32[512,512]{1,0:T(8,128)S(1)}, u32[]{:S(2)}, u32[]{:S(2)}) collective-permute-start(f32[512,512]{1,0:T(8,128)S(1)} %shard_map.147.refs_5_), channel_id=1, source_target_pairs={{0,4},{4,0},{8,12},{12,8},{1,5},{5,1},{9,13},{13,9},{2,6},{6,2},{1... | collective-permute-start | bytes 3145736 | tf_op jit(solution)/shard_map/ppermute | solution.py:582
  197.3 18.7 %collective-permute-start.31 = (f32[512,512]{1,0:T(8,128)}, f32[512,512]{1,0:T(8,128)S(1)}, u32[]{:S(2)}, u32[]{:S(2)}) collective-permute-start(f32[512,512]{1,0:T(8,128)} %copy-done.35), channel_id=1, source_target_pairs={{0,4},{4,0},{8,12},{12,8},{1,5},{5,1},{9,13},{13,9},{2,6},{6,2},{1... | collective-permute-start | bytes 3145736 | tf_op jit(solution)/shard_map/ppermute | solution.py:582
  197.7 24.5 %collective-permute-start.13 = (f32[512,512]{1,0:T(8,128)S(1)}, f32[512,512]{1,0:T(8,128)}, u32[]{:S(2)}, u32[]{:S(2)}) collective-permute-start(f32[512,512]{1,0:T(8,128)S(1)} %copy-done.13), channel_id=1, source_target_pairs={{0,4},{4,0},{8,12},{12,8},{1,5},{5,1},{9,13},{13,9},{2,6},{6,2},{1... | collective-permute-start | bytes 3145736 | tf_op jit(solution)/shard_map/ppermute | solution.py:539
  210.5 26.9 %collective-permute-start.34 = (f32[256,1024]{1,0:T(8,128)}, f32[256,1024]{1,0:T(8,128)}, u32[]{:S(2)}, u32[]{:S(2)}) collective-permute-start(f32[256,1024]{1,0:T(8,128)} %collective-permute-done.33.refs_5_.refs_2_), channel_id=1, source_target_pairs={{0,1},{1,2},{2,3},{3,0},{4,5},{5,6},{6,7},{7,4},{8,9},{9,10},{10,1... | collective-permute-start | bytes 3145736 | tf_op jit(solution)/shard_map/ppermute | solution.py:509
  221.7 25.1 %collective-permute-start.37 = (f32[2,256,512]{2,1,0:T(8,128)}, f32[2,256,512]{2,1,0:T(8,128)}, u32[]{:S(2)}, u32[]{:S(2)}) collective-permute-start(f32[2,256,512]{2,1,0:T(8,128)} %get-tuple-element.37), channel_id=1, source_target_pairs={{0,8},{8,0},{4,12},{12,4},{1,9},{9,1},{5,13},{13,5},{2,10},{10,2},... | collective-permute-start | bytes 3145736 | tf_op jit(solution)/shard_map/ppermute | solution.py:592
  (64 other events, 642.6 us)

commit v3 on v2

--- a/solution.py
+++ b/solution.py
@@ -97,6 +97,7 @@
 
 ACROSS = [(0, 2), (2, 0), (1, 3), (3, 1)]
 SIBLING = [(0, 1), (1, 0), (2, 3), (3, 2)]
+DIAGONAL = [(0, 3), (3, 0), (1, 2), (2, 1)]
 
 
 CHUNKS = 4
@@ -586,8 +587,10 @@
         keep = transposed(which, taken, n, block_r, chain[-1])
         kept.append(keep)
         chain.append([keep])
-    theirs, mine = halved_sums(here, kept, received, chain[-1] + square_rounds[2:])
-    square_rounds.append(turn(square_rounds[-1]))
+    (moved,) = after(chain[-1], square_rounds[-1])
+    chain.append([moved])
+    square_rounds.append(turn(moved))
+    theirs, mine = halved_sums(here, kept, received, chain[-1])
     chain.append([mine])
     sums = mine + lax.ppermute(theirs, "row", ACROSS)
     terms_one = root_terms(here, zroot, own, sibling, across_same, across_other, chain[-1])
@@ -606,12 +609,16 @@
     packed = jnp.concatenate(
         [terms_one.reshape(rows, share_one)] + [t.reshape(rows, share_two) for t in terms_two],
         axis=1,
-    ).reshape(2, 2, -1)
-    packed = lax.dynamic_index_in_dim(packed, core, 1, keepdims=False) + lax.ppermute(
-        lax.dynamic_index_in_dim(packed, 1 - core, 1, keepdims=False), "row", SIBLING
-    )
-    packed = lax.dynamic_index_in_dim(packed, chip, 0, keepdims=False) + lax.ppermute(
-        lax.dynamic_index_in_dim(packed, 1 - chip, 0, keepdims=False), "row", ACROSS
+    )
+
+    def share_of(which):
+        return lax.dynamic_index_in_dim(packed, which, 0, keepdims=False)
+
+    packed = (
+        share_of(row)
+        + lax.ppermute(share_of(row ^ 1), "row", SIBLING)
+        + lax.ppermute(share_of(row ^ 2), "row", ACROSS)
+        + lax.ppermute(share_of(row ^ 3), "row", DIAGONAL)
     )
     var_one = packed[:share_one] + jnp.sum(own_columns * own_columns, axis=0)
     squares = jnp.sum(inv_two * inv_two, axis=1)

time: 257 us -> 255 us (level)
  waiting for transfers between devices: 113 us -> 108 us
    ppermute x1, waiting for transfers between devices: 3.31 us -> 0.01 us  [line_body(): sums = mine + lax.ppermute(theirs, 'row', ACROSS)]
    pallas_call x5 -> x6, Pallas kernels: 3.55 us -> 5.84 us  [after(): pl.pallas_call(kernel, in_specs=[WHOLE] * count + [ANYWHERE] * len(deps),...]
    unnamed x101 -> x98, local copies, waits for them, and re-layouts: 21.6 us -> 19.7 us
  transfers between devices with their start and end apart: 38 -> 39, of which waited for: 17 -> 16; matrix products, arithmetic and copies ran while one was open for 4% -> 4% of each run, Pallas kernels for 32% -> 33%
where the time goes in v3:
time: 255 us; the launch traced here: 253 us
  waiting for transfers between devices  108 us (42%)
  Pallas kernels  91.3 us (36%)
  local copies, waits for them, and re-layouts  20.5 us (8%)
  starting transfers between devices  15.5 us (6%)
  other arithmetic  9.62 us (4%)
  matrix products  6.55 us (3%)
    ppermute x15, waiting for transfers between devices, turn(): return lax.ppermute(x, 'col', [(i, (i + 1) % cols) for i in range(cols)])  101 us
    pallas_call x5, Pallas kernels, with_parent(): pl.pallas_call(kernel, grid=(1,), in_specs=[SCALARS] + [ANYWHERE] * count...  24.7 us
    pallas_call x4, Pallas kernels, root_step(): pl.pallas_call(kernel, grid=(nodes * tiles,), in_specs=[SCALARS, ANYWHERE...  22.3 us
    unnamed x98, local copies, waits for them, and re-layouts  19.7 us
    pallas_call x4, Pallas kernels, transposed(): pl.pallas_call(kernel, grid=(1,), in_specs=[SCALARS] + [pl.BlockSpec((Non...  9.17 us
    pallas_call x1, Pallas kernels, root_terms(): pl.pallas_call(kernel, in_specs=[SCALARS] + [WHOLE] * (1 + count + 3) + [...  7.5 us
    pallas_call x1, Pallas kernels, level_one(): pl.pallas_call(kernel, grid=(width // tile,), in_specs=[pl.BlockSpec((roo...  6.85 us
    ppermute x15, starting transfers between devices, turn(): return lax.ppermute(x, 'col', [(i, (i + 1) % cols) for i in range(cols)])  6.63 us
  transfers between devices with their start and end apart: 39, of which 16 were waited for; matrix products, arithmetic and copies ran while one was open for 4% of the time, Pallas kernels for 33%

profile of v3, /device:TPU:0, one launch (start us, length us, event | category | flops | bytes accessed | tf_op | source)
XLA Modules:
  0.0 252.6 jit_solution(13149229541019428434)
XLA Ops:
  3.8 6.8 %shard_map.129 = (f32[128,1024]{1,0:T(8,128)S(1)}, f32[128,1024]{1,0:T(8,128)S(1)}, f32[128,1024]{1,0:T(8,128)}, f32[128,1024]{1,0:T(8,128)}) custom-call(f32[512,1024]{1,0:T(8,128)S(1)} %bitcast.59, f32[1024,1024]{1,0:T(8,128)} %bitcast.60), custom_call_target="tpu_custom_call" | custom-call | flops 1 | bytes 1 | tf_op jit(solution)/shard_map/pallas_call | solution.py:146
  19.8 5.4 %fusion.refs_4_.refs_5_ = f32[2,512,512]{2,1,0:T(8,128)} fusion(f32[2,512,512]{2,1,0:T(8,128)} %param.15, f32[2,512,512]{2,1,0:T(8,128)} %param.14, f32[2,512]{1,0:T(2,128)S(1)} %compare_convert_fusion, f32[2,512]{1,0:T(2,128)S(1)} %mul.64), kind=kOutput, calls=%fused_computation.1 | convolution fusion | flops 1611661312 | bytes 6299648 | tf_op jit(solution)/shard_map/nak,nkm->nam/dot_general | solution.py:27
  25.3 6.4 %collective-permute-done.1.refs_1_ = f32[128,1024]{1,0:T(8,128)} collective-permute-done((f32[128,1024]{1,0:T(8,128)S(1)}, f32[128,1024]{1,0:T(8,128)}, u32[]{:S(2)}, u32[]{:S(2)}) %collective-permute-start.1) | collective-permute-done | bytes 524320 | tf_op jit(solution)/shard_map/ppermute | solution.py:510
  31.7 11.1 %collective-permute-done.2.refs_2_.refs_1_ = f32[128,1024]{1,0:T(8,128)S(1)} collective-permute-done((f32[128,1024]{1,0:T(8,128)S(1)}, f32[128,1024]{1,0:T(8,128)S(1)}, u32[]{:S(2)}, u32[]{:S(2)}) %collective-permute-start.2) | collective-permute-done | bytes 524320 | tf_op jit(solution)/shard_map/ppermute | solution.py:510
  44.4 4.6 %shard_map.131.refs_3_.refs_0_ = f32[256,1024]{1,0:T(8,128)S(1)} custom-call(f32[1024,256]{1,0:T(8,128)S(1)} %get-tuple-element.41.columns_ref, f32[1024,1024]{1,0:T(8,128)} %bitcast.61, f32[2,256,512]{2,1,0:T(8,128)S(1)} %shard_map.130.refs_0_), custom_call_target="tpu_custom_call" | custom-call | flops 1 | bytes 1 | tf_op jit(solution)/shard_map/pallas_call | solution.py:193
  51.5 13.9 %collective-permute-done.9.refs_5_.refs_1_ = f32[128,1024]{1,0:T(8,128)} collective-permute-done((f32[128,1024]{1,0:T(8,128)}, f32[128,1024]{1,0:T(8,128)}, u32[]{:S(2)}, u32[]{:S(2)}) %collective-permute-start.9) | collective-permute-done | bytes 524320 | tf_op jit(solution)/shard_map/ppermute | solution.py:510
  70.6 6.0 %collective-permute-done.5.refs_1_.refs_2_ = f32[128,1024]{1,0:T(8,128)} collective-permute-done((f32[128,1024]{1,0:T(8,128)}, f32[128,1024]{1,0:T(8,128)}, u32[]{:S(2)}, u32[]{:S(2)}) %collective-permute-start.5) | collective-permute-done | bytes 524320 | tf_op jit(solution)/shard_map/ppermute | solution.py:510
  76.6 11.1 %collective-permute-done.10.refs_4_.refs_2_ = f32[128,1024]{1,0:T(8,128)S(1)} collective-permute-done((f32[128,1024]{1,0:T(8,128)}, f32[128,1024]{1,0:T(8,128)S(1)}, u32[]{:S(2)}, u32[]{:S(2)}) %collective-permute-start.10) | collective-permute-done | bytes 524320 | tf_op jit(solution)/shard_map/ppermute | solution.py:510
  88.6 10.5 %collective-permute-done.6.refs_2_ = f32[128,1024]{1,0:T(8,128)} collective-permute-done((f32[128,1024]{1,0:T(8,128)S(1)}, f32[128,1024]{1,0:T(8,128)}, u32[]{:S(2)}, u32[]{:S(2)}) %collective-permute-start.6) | collective-permute-done | bytes 524320 | tf_op jit(solution)/shard_map/ppermute | solution.py:510
  104.5 5.9 %collective-permute-done.8.refs_3_.refs_2_ = f32[128,1024]{1,0:T(8,128)} collective-permute-done((f32[128,1024]{1,0:T(8,128)}, f32[128,1024]{1,0:T(8,128)}, u32[]{:S(2)}, u32[]{:S(2)}) %collective-permute-start.8) | collective-permute-done | bytes 524320 | tf_op jit(solution)/shard_map/ppermute | solution.py:510
  111.7 9.9 %collective-permute-done.14.refs_3_ = f32[128,1024]{1,0:T(8,128)} collective-permute-done((f32[128,1024]{1,0:T(8,128)}, f32[128,1024]{1,0:T(8,128)}, u32[]{:S(2)}, u32[]{:S(2)}) %collective-permute-start.14) | collective-permute-done | bytes 524320 | tf_op jit(solution)/shard_map/ppermute | solution.py:510
  121.6 4.7 %shard_map.136 = (f32[128,1024]{1,0:T(8,128)S(1)}, f32[2,128,1024]{2,1,0:T(8,128)S(1)}) custom-call(s32[2]{0:T(128)S(1)} %and_select_fusion.choice_ref, f32[128,1024]{1,0:T(8,128)S(1)} %copy-done.21, f32[128,1024]{1,0:T(8,128)} %collective-permute-done.1.refs_1_, f32[128,1024]{1,0:T(8,128)} %collective-permute-done.5.refs_1_.refs_2_, ...), custom_call_target="tpu_custom_call" | custom-call | flops 1 | bytes 1 | tf_op jit(solution)/shard_map/pallas_call | solution.py:232
  126.6 6.2 %collective-permute-done.15.refs_3_ = f32[128,1024]{1,0:T(8,128)} collective-permute-done((f32[128,1024]{1,0:T(8,128)}, f32[128,1024]{1,0:T(8,128)}, u32[]{:S(2)}, u32[]{:S(2)}) %collective-permute-start.15) | collective-permute-done | bytes 524320 | tf_op jit(solution)/shard_map/ppermute | solution.py:510
  138.6 5.3 %collective-permute-done.16.refs_3_ = f32[128,1024]{1,0:T(8,128)S(1)} collective-permute-done((f32[128,1024]{1,0:T(8,128)}, f32[128,1024]{1,0:T(8,128)S(1)}, u32[]{:S(2)}, u32[]{:S(2)}) %collective-permute-start.16) | collective-permute-done | bytes 524320 | tf_op jit(solution)/shard_map/ppermute | solution.py:510
  143.9 5.3 %shard_map.139 = (f32[128,1024]{1,0:T(8,128)S(1)}, f32[2,128,1024]{2,1,0:T(8,128)S(1)}) custom-call(s32[2]{0:T(128)S(1)} %and_select_fusion.choice_ref, f32[128,1024]{1,0:T(8,128)} %get-tuple-element.23.refs_2_.refs_0_, f32[128,1024]{1,0:T(8,128)} %collective-permute-done.7.refs_4_.refs_1_, f32[128,1024]{1,0:T(8,128)} %collective-permute-done.8.refs_3_.refs_2_, ...), custom_call_target="tpu_custom_call" | custom-call | flops 1 | bytes 1 | tf_op jit(solution)/shard_map/pallas_call | solution.py:232
  151.2 4.6 %shard_map.140.refs_6_.refs_4_ = f32[2,512,512]{2,1,0:T(8,128)S(1)} custom-call(s32[4]{0:T(128)S(1)} %pad_add_fusion.1.order_ref, f32[512,2048]{1,0:T(8,128)} %root_ref.9, f32[128,1024]{1,0:T(8,128)S(1)} %get-tuple-element.28.refs_6_.refs_0_, f32[128,1024]{1,0:T(8,128)S(1)} %collective-permute-done.18.refs_1_, ...), custom_call_target="tpu_custom_call" | custom-call | flops 1 | bytes 1 | tf_op jit(solution)/shard_map/pallas_call | solution.py:404
  161.4 5.4 %shard_map.141 = (f32[128,1024]{1,0:T(8,128)}, f32[2,128,1024]{2,1,0:T(8,128)S(1)}) custom-call(s32[2]{0:T(128)S(1)} %and_select_fusion.choice_ref, f32[128,1024]{1,0:T(8,128)} %get-tuple-element.24.refs_3_.refs_0_, f32[128,1024]{1,0:T(8,128)} %collective-permute-done.9.refs_5_.refs_1_, f32[128,1024]{1,0:T(8,128)S(1)} %copy-done.43, ...), custom_call_target="tpu_custom_call" | custom-call | flops 1 | bytes 1 | tf_op jit(solution)/shard_map/pallas_call | solution.py:232
  167.6 5.6 %shard_map.142.refs_4_.refs_5_ = f32[2,512,512]{2,1,0:T(8,128)S(1)} custom-call(s32[4]{0:T(128)S(1)} %pad_add_fusion.1.order_ref, f32[512,2048]{1,0:T(8,128)} %root_ref.9, f32[128,1024]{1,0:T(8,128)S(1)} %get-tuple-element.30.refs_1_.refs_0_, f32[128,1024]{1,0:T(8,128)S(1)} %collective-permute-done.26.refs_1_, ...), custom_call_target="tpu_custom_call" | custom-call | flops 1 | bytes 1 | tf_op jit(solution)/shard_map/pallas_call | solution.py:404
  176.3 5.6 %shard_map.143.refs_1_.refs_4_ = f32[2,512,512]{2,1,0:T(8,128)S(1)} custom-call(s32[4]{0:T(128)S(1)} %pad_add_fusion.1.order_ref, f32[512,2048]{1,0:T(8,128)} %root_ref.9, f32[128,1024]{1,0:T(8,128)S(1)} %get-tuple-element.32.refs_4_.refs_0_.refs_2_, f32[128,1024]{1,0:T(8,128)S(1)} %collective-permute-done.23.refs_1_, ...), custom_call_target="tpu_custom_call" | custom-call | flops 1 | bytes 1 | tf_op jit(solution)/shard_map/pallas_call | solution.py:404
  185.1 6.4 %shard_map.145.refs_4_.refs_5_ = f32[2,512,512]{2,1,0:T(8,128)} custom-call(s32[4]{0:T(128)S(1)} %pad_add_fusion.1.order_ref, f32[512,2048]{1,0:T(8,128)} %root_ref.9, f32[128,1024]{1,0:T(8,128)} %get-tuple-element.34.refs_5_.refs_0_.refs_3_, f32[128,1024]{1,0:T(8,128)} %collective-permute-done.21.refs_1_, f32[128,1024]{1,0:T(8,128)} %shard_map.144.refs_2_.refs_5_, ...), custom_call_target="tpu_custom_call" | custom-call | flops 1 | bytes 1 | tf_op jit(solution)/shard_map/pallas_call | solution.py:404
  203.7 6.8 %collective-permute-done.33.refs_0_.refs_2_ = f32[256,1024]{1,0:T(8,128)} collective-permute-done((f32[256,1024]{1,0:T(8,128)}, f32[256,1024]{1,0:T(8,128)}, u32[]{:S(2)}, u32[]{:S(2)}) %collective-permute-start.33) | collective-permute-done | bytes 1048608 | tf_op jit(solution)/shard_map/ppermute | solution.py:510
  221.6 7.5 %shard_map.152.refs_5_ = f32[1,1024]{1,0:T(1,128)S(1)} custom-call(s32[2]{0:T(128)S(1)} %pad_add_fusion.place_ref.chip_ref, f32[512,2048]{1,0:T(8,128)} %root_ref.9, f32[128,1024]{1,0:T(8,128)S(1)} %copy-done.22, f32[128,1024]{1,0:T(8,128)S(1)} %copy-done.26, f32[128,1024]{1,0:T(8,128)} %get-tuple-element.23.refs_2_.refs_0_, ...), custom_call_target="tpu_custom_call" | custom-call | flops 1 | bytes 1 | tf_op jit(solution)/shard_map/pallas_call | solution.py:362
  233.6 6.1 %collective-permute-done.34.refs_3_ = f32[256,1024]{1,0:T(8,128)} collective-permute-done((f32[256,1024]{1,0:T(8,128)}, f32[256,1024]{1,0:T(8,128)}, u32[]{:S(2)}, u32[]{:S(2)}) %collective-permute-start.34) | collective-permute-done | bytes 1048608 | tf_op jit(solution)/shard_map/ppermute | solution.py:510
  239.7 4.9 %shard_map.154 = (f32[256,1024]{1,0:T(8,128)S(1)}, f32[2,256,1024]{2,1,0:T(8,128)}) custom-call(s32[2]{0:T(128)S(1)} %and_select_fusion.choice_ref, f32[256,1024]{1,0:T(8,128)S(1)} %copy-done.18, f32[256,1024]{1,0:T(8,128)} %collective-permute-done.29.refs_6_.refs_1_, f32[256,1024]{1,0:T(8,128)} %collective-permute-done.33.refs_0_.refs_2_, ...), custom_call_target="tpu_custom_call" | custom-call | flops 1 | bytes 1 | tf_op jit(solution)/shard_map/pallas_call | solution.py:232
  (205 shorter events, 85.1 us)
Async XLA Ops:
  11.9 37.1 %collective-permute-start = (f32[2,256,512]{2,1,0:T(8,128)S(1)}, f32[2,256,512]{2,1,0:T(8,128)}, u32[]{:S(2)}, u32[]{:S(2)}) collective-permute-start(f32[2,256,512]{2,1,0:T(8,128)S(1)} %shard_map.130.refs_0_), channel_id=1, source_target_pairs={{0,8},{8,0},{4,12},{12,4},{1,9},{9,1},{5,13},{13,5},{2,10},{10,2},... | collective-permute-start | bytes 3145736 | tf_op jit(solution)/shard_map/ppermute | solution.py:523
  14.9 16.8 %collective-permute-start.1 = (f32[128,1024]{1,0:T(8,128)S(1)}, f32[128,1024]{1,0:T(8,128)}, u32[]{:S(2)}, u32[]{:S(2)}) collective-permute-start(f32[128,1024]{1,0:T(8,128)S(1)} %get-tuple-element.21.refs_1_.refs_0_), channel_id=1, source_target_pairs={{0,1},{1,2},{2,3},{3,0},{4,5},{5,6},{6,7},{7,4},{8,9},{9,10},{10,1... | collective-permute-start | bytes 1572872 | tf_op jit(solution)/shard_map/ppermute | solution.py:510
  16.5 26.3 %collective-permute-start.2 = (f32[128,1024]{1,0:T(8,128)S(1)}, f32[128,1024]{1,0:T(8,128)S(1)}, u32[]{:S(2)}, u32[]{:S(2)}) collective-permute-start(f32[128,1024]{1,0:T(8,128)S(1)} %get-tuple-element.22.refs_1_.refs_0_), channel_id=1, source_target_pairs={{0,1},{1,2},{2,3},{3,0},{4,5},{5,6},{6,7},{7,4},{8,9},{9,10},{10,1... | collective-permute-start | bytes 1572872 | tf_op jit(solution)/shard_map/ppermute | solution.py:510
  18.1 52.1 %collective-permute-start.11 = (f32[2,256,512]{2,1,0:T(8,128)S(1)}, f32[2,256,512]{2,1,0:T(8,128)}, u32[]{:S(2)}, u32[]{:S(2)}) collective-permute-start(f32[2,256,512]{2,1,0:T(8,128)S(1)} %shard_map.130.refs_0_), channel_id=1, source_target_pairs={{0,4},{4,0},{8,12},{12,8},{1,5},{5,1},{9,13},{13,9},{2,6},{6,2},{1... | collective-permute-start | bytes 3145736 | tf_op jit(solution)/shard_map/ppermute | solution.py:524
  18.1 52.1 %collective-permute-start.7 = (f32[128,1024]{1,0:T(8,128)}, f32[128,1024]{1,0:T(8,128)}, u32[]{:S(2)}, u32[]{:S(2)}) collective-permute-start(f32[128,1024]{1,0:T(8,128)} %get-tuple-element.23.refs_2_.refs_0_), channel_id=1, source_target_pairs={{0,1},{1,2},{2,3},{3,0},{4,5},{5,6},{6,7},{7,4},{8,9},{9,10},{10,1... | collective-permute-start | bytes 1572872 | tf_op jit(solution)/shard_map/ppermute | solution.py:510
  31.7 33.7 %collective-permute-start.9 = (f32[128,1024]{1,0:T(8,128)}, f32[128,1024]{1,0:T(8,128)}, u32[]{:S(2)}, u32[]{:S(2)}) collective-permute-start(f32[128,1024]{1,0:T(8,128)} %get-tuple-element.24.refs_3_.refs_0_), channel_id=1, source_target_pairs={{0,1},{1,2},{2,3},{3,0},{4,5},{5,6},{6,7},{7,4},{8,9},{9,10},{10,1... | collective-permute-start | bytes 1572872 | tf_op jit(solution)/shard_map/ppermute | solution.py:510
  42.8 33.8 %collective-permute-start.5 = (f32[128,1024]{1,0:T(8,128)}, f32[128,1024]{1,0:T(8,128)}, u32[]{:S(2)}, u32[]{:S(2)}) collective-permute-start(f32[128,1024]{1,0:T(8,128)} %collective-permute-done.1.refs_1_), channel_id=1, source_target_pairs={{0,1},{1,2},{2,3},{3,0},{4,5},{5,6},{6,7},{7,4},{8,9},{9,10},{10,1... | collective-permute-start | bytes 1572872 | tf_op jit(solution)/shard_map/ppermute | solution.py:510
  51.4 47.7 %collective-permute-start.12 = (f32[2,256,512]{2,1,0:T(8,128)S(1)}, f32[2,256,512]{2,1,0:T(8,128)}, u32[]{:S(2)}, u32[]{:S(2)}) collective-permute-start(f32[2,256,512]{2,1,0:T(8,128)S(1)} %shard_map.132.refs_4_.refs_2_), channel_id=1, source_target_pairs={{0,4},{4,0},{8,12},{12,8},{1,5},{5,1},{9,13},{13,9},{2,6},{6,2},{1... | collective-permute-start | bytes 3145736 | tf_op jit(solution)/shard_map/ppermute | solution.py:529
  65.4 22.4 %collective-permute-start.10 = (f32[128,1024]{1,0:T(8,128)}, f32[128,1024]{1,0:T(8,128)S(1)}, u32[]{:S(2)}, u32[]{:S(2)}) collective-permute-start(f32[128,1024]{1,0:T(8,128)} %collective-permute-done.9.refs_5_.refs_1_), channel_id=1, source_target_pairs={{0,1},{1,2},{2,3},{3,0},{4,5},{5,6},{6,7},{7,4},{8,9},{9,10},{10,1... | collective-permute-start | bytes 1572872 | tf_op jit(solution)/shard_map/ppermute | solution.py:510
  70.2 40.1 %collective-permute-start.3 = (f32[512,512]{1,0:T(8,128)}, f32[512,512]{1,0:T(8,128)}, u32[]{:S(2)}, u32[]{:S(2)}) collective-permute-start(f32[512,512]{1,0:T(8,128)} %get-tuple-element.25), channel_id=1, source_target_pairs={{0,4},{4,0},{8,12},{12,8},{1,5},{5,1},{9,13},{13,9},{2,6},{6,2},{1... | collective-permute-start | bytes 3145736 | tf_op jit(solution)/shard_map/ppermute | solution.py:532
  70.2 40.1 %collective-permute-start.4 = (f32[512,512]{1,0:T(8,128)}, f32[512,512]{1,0:T(8,128)}, u32[]{:S(2)}, u32[]{:S(2)}) collective-permute-start(f32[512,512]{1,0:T(8,128)} %get-tuple-element.26.refs_6_), channel_id=1, source_target_pairs={{0,8},{8,0},{4,12},{12,4},{1,9},{9,1},{5,13},{13,5},{2,10},{10,2},... | collective-permute-start | bytes 3145736 | tf_op jit(solution)/shard_map/ppermute | solution.py:531
  76.6 22.5 %collective-permute-start.6 = (f32[128,1024]{1,0:T(8,128)S(1)}, f32[128,1024]{1,0:T(8,128)}, u32[]{:S(2)}, u32[]{:S(2)}) collective-permute-start(f32[128,1024]{1,0:T(8,128)S(1)} %copy-done.40), channel_id=1, source_target_pairs={{0,1},{1,2},{2,3},{3,0},{4,5},{5,6},{6,7},{7,4},{8,9},{9,10},{10,1... | collective-permute-start | bytes 1572872 | tf_op jit(solution)/shard_map/ppermute | solution.py:510
  88.5 21.8 %collective-permute-start.8 = (f32[128,1024]{1,0:T(8,128)}, f32[128,1024]{1,0:T(8,128)}, u32[]{:S(2)}, u32[]{:S(2)}) collective-permute-start(f32[128,1024]{1,0:T(8,128)} %collective-permute-done.7.refs_4_.refs_1_), channel_id=1, source_target_pairs={{0,1},{1,2},{2,3},{3,0},{4,5},{5,6},{6,7},{7,4},{8,9},{9,10},{10,1... | collective-permute-start | bytes 1572872 | tf_op jit(solution)/shard_map/ppermute | solution.py:510
  99.1 22.5 %collective-permute-start.14 = (f32[128,1024]{1,0:T(8,128)}, f32[128,1024]{1,0:T(8,128)}, u32[]{:S(2)}, u32[]{:S(2)}) collective-permute-start(f32[128,1024]{1,0:T(8,128)} %collective-permute-done.5.refs_1_.refs_2_), channel_id=1, source_target_pairs={{0,1},{1,2},{2,3},{3,0},{4,5},{5,6},{6,7},{7,4},{8,9},{9,10},{10,1... | collective-permute-start | bytes 1572872 | tf_op jit(solution)/shard_map/ppermute | solution.py:510
  99.1 33.7 %collective-permute-start.15 = (f32[128,1024]{1,0:T(8,128)}, f32[128,1024]{1,0:T(8,128)}, u32[]{:S(2)}, u32[]{:S(2)}) collective-permute-start(f32[128,1024]{1,0:T(8,128)} %collective-permute-done.6.refs_2_), channel_id=1, source_target_pairs={{0,1},{1,2},{2,3},{3,0},{4,5},{5,6},{6,7},{7,4},{8,9},{9,10},{10,1... | collective-permute-start | bytes 1572872 | tf_op jit(solution)/shard_map/ppermute | solution.py:510
  126.6 17.4 %collective-permute-start.16 = (f32[128,1024]{1,0:T(8,128)}, f32[128,1024]{1,0:T(8,128)S(1)}, u32[]{:S(2)}, u32[]{:S(2)}) collective-permute-start(f32[128,1024]{1,0:T(8,128)} %collective-permute-done.8.refs_3_.refs_2_), channel_id=1, source_target_pairs={{0,1},{1,2},{2,3},{3,0},{4,5},{5,6},{6,7},{7,4},{8,9},{9,10},{10,1... | collective-permute-start | bytes 1572872 | tf_op jit(solution)/shard_map/ppermute | solution.py:510
  126.6 24.0 %collective-permute-start.18 = (f32[128,1024]{1,0:T(8,128)S(1)}, f32[128,1024]{1,0:T(8,128)S(1)}, u32[]{:S(2)}, u32[]{:S(2)}) collective-permute-start(f32[128,1024]{1,0:T(8,128)S(1)} %get-tuple-element.28.refs_6_.refs_0_), channel_id=1, source_target_pairs={{0,4},{4,0},{8,12},{12,8},{1,5},{5,1},{9,13},{13,9},{2,6},{6,2},{1... | collective-permute-start | bytes 1572872 | tf_op jit(solution)/shard_map/ppermute | solution.py:506
  138.5 18.8 %collective-permute-start.17 = (f32[128,1024]{1,0:T(8,128)S(1)}, f32[128,1024]{1,0:T(8,128)S(1)}, u32[]{:S(2)}, u32[]{:S(2)}) collective-permute-start(f32[128,1024]{1,0:T(8,128)S(1)} %copy-done.43), channel_id=1, source_target_pairs={{0,1},{1,2},{2,3},{3,0},{4,5},{5,6},{6,7},{7,4},{8,9},{9,10},{10,1... | collective-permute-start | bytes 1572872 | tf_op jit(solution)/shard_map/ppermute | solution.py:510
  150.6 25.7 %collective-permute-start.29 = (f32[256,1024]{1,0:T(8,128)S(1)}, f32[256,1024]{1,0:T(8,128)}, u32[]{:S(2)}, u32[]{:S(2)}) collective-permute-start(f32[256,1024]{1,0:T(8,128)S(1)} %shard_map.138.refs_6_.refs_0_), channel_id=1, source_target_pairs={{0,1},{1,2},{2,3},{3,0},{4,5},{5,6},{6,7},{7,4},{8,9},{9,10},{10,1... | collective-permute-start | bytes 3145736 | tf_op jit(solution)/shard_map/ppermute | solution.py:510
  157.3 17.3 %collective-permute-start.23 = (f32[128,1024]{1,0:T(8,128)S(1)}, f32[128,1024]{1,0:T(8,128)S(1)}, u32[]{:S(2)}, u32[]{:S(2)}) collective-permute-start(f32[128,1024]{1,0:T(8,128)S(1)} %get-tuple-element.32.refs_4_.refs_0_.refs_2_), channel_id=1, source_target_pairs={{0,4},{4,0},{8,12},{12,8},{1,5},{5,1},{9,13},{13,9},{2,6},{6,2},{1... | collective-permute-start | bytes 1572872 | tf_op jit(solution)/shard_map/ppermute | solution.py:506
  182.8 27.7 %collective-permute-start.33 = (f32[256,1024]{1,0:T(8,128)}, f32[256,1024]{1,0:T(8,128)}, u32[]{:S(2)}, u32[]{:S(2)}) collective-permute-start(f32[256,1024]{1,0:T(8,128)} %collective-permute-done.29.refs_6_.refs_1_), channel_id=1, source_target_pairs={{0,1},{1,2},{2,3},{3,0},{4,5},{5,6},{6,7},{7,4},{8,9},{9,10},{10,1... | collective-permute-start | bytes 3145736 | tf_op jit(solution)/shard_map/ppermute | solution.py:510
  197.7 21.8 %collective-permute-start.13 = (f32[512,512]{1,0:T(8,128)S(1)}, f32[512,512]{1,0:T(8,128)}, u32[]{:S(2)}, u32[]{:S(2)}) collective-permute-start(f32[512,512]{1,0:T(8,128)S(1)} %copy-done.13), channel_id=1, source_target_pairs={{0,4},{4,0},{8,12},{12,8},{1,5},{5,1},{9,13},{13,9},{2,6},{6,2},{1... | collective-permute-start | bytes 3145736 | tf_op jit(solution)/shard_map/ppermute | solution.py:540
  212.8 26.9 %collective-permute-start.34 = (f32[256,1024]{1,0:T(8,128)}, f32[256,1024]{1,0:T(8,128)}, u32[]{:S(2)}, u32[]{:S(2)}) collective-permute-start(f32[256,1024]{1,0:T(8,128)} %shard_map.150.refs_4_), channel_id=1, source_target_pairs={{0,1},{1,2},{2,3},{3,0},{4,5},{5,6},{6,7},{7,4},{8,9},{9,10},{10,1... | collective-permute-start | bytes 3145736 | tf_op jit(solution)/shard_map/ppermute | solution.py:510
  217.2 28.6 %collective-permute-start.38 = (f32[2,256,512]{2,1,0:T(8,128)}, f32[2,256,512]{2,1,0:T(8,128)}, u32[]{:S(2)}, u32[]{:S(2)}) collective-permute-start(f32[2,256,512]{2,1,0:T(8,128)} %get-tuple-element.37), channel_id=1, source_target_pairs={{0,8},{8,0},{4,12},{12,4},{1,9},{9,1},{5,13},{13,5},{2,10},{10,2},... | collective-permute-start | bytes 3145736 | tf_op jit(solution)/shard_map/ppermute | solution.py:595
  (64 other events, 638.7 us)

commit v4 on v3

--- a/solution.py
+++ b/solution.py
@@ -174,6 +174,21 @@
         compiler_params=params(),
         cost_estimate=cost(),
     )(*arrays, *deps)
+
+
+def in_place_after(deps, x):
+    def kernel(*refs):
+        del refs
+
+    return pl.pallas_call(
+        kernel,
+        in_specs=[ANYWHERE] * (1 + len(deps)),
+        out_specs=ANYWHERE,
+        out_shape=jax.ShapeDtypeStruct(x.shape, x.dtype),
+        input_output_aliases={0: 0},
+        compiler_params=params(),
+        cost_estimate=cost(),
+    )(x, *deps)
 
 
 def square_rows(columns, inverse, deps):
@@ -587,8 +602,9 @@
         keep = transposed(which, taken, n, block_r, chain[-1])
         kept.append(keep)
         chain.append([keep])
-    (moved,) = after(chain[-1], square_rounds[-1])
+    moved = in_place_after(chain[-1], square_rounds[-1])
     chain.append([moved])
+    square_rounds[-1] = moved
     square_rounds.append(turn(moved))
     theirs, mine = halved_sums(here, kept, received, chain[-1])
     chain.append([mine])

time: 255 us -> 252 us (0.988)
    pallas_call x6 -> x5, Pallas kernels: 5.84 us -> 3.55 us  [after(): pl.pallas_call(kernel, in_specs=[WHOLE] * count + [ANYWHERE] * len(deps),...]
  transfers between devices with their start and end apart: 39 -> 39, of which waited for: 16 -> 16; matrix products, arithmetic and copies ran while one was open for 4% -> 5% of each run, Pallas kernels for 33% -> 33%
where the time goes in v4:
time: 252 us; the launch traced here: 250 us
  waiting for transfers between devices  106 us (42%)
  Pallas kernels  88.9 us (35%)
  local copies, waits for them, and re-layouts  20.4 us (8%)
  starting transfers between devices  17 us (7%)
  other arithmetic  9.62 us (4%)
  matrix products  6.56 us (3%)
    ppermute x15, waiting for transfers between devices, turn(): return lax.ppermute(x, 'col', [(i, (i + 1) % cols) for i in range(cols)])  99.3 us
    pallas_call x5, Pallas kernels, with_parent(): pl.pallas_call(kernel, grid=(1,), in_specs=[SCALARS] + [ANYWHERE] * count...  24.7 us
    pallas_call x4, Pallas kernels, root_step(): pl.pallas_call(kernel, grid=(nodes * tiles,), in_specs=[SCALARS, ANYWHERE...  22.3 us
    unnamed x98, local copies, waits for them, and re-layouts  19.6 us
    pallas_call x4, Pallas kernels, transposed(): pl.pallas_call(kernel, grid=(1,), in_specs=[SCALARS] + [pl.BlockSpec((Non...  9.16 us
    ppermute x15, starting transfers between devices, turn(): return lax.ppermute(x, 'col', [(i, (i + 1) % cols) for i in range(cols)])  7.78 us
    pallas_call x1, Pallas kernels, root_terms(): pl.pallas_call(kernel, in_specs=[SCALARS] + [WHOLE] * (1 + count + 3) + [...  7.5 us
    pallas_call x1, Pallas kernels, level_one(): pl.pallas_call(kernel, grid=(width // tile,), in_specs=[pl.BlockSpec((roo...  6.83 us
  transfers between devices with their start and end apart: 39, of which 16 were waited for; matrix products, arithmetic and copies ran while one was open for 5% of the time, Pallas kernels for 33%

profile of v4, /device:TPU:0, one launch (start us, length us, event | category | flops | bytes accessed | tf_op | source)
XLA Modules:
  0.0 250.2 jit_solution(954604756662916124)
XLA Ops:
  3.8 6.8 %shard_map.129 = (f32[128,1024]{1,0:T(8,128)S(1)}, f32[128,1024]{1,0:T(8,128)S(1)}, f32[128,1024]{1,0:T(8,128)}, f32[128,1024]{1,0:T(8,128)}) custom-call(f32[512,1024]{1,0:T(8,128)S(1)} %bitcast.59, f32[1024,1024]{1,0:T(8,128)} %bitcast.60), custom_call_target="tpu_custom_call" | custom-call | flops 1 | bytes 1 | tf_op jit(solution)/shard_map/pallas_call | solution.py:146
  19.8 5.4 %fusion.refs_4_.refs_5_ = f32[2,512,512]{2,1,0:T(8,128)} fusion(f32[2,512,512]{2,1,0:T(8,128)} %param.15, f32[2,512,512]{2,1,0:T(8,128)} %param.14, f32[2,512]{1,0:T(2,128)S(1)} %compare_convert_fusion, f32[2,512]{1,0:T(2,128)S(1)} %mul.64), kind=kOutput, calls=%fused_computation.1 | convolution fusion | flops 1611661312 | bytes 6299648 | tf_op jit(solution)/shard_map/nak,nkm->nam/dot_general | solution.py:27
  25.3 6.4 %collective-permute-done.1.refs_1_ = f32[128,1024]{1,0:T(8,128)} collective-permute-done((f32[128,1024]{1,0:T(8,128)S(1)}, f32[128,1024]{1,0:T(8,128)}, u32[]{:S(2)}, u32[]{:S(2)}) %collective-permute-start.1) | collective-permute-done | bytes 524320 | tf_op jit(solution)/shard_map/ppermute | solution.py:525
  31.7 11.1 %collective-permute-done.2.refs_2_.refs_1_ = f32[128,1024]{1,0:T(8,128)S(1)} collective-permute-done((f32[128,1024]{1,0:T(8,128)S(1)}, f32[128,1024]{1,0:T(8,128)S(1)}, u32[]{:S(2)}, u32[]{:S(2)}) %collective-permute-start.2) | collective-permute-done | bytes 524320 | tf_op jit(solution)/shard_map/ppermute | solution.py:525
  44.4 4.6 %shard_map.131.refs_3_.refs_0_ = f32[256,1024]{1,0:T(8,128)S(1)} custom-call(f32[1024,256]{1,0:T(8,128)S(1)} %get-tuple-element.41.columns_ref, f32[1024,1024]{1,0:T(8,128)} %bitcast.61, f32[2,256,512]{2,1,0:T(8,128)S(1)} %shard_map.130.refs_0_), custom_call_target="tpu_custom_call" | custom-call | flops 1 | bytes 1 | tf_op jit(solution)/shard_map/pallas_call | solution.py:208
  51.5 13.8 %collective-permute-done.9.refs_5_.refs_1_ = f32[128,1024]{1,0:T(8,128)} collective-permute-done((f32[128,1024]{1,0:T(8,128)}, f32[128,1024]{1,0:T(8,128)}, u32[]{:S(2)}, u32[]{:S(2)}) %collective-permute-start.9) | collective-permute-done | bytes 524320 | tf_op jit(solution)/shard_map/ppermute | solution.py:525
  70.6 6.1 %collective-permute-done.5.refs_1_.refs_2_ = f32[128,1024]{1,0:T(8,128)} collective-permute-done((f32[128,1024]{1,0:T(8,128)}, f32[128,1024]{1,0:T(8,128)}, u32[]{:S(2)}, u32[]{:S(2)}) %collective-permute-start.5) | collective-permute-done | bytes 524320 | tf_op jit(solution)/shard_map/ppermute | solution.py:525
  76.6 11.1 %collective-permute-done.10.refs_4_.refs_2_ = f32[128,1024]{1,0:T(8,128)S(1)} collective-permute-done((f32[128,1024]{1,0:T(8,128)}, f32[128,1024]{1,0:T(8,128)S(1)}, u32[]{:S(2)}, u32[]{:S(2)}) %collective-permute-start.10) | collective-permute-done | bytes 524320 | tf_op jit(solution)/shard_map/ppermute | solution.py:525
  88.5 10.6 %collective-permute-done.6.refs_2_ = f32[128,1024]{1,0:T(8,128)} collective-permute-done((f32[128,1024]{1,0:T(8,128)S(1)}, f32[128,1024]{1,0:T(8,128)}, u32[]{:S(2)}, u32[]{:S(2)}) %collective-permute-start.6) | collective-permute-done | bytes 524320 | tf_op jit(solution)/shard_map/ppermute | solution.py:525
  104.5 5.8 %collective-permute-done.8.refs_3_.refs_2_ = f32[128,1024]{1,0:T(8,128)} collective-permute-done((f32[128,1024]{1,0:T(8,128)}, f32[128,1024]{1,0:T(8,128)}, u32[]{:S(2)}, u32[]{:S(2)}) %collective-permute-start.8) | collective-permute-done | bytes 524320 | tf_op jit(solution)/shard_map/ppermute | solution.py:525
  111.7 9.9 %collective-permute-done.14.refs_3_ = f32[128,1024]{1,0:T(8,128)} collective-permute-done((f32[128,1024]{1,0:T(8,128)}, f32[128,1024]{1,0:T(8,128)}, u32[]{:S(2)}, u32[]{:S(2)}) %collective-permute-start.14) | collective-permute-done | bytes 524320 | tf_op jit(solution)/shard_map/ppermute | solution.py:525
  121.6 4.7 %shard_map.136 = (f32[128,1024]{1,0:T(8,128)S(1)}, f32[2,128,1024]{2,1,0:T(8,128)S(1)}) custom-call(s32[2]{0:T(128)S(1)} %and_select_fusion.choice_ref, f32[128,1024]{1,0:T(8,128)S(1)} %copy-done.21, f32[128,1024]{1,0:T(8,128)} %collective-permute-done.1.refs_1_, f32[128,1024]{1,0:T(8,128)} %collective-permute-done.5.refs_1_.refs_2_, ...), custom_call_target="tpu_custom_call" | custom-call | flops 1 | bytes 1 | tf_op jit(solution)/shard_map/pallas_call | solution.py:247
  127.2 5.6 %collective-permute-done.15.refs_3_ = f32[128,1024]{1,0:T(8,128)} collective-permute-done((f32[128,1024]{1,0:T(8,128)}, f32[128,1024]{1,0:T(8,128)}, u32[]{:S(2)}, u32[]{:S(2)}) %collective-permute-start.15) | collective-permute-done | bytes 524320 | tf_op jit(solution)/shard_map/ppermute | solution.py:525
  132.8 4.4 %shard_map.137 = (f32[128,1024]{1,0:T(8,128)S(1)}, f32[2,128,1024]{2,1,0:T(8,128)S(1)}) custom-call(s32[2]{0:T(128)S(1)} %and_select_fusion.choice_ref, f32[128,1024]{1,0:T(8,128)S(1)} %copy-done.25, f32[128,1024]{1,0:T(8,128)S(1)} %copy-done.41, f32[128,1024]{1,0:T(8,128)} %collective-permute-done.6.refs_2_, f32[128,1024]{1,0:T(8,128)} %collective-permute-done.15.refs_3_, ...), custom_call_target="tpu_custom_call" | custom-call | flops 1 | bytes 1 | tf_op jit(solution)/shard_map/pallas_call | solution.py:247
  143.9 5.3 %shard_map.139 = (f32[128,1024]{1,0:T(8,128)S(1)}, f32[2,128,1024]{2,1,0:T(8,128)S(1)}) custom-call(s32[2]{0:T(128)S(1)} %and_select_fusion.choice_ref, f32[128,1024]{1,0:T(8,128)} %get-tuple-element.23.refs_2_.refs_0_, f32[128,1024]{1,0:T(8,128)} %collective-permute-done.7.refs_4_.refs_1_, f32[128,1024]{1,0:T(8,128)} %collective-permute-done.8.refs_3_.refs_2_, ...), custom_call_target="tpu_custom_call" | custom-call | flops 1 | bytes 1 | tf_op jit(solution)/shard_map/pallas_call | solution.py:247
  151.3 4.6 %shard_map.140.refs_6_.refs_4_ = f32[2,512,512]{2,1,0:T(8,128)S(1)} custom-call(s32[4]{0:T(128)S(1)} %pad_add_fusion.1.order_ref, f32[512,2048]{1,0:T(8,128)} %root_ref.9, f32[128,1024]{1,0:T(8,128)S(1)} %get-tuple-element.28.refs_6_.refs_0_, f32[128,1024]{1,0:T(8,128)S(1)} %collective-permute-done.18.refs_1_, ...), custom_call_target="tpu_custom_call" | custom-call | flops 1 | bytes 1 | tf_op jit(solution)/shard_map/pallas_call | solution.py:419
  161.4 5.4 %shard_map.141 = (f32[128,1024]{1,0:T(8,128)}, f32[2,128,1024]{2,1,0:T(8,128)S(1)}) custom-call(s32[2]{0:T(128)S(1)} %and_select_fusion.choice_ref, f32[128,1024]{1,0:T(8,128)} %get-tuple-element.24.refs_3_.refs_0_, f32[128,1024]{1,0:T(8,128)} %collective-permute-done.9.refs_5_.refs_1_, f32[128,1024]{1,0:T(8,128)S(1)} %copy-done.43, ...), custom_call_target="tpu_custom_call" | custom-call | flops 1 | bytes 1 | tf_op jit(solution)/shard_map/pallas_call | solution.py:247
  167.8 5.6 %shard_map.142.refs_4_.refs_5_ = f32[2,512,512]{2,1,0:T(8,128)S(1)} custom-call(s32[4]{0:T(128)S(1)} %pad_add_fusion.1.order_ref, f32[512,2048]{1,0:T(8,128)} %root_ref.9, f32[128,1024]{1,0:T(8,128)S(1)} %get-tuple-element.30.refs_1_.refs_0_, f32[128,1024]{1,0:T(8,128)S(1)} %collective-permute-done.26.refs_1_, ...), custom_call_target="tpu_custom_call" | custom-call | flops 1 | bytes 1 | tf_op jit(solution)/shard_map/pallas_call | solution.py:419
  176.3 5.6 %shard_map.143.refs_1_.refs_4_ = f32[2,512,512]{2,1,0:T(8,128)S(1)} custom-call(s32[4]{0:T(128)S(1)} %pad_add_fusion.1.order_ref, f32[512,2048]{1,0:T(8,128)} %root_ref.9, f32[128,1024]{1,0:T(8,128)S(1)} %get-tuple-element.32.refs_4_.refs_0_.refs_2_, f32[128,1024]{1,0:T(8,128)S(1)} %collective-permute-done.23.refs_1_, ...), custom_call_target="tpu_custom_call" | custom-call | flops 1 | bytes 1 | tf_op jit(solution)/shard_map/pallas_call | solution.py:419
  185.1 6.4 %shard_map.145.refs_4_.refs_5_ = f32[2,512,512]{2,1,0:T(8,128)} custom-call(s32[4]{0:T(128)S(1)} %pad_add_fusion.1.order_ref, f32[512,2048]{1,0:T(8,128)} %root_ref.9, f32[128,1024]{1,0:T(8,128)} %get-tuple-element.34.refs_5_.refs_0_.refs_3_, f32[128,1024]{1,0:T(8,128)} %collective-permute-done.21.refs_1_, f32[128,1024]{1,0:T(8,128)} %shard_map.144.refs_2_.refs_5_, ...), custom_call_target="tpu_custom_call" | custom-call | flops 1 | bytes 1 | tf_op jit(solution)/shard_map/pallas_call | solution.py:419
  203.7 6.8 %collective-permute-done.33.refs_0_ = f32[256,1024]{1,0:T(8,128)} collective-permute-done((f32[256,1024]{1,0:T(8,128)}, f32[256,1024]{1,0:T(8,128)}, u32[]{:S(2)}, u32[]{:S(2)}) %collective-permute-start.33) | collective-permute-done | bytes 1048608 | tf_op jit(solution)/shard_map/ppermute | solution.py:525
  219.3 7.5 %shard_map.152.refs_5_ = f32[1,1024]{1,0:T(1,128)S(1)} custom-call(s32[2]{0:T(128)S(1)} %pad_add_fusion.place_ref.chip_ref, f32[512,2048]{1,0:T(8,128)} %root_ref.9, f32[128,1024]{1,0:T(8,128)S(1)} %copy-done.22, f32[128,1024]{1,0:T(8,128)S(1)} %copy-done.26, f32[128,1024]{1,0:T(8,128)} %get-tuple-element.23.refs_2_.refs_0_, ...), custom_call_target="tpu_custom_call" | custom-call | flops 1 | bytes 1 | tf_op jit(solution)/shard_map/pallas_call | solution.py:377
  231.3 6.1 %collective-permute-done.34.refs_3_ = f32[256,1024]{1,0:T(8,128)} collective-permute-done((f32[256,1024]{1,0:T(8,128)}, f32[256,1024]{1,0:T(8,128)}, u32[]{:S(2)}, u32[]{:S(2)}) %collective-permute-start.34) | collective-permute-done | bytes 1048608 | tf_op jit(solution)/shard_map/ppermute | solution.py:525
  237.4 4.8 %shard_map.154 = (f32[256,1024]{1,0:T(8,128)S(1)}, f32[2,256,1024]{2,1,0:T(8,128)}) custom-call(s32[2]{0:T(128)S(1)} %and_select_fusion.choice_ref, f32[256,1024]{1,0:T(8,128)S(1)} %copy-done.18, f32[256,1024]{1,0:T(8,128)} %collective-permute-done.29.refs_6_.refs_1_, f32[256,1024]{1,0:T(8,128)} %shard_map.150.refs_4_.refs_2_, ...), custom_call_target="tpu_custom_call" | custom-call | flops 1 | bytes 1 | tf_op jit(solution)/shard_map/pallas_call | solution.py:247
  (205 shorter events, 84.3 us)
Async XLA Ops:
  11.9 37.1 %collective-permute-start = (f32[2,256,512]{2,1,0:T(8,128)S(1)}, f32[2,256,512]{2,1,0:T(8,128)}, u32[]{:S(2)}, u32[]{:S(2)}) collective-permute-start(f32[2,256,512]{2,1,0:T(8,128)S(1)} %shard_map.130.refs_0_), channel_id=1, source_target_pairs={{0,8},{8,0},{4,12},{12,4},{1,9},{9,1},{5,13},{13,5},{2,10},{10,2},... | collective-permute-start | bytes 3145736 | tf_op jit(solution)/shard_map/ppermute | solution.py:538
  16.5 26.3 %collective-permute-start.2 = (f32[128,1024]{1,0:T(8,128)S(1)}, f32[128,1024]{1,0:T(8,128)S(1)}, u32[]{:S(2)}, u32[]{:S(2)}) collective-permute-start(f32[128,1024]{1,0:T(8,128)S(1)} %get-tuple-element.22.refs_1_.refs_0_), channel_id=1, source_target_pairs={{0,1},{1,2},{2,3},{3,0},{4,5},{5,6},{6,7},{7,4},{8,9},{9,10},{10,1... | collective-permute-start | bytes 1572872 | tf_op jit(solution)/shard_map/ppermute | solution.py:525
  18.1 52.1 %collective-permute-start.11 = (f32[2,256,512]{2,1,0:T(8,128)S(1)}, f32[2,256,512]{2,1,0:T(8,128)}, u32[]{:S(2)}, u32[]{:S(2)}) collective-permute-start(f32[2,256,512]{2,1,0:T(8,128)S(1)} %shard_map.130.refs_0_), channel_id=1, source_target_pairs={{0,4},{4,0},{8,12},{12,8},{1,5},{5,1},{9,13},{13,9},{2,6},{6,2},{1... | collective-permute-start | bytes 3145736 | tf_op jit(solution)/shard_map/ppermute | solution.py:539
  18.1 52.1 %collective-permute-start.7 = (f32[128,1024]{1,0:T(8,128)}, f32[128,1024]{1,0:T(8,128)}, u32[]{:S(2)}, u32[]{:S(2)}) collective-permute-start(f32[128,1024]{1,0:T(8,128)} %get-tuple-element.23.refs_2_.refs_0_), channel_id=1, source_target_pairs={{0,1},{1,2},{2,3},{3,0},{4,5},{5,6},{6,7},{7,4},{8,9},{9,10},{10,1... | collective-permute-start | bytes 1572872 | tf_op jit(solution)/shard_map/ppermute | solution.py:525
  31.7 33.7 %collective-permute-start.9 = (f32[128,1024]{1,0:T(8,128)}, f32[128,1024]{1,0:T(8,128)}, u32[]{:S(2)}, u32[]{:S(2)}) collective-permute-start(f32[128,1024]{1,0:T(8,128)} %get-tuple-element.24.refs_3_.refs_0_), channel_id=1, source_target_pairs={{0,1},{1,2},{2,3},{3,0},{4,5},{5,6},{6,7},{7,4},{8,9},{9,10},{10,1... | collective-permute-start | bytes 1572872 | tf_op jit(solution)/shard_map/ppermute | solution.py:525
  42.8 33.8 %collective-permute-start.5 = (f32[128,1024]{1,0:T(8,128)}, f32[128,1024]{1,0:T(8,128)}, u32[]{:S(2)}, u32[]{:S(2)}) collective-permute-start(f32[128,1024]{1,0:T(8,128)} %collective-permute-done.1.refs_1_), channel_id=1, source_target_pairs={{0,1},{1,2},{2,3},{3,0},{4,5},{5,6},{6,7},{7,4},{8,9},{9,10},{10,1... | collective-permute-start | bytes 1572872 | tf_op jit(solution)/shard_map/ppermute | solution.py:525
  51.4 47.7 %collective-permute-start.12 = (f32[2,256,512]{2,1,0:T(8,128)S(1)}, f32[2,256,512]{2,1,0:T(8,128)}, u32[]{:S(2)}, u32[]{:S(2)}) collective-permute-start(f32[2,256,512]{2,1,0:T(8,128)S(1)} %shard_map.132.refs_4_.refs_2_), channel_id=1, source_target_pairs={{0,4},{4,0},{8,12},{12,8},{1,5},{5,1},{9,13},{13,9},{2,6},{6,2},{1... | collective-permute-start | bytes 3145736 | tf_op jit(solution)/shard_map/ppermute | solution.py:544
  65.4 22.4 %collective-permute-start.10 = (f32[128,1024]{1,0:T(8,128)}, f32[128,1024]{1,0:T(8,128)S(1)}, u32[]{:S(2)}, u32[]{:S(2)}) collective-permute-start(f32[128,1024]{1,0:T(8,128)} %collective-permute-done.9.refs_5_.refs_1_), channel_id=1, source_target_pairs={{0,1},{1,2},{2,3},{3,0},{4,5},{5,6},{6,7},{7,4},{8,9},{9,10},{10,1... | collective-permute-start | bytes 1572872 | tf_op jit(solution)/shard_map/ppermute | solution.py:525
  70.2 40.1 %collective-permute-start.3 = (f32[512,512]{1,0:T(8,128)}, f32[512,512]{1,0:T(8,128)}, u32[]{:S(2)}, u32[]{:S(2)}) collective-permute-start(f32[512,512]{1,0:T(8,128)} %get-tuple-element.25), channel_id=1, source_target_pairs={{0,4},{4,0},{8,12},{12,8},{1,5},{5,1},{9,13},{13,9},{2,6},{6,2},{1... | collective-permute-start | bytes 3145736 | tf_op jit(solution)/shard_map/ppermute | solution.py:547
  70.2 40.1 %collective-permute-start.4 = (f32[512,512]{1,0:T(8,128)}, f32[512,512]{1,0:T(8,128)}, u32[]{:S(2)}, u32[]{:S(2)}) collective-permute-start(f32[512,512]{1,0:T(8,128)} %get-tuple-element.26.refs_6_), channel_id=1, source_target_pairs={{0,8},{8,0},{4,12},{12,4},{1,9},{9,1},{5,13},{13,5},{2,10},{10,2},... | collective-permute-start | bytes 3145736 | tf_op jit(solution)/shard_map/ppermute | solution.py:546
  76.6 22.5 %collective-permute-start.6 = (f32[128,1024]{1,0:T(8,128)S(1)}, f32[128,1024]{1,0:T(8,128)}, u32[]{:S(2)}, u32[]{:S(2)}) collective-permute-start(f32[128,1024]{1,0:T(8,128)S(1)} %copy-done.40), channel_id=1, source_target_pairs={{0,1},{1,2},{2,3},{3,0},{4,5},{5,6},{6,7},{7,4},{8,9},{9,10},{10,1... | collective-permute-start | bytes 1572872 | tf_op jit(solution)/shard_map/ppermute | solution.py:525
  88.5 21.8 %collective-permute-start.8 = (f32[128,1024]{1,0:T(8,128)}, f32[128,1024]{1,0:T(8,128)}, u32[]{:S(2)}, u32[]{:S(2)}) collective-permute-start(f32[128,1024]{1,0:T(8,128)} %collective-permute-done.7.refs_4_.refs_1_), channel_id=1, source_target_pairs={{0,1},{1,2},{2,3},{3,0},{4,5},{5,6},{6,7},{7,4},{8,9},{9,10},{10,1... | collective-permute-start | bytes 1572872 | tf_op jit(solution)/shard_map/ppermute | solution.py:525
  99.1 22.5 %collective-permute-start.14 = (f32[128,1024]{1,0:T(8,128)}, f32[128,1024]{1,0:T(8,128)}, u32[]{:S(2)}, u32[]{:S(2)}) collective-permute-start(f32[128,1024]{1,0:T(8,128)} %collective-permute-done.5.refs_1_.refs_2_), channel_id=1, source_target_pairs={{0,1},{1,2},{2,3},{3,0},{4,5},{5,6},{6,7},{7,4},{8,9},{9,10},{10,1... | collective-permute-start | bytes 1572872 | tf_op jit(solution)/shard_map/ppermute | solution.py:525
  99.1 33.7 %collective-permute-start.15 = (f32[128,1024]{1,0:T(8,128)}, f32[128,1024]{1,0:T(8,128)}, u32[]{:S(2)}, u32[]{:S(2)}) collective-permute-start(f32[128,1024]{1,0:T(8,128)} %collective-permute-done.6.refs_2_), channel_id=1, source_target_pairs={{0,1},{1,2},{2,3},{3,0},{4,5},{5,6},{6,7},{7,4},{8,9},{9,10},{10,1... | collective-permute-start | bytes 1572872 | tf_op jit(solution)/shard_map/ppermute | solution.py:525
  126.5 17.4 %collective-permute-start.16 = (f32[128,1024]{1,0:T(8,128)}, f32[128,1024]{1,0:T(8,128)S(1)}, u32[]{:S(2)}, u32[]{:S(2)}) collective-permute-start(f32[128,1024]{1,0:T(8,128)} %collective-permute-done.8.refs_3_.refs_2_), channel_id=1, source_target_pairs={{0,1},{1,2},{2,3},{3,0},{4,5},{5,6},{6,7},{7,4},{8,9},{9,10},{10,1... | collective-permute-start | bytes 1572872 | tf_op jit(solution)/shard_map/ppermute | solution.py:525
  127.2 23.4 %collective-permute-start.18 = (f32[128,1024]{1,0:T(8,128)S(1)}, f32[128,1024]{1,0:T(8,128)S(1)}, u32[]{:S(2)}, u32[]{:S(2)}) collective-permute-start(f32[128,1024]{1,0:T(8,128)S(1)} %get-tuple-element.28.refs_6_.refs_0_), channel_id=1, source_target_pairs={{0,4},{4,0},{8,12},{12,8},{1,5},{5,1},{9,13},{13,9},{2,6},{6,2},{1... | collective-permute-start | bytes 1572872 | tf_op jit(solution)/shard_map/ppermute | solution.py:521
  138.4 18.8 %collective-permute-start.17 = (f32[128,1024]{1,0:T(8,128)S(1)}, f32[128,1024]{1,0:T(8,128)S(1)}, u32[]{:S(2)}, u32[]{:S(2)}) collective-permute-start(f32[128,1024]{1,0:T(8,128)S(1)} %copy-done.43), channel_id=1, source_target_pairs={{0,1},{1,2},{2,3},{3,0},{4,5},{5,6},{6,7},{7,4},{8,9},{9,10},{10,1... | collective-permute-start | bytes 1572872 | tf_op jit(solution)/shard_map/ppermute | solution.py:525
  150.6 25.7 %collective-permute-start.29 = (f32[256,1024]{1,0:T(8,128)S(1)}, f32[256,1024]{1,0:T(8,128)}, u32[]{:S(2)}, u32[]{:S(2)}) collective-permute-start(f32[256,1024]{1,0:T(8,128)S(1)} %shard_map.138.refs_6_.refs_0_), channel_id=1, source_target_pairs={{0,1},{1,2},{2,3},{3,0},{4,5},{5,6},{6,7},{7,4},{8,9},{9,10},{10,1... | collective-permute-start | bytes 3145736 | tf_op jit(solution)/shard_map/ppermute | solution.py:525
  150.8 16.9 %collective-permute-start.28 = (f32[128,1024]{1,0:T(8,128)S(1)}, f32[128,1024]{1,0:T(8,128)S(1)}, u32[]{:S(2)}, u32[]{:S(2)}) collective-permute-start(f32[128,1024]{1,0:T(8,128)S(1)} %collective-permute-done.27.refs_2_), channel_id=1, source_target_pairs={{0,4},{4,0},{8,12},{12,8},{1,5},{5,1},{9,13},{13,9},{2,6},{6,2},{1... | collective-permute-start | bytes 1572872 | tf_op jit(solution)/shard_map/ppermute | solution.py:522
  157.2 17.6 %collective-permute-start.23 = (f32[128,1024]{1,0:T(8,128)S(1)}, f32[128,1024]{1,0:T(8,128)S(1)}, u32[]{:S(2)}, u32[]{:S(2)}) collective-permute-start(f32[128,1024]{1,0:T(8,128)S(1)} %get-tuple-element.32.refs_4_.refs_0_.refs_2_), channel_id=1, source_target_pairs={{0,4},{4,0},{8,12},{12,8},{1,5},{5,1},{9,13},{13,9},{2,6},{6,2},{1... | collective-permute-start | bytes 1572872 | tf_op jit(solution)/shard_map/ppermute | solution.py:521
  182.8 27.7 %collective-permute-start.33 = (f32[256,1024]{1,0:T(8,128)}, f32[256,1024]{1,0:T(8,128)}, u32[]{:S(2)}, u32[]{:S(2)}) collective-permute-start(f32[256,1024]{1,0:T(8,128)} %collective-permute-done.29.refs_6_.refs_1_), channel_id=1, source_target_pairs={{0,1},{1,2},{2,3},{3,0},{4,5},{5,6},{6,7},{7,4},{8,9},{9,10},{10,1... | collective-permute-start | bytes 3145736 | tf_op jit(solution)/shard_map/ppermute | solution.py:525
  197.7 19.5 %collective-permute-start.13 = (f32[512,512]{1,0:T(8,128)S(1)}, f32[512,512]{1,0:T(8,128)}, u32[]{:S(2)}, u32[]{:S(2)}) collective-permute-start(f32[512,512]{1,0:T(8,128)S(1)} %copy-done.13), channel_id=1, source_target_pairs={{0,4},{4,0},{8,12},{12,8},{1,5},{5,1},{9,13},{13,9},{2,6},{6,2},{1... | collective-permute-start | bytes 3145736 | tf_op jit(solution)/shard_map/ppermute | solution.py:555
  210.5 26.9 %collective-permute-start.34 = (f32[256,1024]{1,0:T(8,128)}, f32[256,1024]{1,0:T(8,128)}, u32[]{:S(2)}, u32[]{:S(2)}) collective-permute-start(f32[256,1024]{1,0:T(8,128)} %shard_map.150.refs_4_.refs_2_), channel_id=1, source_target_pairs={{0,1},{1,2},{2,3},{3,0},{4,5},{5,6},{6,7},{7,4},{8,9},{9,10},{10,1... | collective-permute-start | bytes 3145736 | tf_op jit(solution)/shard_map/ppermute | solution.py:525
  214.9 28.6 %collective-permute-start.38 = (f32[2,256,512]{2,1,0:T(8,128)}, f32[2,256,512]{2,1,0:T(8,128)}, u32[]{:S(2)}, u32[]{:S(2)}) collective-permute-start(f32[2,256,512]{2,1,0:T(8,128)} %get-tuple-element.37), channel_id=1, source_target_pairs={{0,8},{8,0},{4,12},{12,4},{1,9},{9,1},{5,13},{13,5},{2,10},{10,2},... | collective-permute-start | bytes 3145736 | tf_op jit(solution)/shard_map/ppermute | solution.py:611
  (64 other events, 632.3 us)
